TPU v7x, 32 devices: a whole 2x2x4 slice. The times are simulated.
32 devices in a mesh: dp: 16 (over z, y, x), tensor: 2 (over core).
Axes of the slice: x: 2, y: 2, z: 4, core: 2. Of those that a mesh axis runs over, the one named last changes fastest.
Arguments:
- inputs: bfloat16 [4096, 2048], P(('dp', 'tensor')), may hold values from -6 to 6
- attention_gain: float32 [2048], replicated, may hold values from 0.5 to 1.5
- query_weight: bfloat16 [2048, 4096], P('dp', 'tensor'), may hold values from -0.125 to 0.125
- key_weight: bfloat16 [2048, 512], P('dp', 'tensor'), may hold values from -0.125 to 0.125
- value_weight: bfloat16 [2048, 512], P('dp', 'tensor'), may hold values from -0.125 to 0.125
- query_gain: float32 [128], replicated, may hold values from 0.5 to 1.5
- key_gain: float32 [128], replicated, may hold values from 0.5 to 1.5
- out_weight: bfloat16 [4096, 2048], P('tensor', 'dp'), may hold values from -0.75 to 0.75
- feedforward_gain: float32 [2048], replicated, may hold values from 0.5 to 1.5
- router_weight: bfloat16 [2048, 32], P('dp'), may hold values from -0.0625 to 0.0625
- gate_weight: bfloat16 [32, 2048, 768], P(('dp', 'tensor')), may hold values from -0.125 to 0.125
- up_weight: bfloat16 [32, 2048, 768], P(('dp', 'tensor')), may hold values from -0.125 to 0.125
- down_weight: bfloat16 [32, 768, 2048], P(('dp', 'tensor')), may hold values from -0.875 to 0.875
- routes: int32 [4096, 8], P(('dp', 'tensor')), may hold values from 0 to 31, all different within a row; in each aligned block of 128 rows (0 to 127, 128 to 255, ...) at most 44 rows name the same one
- cotangent: bfloat16 [4096, 2048], P(('dp', 'tensor')), may hold values from -6 to 6
Outputs:
- output: bfloat16 [4096, 2048], P(('dp', 'tensor'))
- grad_inputs: float32 [4096, 2048], P(('dp', 'tensor'))
- grad_attention_gain: float32 [2048], replicated
- grad_query_weight: float32 [2048, 4096], P('dp', 'tensor')
- grad_key_weight: float32 [2048, 512], P('dp', 'tensor')
- grad_value_weight: float32 [2048, 512], P('dp', 'tensor')
- grad_query_gain: float32 [128], replicated
- grad_key_gain: float32 [128], replicated
- grad_out_weight: float32 [4096, 2048], P('tensor', 'dp')
- grad_feedforward_gain: float32 [2048], replicated
- grad_router_weight: float32 [2048, 32], P('dp')
- grad_gate_weight: float32 [32, 2048, 768], P(('dp', 'tensor'))
- grad_up_weight: float32 [32, 2048, 768], P(('dp', 'tensor'))
- grad_down_weight: float32 [32, 768, 2048], P(('dp', 'tensor'))
Inputs may be any that keep to these rules, and one draw needn't show every extreme that they name: `routes`: each row names 8 different experts; among the rows of one device (aligned blocks of 128 rows) no expert is named more than 44 times, and in every draw some expert is named exactly 44 times in some such block.
All inputs are finite; a program needn't handle non-finite values.
Results may differ from a plain program's by a relative error of at most 0.02.
Values may be sent and summed in bfloat16 or wider, within the bound.
No kernel may reach another device: no remote copies, remote signals or barrier semaphores. Data moves between devices by JAX's collectives and lax.ppermute only.
A program may use at most 256 MiB of HBM per device.

v0:
```python
import jax
import jax.numpy as jnp
from jax import lax
from jax.sharding import PartitionSpec as P

EPS = 1e-06
THETA = 1000000.0
HIGH = lax.Precision.HIGHEST
block_limit = 512


def rms_scale(values, scales):
    inverse = lax.rsqrt(jnp.mean(values * values, axis=-1, keepdims=True) + EPS)
    return values * inverse * scales


def rope_tables(length, columns):
    halfway = columns // 2
    frequency = THETA ** (-(jnp.arange(halfway, dtype=jnp.float32) * 2.0 / columns))
    angles = jnp.arange(length, dtype=jnp.float32)[:, None] * frequency[None, :]
    return (jnp.cos(angles), jnp.sin(angles))


def head_prep(raw_rows, scales, cosine_table, sine_table):
    length = raw_rows.shape[0]
    columns = scales.shape[0]
    shaped = rms_scale(raw_rows.reshape(length, -1, columns), scales)
    halfway = columns // 2
    leading = shaped[..., :halfway]
    second = shaped[..., halfway:]
    cos_part = cosine_table[:, None, :]
    sin_part = sine_table[:, None, :]
    turned = jnp.concatenate(
        [leading * cos_part - second * sin_part, second * cos_part + leading * sin_part], axis=-1
    )
    return turned.reshape(length, -1)


def masked_scores(offset, block_rows, queries, key_rows, score_scale):
    scores = (
        jnp.einsum("qkgd,ckd->kgqc", queries, key_rows, preferred_element_type=jnp.float32)
        * score_scale
    )
    row_places = offset + jnp.arange(block_rows, dtype=jnp.int32)
    key_places = jnp.arange(key_rows.shape[0], dtype=jnp.int32)
    allowed = key_places[None, :] <= row_places[:, None]
    return (queries, jnp.where(allowed, scores, -1e30))


def slot_layout(routes, expert_count, capacity):
    flat_routes = routes.reshape(-1)
    onehot = (flat_routes[:, None] == jnp.arange(expert_count, dtype=jnp.int32)[None, :]).astype(
        jnp.int32
    )
    position = jnp.sum((jnp.cumsum(onehot, axis=0) - onehot) * onehot, axis=1)
    return flat_routes * capacity + position


def route_rows(buffer):
    return lax.all_to_all(buffer, ("dp", "tensor"), split_axis=0, concat_axis=0, tiled=True)


def local(
    inputs,
    attention_gain,
    query_weight,
    key_weight,
    value_weight,
    query_gain,
    key_gain,
    out_weight,
    feedforward_gain,
    router_weight,
    gate_weight,
    up_weight,
    down_weight,
    routes,
    cotangent,
):
    tok_rows, model_width = inputs.shape
    head_width = query_gain.shape[0]
    top_count = routes.shape[1]
    expert_count = router_weight.shape[1]
    local_experts = gate_weight.shape[0]
    capacity = tok_rows * top_count * 11 // (expert_count * 8)
    full_query, full_key, full_value, full_out, full_router = (
        lax.all_gather(query_weight, "dp", axis=0, tiled=True),
        lax.all_gather(key_weight, "dp", axis=0, tiled=True),
        lax.all_gather(value_weight, "dp", axis=0, tiled=True),
        lax.all_gather(out_weight, "dp", axis=1, tiled=True),
        lax.all_gather(router_weight, "dp", axis=0, tiled=True),
    )
    inputs_float = inputs.astype(jnp.float32)
    normed_attention, attention_back = jax.vjp(rms_scale, inputs_float, attention_gain)
    sequence = lax.all_gather(normed_attention.astype(jnp.bfloat16), "tensor", axis=0, tiled=True)
    length = sequence.shape[0]
    query_raw = jnp.dot(sequence, full_query, preferred_element_type=jnp.float32)
    key_raw = jnp.dot(sequence, full_key, preferred_element_type=jnp.float32)
    value_raw = jnp.dot(sequence, full_value, preferred_element_type=jnp.float32)
    cosine_table, sine_table = rope_tables(length, head_width)

    def prepare(raw_rows, scales):
        return head_prep(raw_rows, scales, cosine_table, sine_table)

    query_ready, query_back = jax.vjp(prepare, query_raw, query_gain)
    key_ready, key_back = jax.vjp(prepare, key_raw, key_gain)
    kv_heads = key_raw.shape[1] // head_width
    group_size = query_raw.shape[1] // head_width // kv_heads
    queries = query_ready.astype(jnp.bfloat16).reshape(length, kv_heads, group_size, head_width)
    key_rows = key_ready.astype(jnp.bfloat16).reshape(length, kv_heads, head_width)
    value_rows = value_raw.astype(jnp.bfloat16).reshape(length, kv_heads, head_width)
    score_scale = head_width ** (-0.5)
    block_rows = min(block_limit, length)
    block_count = length // block_rows
    offsets = jnp.arange(block_count, dtype=jnp.int32) * block_rows

    def forward_block(offset):
        query_block, masked = masked_scores(offset, block_rows, queries, key_rows, score_scale)
        peak_value = jnp.max(masked, axis=-1, keepdims=True)
        exp_total = jnp.sum(jnp.exp(masked - peak_value), axis=-1, keepdims=True)
        log_total = peak_value + jnp.log(exp_total)
        soft_weights = jnp.exp(masked - log_total).astype(jnp.bfloat16)
        mixture = jnp.einsum(
            "kgqc,ckd->qkgd", soft_weights, value_rows, preferred_element_type=jnp.float32
        )
        return (mixture, log_total)

    mixed_blocks, log_totals = lax.map(forward_block, offsets)
    attended = mixed_blocks.reshape(length, -1).astype(jnp.bfloat16)
    branch = lax.psum_scatter(
        jnp.dot(attended, full_out, preferred_element_type=jnp.float32).astype(jnp.bfloat16),
        "tensor",
        scatter_dimension=0,
        tiled=True,
    ).astype(jnp.float32)
    hidden = inputs_float + branch
    normed_experts, experts_back = jax.vjp(rms_scale, hidden, feedforward_gain)
    moe_in = normed_experts.astype(jnp.bfloat16)
    logits = jnp.dot(moe_in, full_router, preferred_element_type=jnp.float32)
    onehot_routes = (
        routes[:, :, None] == jnp.arange(expert_count, dtype=jnp.int32)[None, None, :]
    ).astype(jnp.float32)
    chosen = jnp.einsum("tke,te->tk", onehot_routes, logits, precision=HIGH)
    gate_values = jax.nn.softmax(chosen, axis=-1)
    slots = slot_layout(routes, expert_count, capacity)
    buffer_shape = (expert_count // local_experts, local_experts, capacity, model_width)
    dispatch = (
        jnp.zeros((expert_count * capacity, model_width), jnp.bfloat16)
        .at[slots]
        .set(jnp.repeat(moe_in, top_count, axis=0))
    )
    received = route_rows(dispatch.reshape(buffer_shape))
    gate_pre = jnp.einsum(
        "secd,edf->secf", received, gate_weight, preferred_element_type=jnp.float32
    )
    up_pre = jnp.einsum("secd,edf->secf", received, up_weight, preferred_element_type=jnp.float32)
    sigmoid_gate = jax.nn.sigmoid(gate_pre)
    silu_gate = gate_pre * sigmoid_gate
    activated = (silu_gate * up_pre).astype(jnp.bfloat16)
    expert_out = jnp.einsum(
        "secf,efd->secd", activated, down_weight, preferred_element_type=jnp.float32
    ).astype(jnp.bfloat16)
    returned = route_rows(expert_out).reshape(expert_count * capacity, model_width)
    picked = returned[slots].reshape(tok_rows, top_count, model_width).astype(jnp.float32)
    mixture_out = jnp.sum(gate_values[:, :, None] * picked, axis=1)
    output = (hidden + mixture_out).astype(jnp.bfloat16)
    grad_output = cotangent.astype(jnp.float32)
    grad_gates = jnp.sum(picked * grad_output[:, None, :], axis=2)
    grad_picks = (
        (gate_values[:, :, None] * grad_output[:, None, :])
        .astype(jnp.bfloat16)
        .reshape(-1, model_width)
    )
    grad_dispatch = (
        jnp.zeros((expert_count * capacity, model_width), jnp.bfloat16).at[slots].set(grad_picks)
    )
    grad_received = route_rows(grad_dispatch.reshape(buffer_shape))
    grad_act = jnp.einsum(
        "secd,efd->secf", grad_received, down_weight, preferred_element_type=jnp.float32
    )
    grad_down = jnp.einsum(
        "secf,secd->efd", activated, grad_received, preferred_element_type=jnp.float32
    )
    grad_gate_pre = (
        grad_act * up_pre * sigmoid_gate * (1.0 + gate_pre * (1.0 - sigmoid_gate))
    ).astype(jnp.bfloat16)
    grad_up_pre = (grad_act * silu_gate).astype(jnp.bfloat16)
    grad_gate = jnp.einsum(
        "secd,secf->edf", received, grad_gate_pre, preferred_element_type=jnp.float32
    )
    grad_up = jnp.einsum(
        "secd,secf->edf", received, grad_up_pre, preferred_element_type=jnp.float32
    )
    grad_sent = jnp.einsum(
        "secf,edf->secd", grad_gate_pre, gate_weight, preferred_element_type=jnp.float32
    )
    grad_sent = (
        grad_sent
        + jnp.einsum("secf,edf->secd", grad_up_pre, up_weight, preferred_element_type=jnp.float32)
    ).astype(jnp.bfloat16)
    grad_back = route_rows(grad_sent).reshape(expert_count * capacity, model_width)
    grad_moe_in = jnp.sum(
        grad_back[slots].reshape(tok_rows, top_count, model_width).astype(jnp.float32), axis=1
    )
    grad_chosen = gate_values * (
        grad_gates - jnp.sum(gate_values * grad_gates, axis=1, keepdims=True)
    )
    grad_logits = jnp.einsum("tk,tke->te", grad_chosen, onehot_routes, precision=HIGH)
    router_float = full_router.astype(jnp.float32)
    grad_moe_in = grad_moe_in + jnp.einsum("te,de->td", grad_logits, router_float, precision=HIGH)
    grad_router = jnp.einsum("td,te->de", moe_in.astype(jnp.float32), grad_logits, precision=HIGH)
    grad_hidden_norm, grad_experts_gain = experts_back(grad_moe_in)
    grad_hidden = grad_output + grad_hidden_norm
    grad_branch = lax.all_gather(grad_hidden.astype(jnp.bfloat16), "tensor", axis=0, tiled=True)
    grad_attended = jnp.einsum(
        "td,ad->ta", grad_branch, full_out, preferred_element_type=jnp.float32
    ).astype(jnp.bfloat16)
    grad_blocks = grad_attended.reshape(block_count, block_rows, kv_heads, group_size, head_width)

    def backward_block(carry, item):
        key_sum, value_sum = carry
        offset, log_total, grad_block = item
        query_block, masked = masked_scores(offset, block_rows, queries, key_rows, score_scale)
        soft_weights = jnp.exp(masked - log_total)
        soft_low = soft_weights.astype(jnp.bfloat16)
        grad_soft = jnp.einsum(
            "qkgd,ckd->kgqc", grad_block, value_rows, preferred_element_type=jnp.float32
        )
        inner_sum = jnp.sum(soft_weights * grad_soft, axis=-1, keepdims=True)
        grad_scores = (soft_weights * (grad_soft - inner_sum)).astype(jnp.bfloat16)
        grad_query_block = (
            jnp.einsum("kgqc,ckd->qkgd", grad_scores, key_rows, preferred_element_type=jnp.float32)
            * score_scale
        )
        key_sum = (
            key_sum
            + jnp.einsum(
                "kgqc,qkgd->ckd", grad_scores, query_block, preferred_element_type=jnp.float32
            )
            * score_scale
        )
        value_sum = value_sum + jnp.einsum(
            "kgqc,qkgd->ckd", soft_low, grad_block, preferred_element_type=jnp.float32
        )
        return ((key_sum, value_sum), grad_query_block)

    zero_rows = jnp.zeros((length, kv_heads, head_width), jnp.float32)
    (key_sum, value_sum), grad_query_blocks = lax.scan(
        backward_block, (zero_rows, zero_rows), (offsets, log_totals, grad_blocks)
    )
    grad_query_raw, grad_query_gain = query_back(grad_query_blocks.reshape(length, -1))
    grad_key_raw, grad_key_gain = key_back(key_sum.reshape(length, -1))
    grad_query_low = grad_query_raw.astype(jnp.bfloat16)
    grad_key_low = grad_key_raw.astype(jnp.bfloat16)
    grad_value_low = value_sum.reshape(length, -1).astype(jnp.bfloat16)
    total = jnp.einsum("tc,dc->td", grad_query_low, full_query, preferred_element_type=jnp.float32)
    total = total + jnp.einsum(
        "tc,dc->td", grad_key_low, full_key, preferred_element_type=jnp.float32
    )
    grad_sequence = lax.psum_scatter(
        (
            total
            + jnp.einsum(
                "tc,dc->td", grad_value_low, full_value, preferred_element_type=jnp.float32
            )
        ).astype(jnp.bfloat16),
        "tensor",
        scatter_dimension=0,
        tiled=True,
    ).astype(jnp.float32)
    grad_inputs_norm, grad_attention_gain = attention_back(grad_sequence)
    grad_inputs = grad_hidden + grad_inputs_norm
    query_cols = grad_query_low.shape[1]
    key_cols = grad_key_low.shape[1]
    grad_raw_all = jnp.concatenate([grad_query_low, grad_key_low, grad_value_low], axis=1)
    inward = jnp.einsum("td,tc->dc", sequence, grad_raw_all, preferred_element_type=jnp.float32)
    outward = jnp.einsum("td,ta->da", grad_branch, attended, preferred_element_type=jnp.float32)
    owned = lax.psum_scatter(
        jnp.concatenate([inward, outward], axis=1), "dp", scatter_dimension=0, tiled=True
    )
    grad_query_weight = owned[:, :query_cols]
    grad_key_weight = owned[:, query_cols : query_cols + key_cols]
    grad_value_weight = owned[:, query_cols + key_cols : query_cols + 2 * key_cols]
    grad_out_weight = owned[:, query_cols + 2 * key_cols :].T
    router_total, attention_total, query_total, key_total, experts_total = lax.psum(
        (grad_router, grad_attention_gain, grad_query_gain, grad_key_gain, grad_experts_gain),
        ("dp", "tensor"),
    )
    router_rows = router_weight.shape[0]
    router_share = lax.dynamic_slice_in_dim(
        router_total, lax.axis_index("dp") * router_rows, router_rows, 0
    )
    return (
        output,
        grad_inputs,
        attention_total,
        grad_query_weight,
        grad_key_weight,
        grad_value_weight,
        query_total,
        key_total,
        grad_out_weight,
        experts_total,
        router_share,
        grad_gate,
        grad_up,
        grad_down,
    )


def solution(mesh):
    in_specs = (
        P(("dp", "tensor"), None),
        P(),
        P("dp", "tensor"),
        P("dp", "tensor"),
        P("dp", "tensor"),
        P(),
        P(),
        P("tensor", "dp"),
        P(),
        P("dp", None),
        P(("dp", "tensor"), None, None),
        P(("dp", "tensor"), None, None),
        P(("dp", "tensor"), None, None),
        P(("dp", "tensor"), None),
        P(("dp", "tensor"), None),
    )
    out_specs = (
        P(("dp", "tensor"), None),
        P(("dp", "tensor"), None),
        P(),
        P("dp", "tensor"),
        P("dp", "tensor"),
        P("dp", "tensor"),
        P(),
        P(),
        P("tensor", "dp"),
        P(),
        P("dp", None),
        P(("dp", "tensor"), None, None),
        P(("dp", "tensor"), None, None),
        P(("dp", "tensor"), None, None),
    )
    return jax.shard_map(local, mesh=mesh, in_specs=in_specs, out_specs=out_specs, check_vma=False)
```

profile of v0, /device:TPU:0, one launch (start us, length us, event | category | flops | bytes accessed | tf_op | source)
XLA Modules:
  0.0 1851.2 jit_solution(16832148632103627454)
XLA Ops:
  15.8 7.9 all-gather.7.cloned.1.call-done
  23.7 59.2 %all-gather.11.cloned.1.call-done = bf16[2048,256]{1,0:T(8,128)(2,1)} async-done(((bf16[128,256]{1,0:T(8,128)(2,1)}), bf16[2048,256]{1,0:T(8,128)(2,1)}) %all-gather.11.cloned.1.call-update) | async-done | bytes 1048592 | tf_op jit(solution)/shard_map/all_gather | solution.py:88
  89.4 50.4 %all-gather.9.cloned.1.call-done = bf16[2048,256]{1,0:T(8,128)(2,1)} async-done(((bf16[128,256]{1,0:T(8,128)(2,1)}), bf16[2048,256]{1,0:T(8,128)(2,1)}) %all-gather.9.cloned.1.call-update) | async-done | bytes 1048592 | tf_op jit(solution)/shard_map/all_gather | solution.py:89
  142.6 111.6 %all-gather.13.cloned.1.call-done = bf16[2048,2048]{1,0:T(8,128)(2,1)} async-done(((bf16[128,2048]{1,0:T(8,128)(2,1)}), bf16[2048,2048]{1,0:T(8,128)(2,1)}) %all-gather.13.cloned.1.call-update) | async-done | bytes 8388624 | tf_op jit(solution)/shard_map/all_gather | solution.py:87
  274.9 122.3 %all-gather.15.cloned.1.call-done = bf16[2048,2048]{1,0:T(8,128)(2,1)} async-done(((bf16[2048,128]{1,0:T(8,128)(2,1)}), bf16[2048,2048]{1,0:T(8,128)(2,1)}) %all-gather.15.cloned.1.call-update) | async-done | bytes 8388624 | tf_op jit(solution)/shard_map/all_gather | solution.py:90
  406.7 15.7 reduce-window.6
  430.8 38.7 %all_gather.26 = bf16[2048,32]{0,1:T(8,128)(2,1)S(1)} all-gather(bf16[128,32]{0,1:T(8,128)(2,1)} %param.24), channel_id=1, replica_groups=mesh['dp'=16,'tensor'=2] {'dp'}, dimensions={0}, use_global_device_ids=true | all-gather | bytes 139264 | tf_op jit(solution)/shard_map/all_gather | solution.py:91
  483.4 11.1 scatter_custom_fusion.1
  494.5 7.9 reshape.332
  506.1 10.4 scatter_custom_fusion
  516.5 7.9 reshape.325
  524.4 121.6 %all-to-all-done.2 = bf16[32,1,44,2048]{3,2,1,0:T(8,128)(2,1)} async-done(((bf16[32,1,44,2048]{3,2,1,0:T(8,128)(2,1)}), bf16[32,1,44,2048]{3,2,1,0:T(8,128)(2,1)}, u32[]{:S(2)}, u32[]{:S(2)}) %all-to-all-start.2) | async-done | bytes 5767200 | tf_op jit(solution)/shard_map/all_to_all | solution.py:60
  649.8 9.6 fusion.6
  659.4 130.4 %all-to-all-done = bf16[32,1,44,2048]{3,2,1,0:T(8,128)(2,1)} async-done(((bf16[32,1,44,2048]{3,2,1,0:T(8,128)(2,1)}), bf16[32,1,44,2048]{3,2,1,0:T(8,128)(2,1)}, u32[]{:S(2)}, u32[]{:S(2)}) %all-to-all-start) | async-done | bytes 5767200 | tf_op jit(solution)/shard_map/all_to_all | solution.py:60
  789.7 8.2 fusion.12
  798.0 11.5 fusion.55
  835.8 125.6 %all-to-all-done.1 = bf16[32,1,44,2048]{3,2,1,0:T(8,128)(2,1)} async-done(((bf16[32,1,44,2048]{3,2,1,0:T(8,128)(2,1)}), bf16[32,1,44,2048]{3,2,1,0:T(8,128)(2,1)}, u32[]{:S(2)}, u32[]{:S(2)}) %all-to-all-start.1) | async-done | bytes 5767200 | tf_op jit(solution)/shard_map/all_to_all | solution.py:60
  965.1 8.4 reshape.331
  973.5 12.3 gather_fusion
  992.7 112.3 %all-to-all-done.3 = bf16[32,1,44,2048]{3,2,1,0:T(8,128)(2,1)} async-done(((bf16[32,1,44,2048]{3,2,1,0:T(8,128)(2,1)}), bf16[32,1,44,2048]{3,2,1,0:T(8,128)(2,1)}, u32[]{:S(2)}, u32[]{:S(2)}) %all-to-all-start.3) | async-done | bytes 5767200 | tf_op jit(solution)/shard_map/all_to_all | solution.py:60
  1105.0 8.0 reshape.336
  1113.0 12.2 gather_fusion.1
  1181.1 9.5 fusion.112
  1190.7 9.1 fusion.62
  1199.8 24.8 %pad_maximum_fusion = f32[2048,4608]{1,0:T(8,128)} fusion(f32[2048,2048]{1,0:T(8,128)} %fusion.112, f32[2048,2560]{1,0:T(8,128)} %fusion.62), kind=kLoop, calls=%fused_computation.4 | loop fusion | flops 9437184 | bytes 75497472 | tf_op jit(solution)/shard_map/concatenate | solution.py:279
  1224.6 9.8 fusion.40
  1234.3 9.8 fusion.37
  1244.2 9.7 fusion.34
  1253.9 20.8 %all-reduce.7.cloned.1.call-done = f32[2048,32]{0,1:T(8,128)} async-done(((f32[2048,32]{0,1:T(8,128)}), f32[2048,32]{0,1:T(8,128)}) %all-reduce.7.cloned.1.call-update) | async-done | bytes 262160 | tf_op jit(solution)/shard_map/psum | solution.py:285
  1276.0 9.2 reduce-scatter.6.cloned.1.call-done
  1286.9 44.3 %all-reduce.4 = (f32[2048]{0:T(1024)}, f32[128]{0:T(128)}, f32[128]{0:T(128)}, f32[2048]{0:T(1024)}) all-reduce(f32[2048]{0:T(1024)S(1)} %get-tuple-element.135, f32[128]{0:T(128)S(1)} %get-tuple-element.129, f32[128]{0:T(128)S(1)} %get-tuple-element.137, f32[2048]{0:T(1024)S(1)} %copy-done.50), channel_id=1, replica_groups=mesh['dp'=16,'tensor'=2] {'dp','tensor'}, use_global_device_ids=true, to_apply=%region_25.26 | all-reduce | flops 4352 | bytes 34816 | tf_op jit(solution)/shard_map/psum | solution.py:285
  1335.4 501.3 %reduce-scatter.8.cloned.1.call-done = f32[128,4608]{1,0:T(8,128)} async-done(((f32[2048,4608]{1,0:T(8,128)}), f32[128,4608]{1,0:T(8,128)}) %reduce-scatter.8.cloned.1.call-update) | async-done | bytes 2359312 | tf_op jit(solution)/shard_map/reduce_scatter | solution.py:278
  (284 shorter events, 184.0 us)
Async XLA Ops:
  7.2 790.8 %copy-start = (bf16[1,2048,768]{2,1,0:T(8,128)(2,1)S(1)}, bf16[1,2048,768]{2,1,0:T(8,128)(2,1)}, u32[]{:S(2)}) copy-start(bf16[1,2048,768]{2,1,0:T(8,128)(2,1)} %param.25) | copy-start | bytes 9437188
  7.2 80.3 %copy-start.61 = (f32[128]{0:T(128)S(1)}, f32[128]{0:T(128)}, u32[]{:S(2)}) copy-start(f32[128]{0:T(128)} %param.21) | copy-start | bytes 1540
  7.2 16.5 all-gather.7.cloned.1.call-start
  11.8 71.1 %all-gather.11.cloned.1.call-start = ((), (), s32[]{:S(2)}) async-start(), calls=%async_computation.9 | async-start | bytes 1114112 | tf_op jit(solution)/shard_map/all_gather | solution.py:88
  12.6 127.2 %all-gather.9.cloned.1.call-start = ((), (), s32[]{:S(2)}) async-start(), calls=%async_computation.8 | async-start | bytes 1114112 | tf_op jit(solution)/shard_map/all_gather | solution.py:89
  13.3 240.8 %all-gather.13.cloned.1.call-start = ((), (), s32[]{:S(2)}) async-start(), calls=%async_computation.10 | async-start | bytes 8912896 | tf_op jit(solution)/shard_map/all_gather | solution.py:87
  13.9 383.4 %all-gather.15.cloned.1.call-start = ((), (), s32[]{:S(2)}) async-start(), calls=%async_computation.11 | async-start | bytes 8912896 | tf_op jit(solution)/shard_map/all_gather | solution.py:90
  14.5 458.1 %reduce-scatter.4.cloned.1.call-start = ((), (), s32[]{:S(2)}) async-start(), calls=%async_computation.12 | async-start | bytes 1572864 | tf_op jit(solution)/shard_map/reduce_scatter | solution.py:130
  85.7 174.4 %copy-start.51 = (f32[256,2]{0,1:T(2,128)}, f32[256,2]{0,1:T(2,128)S(1)}, u32[]{:S(2)}) copy-start(f32[256,2]{0,1:T(2,128)S(1)} %get-tuple-element.164) | copy-start | bytes 6148
  86.8 173.4 %copy-start.23 = (f32[256,2,128]{2,0,1:T(8,128)}, f32[256,2,128]{2,0,1:T(8,128)S(1)}, u32[]{:S(2)}) copy-start(f32[256,2,128]{2,0,1:T(8,128)S(1)} %copy.138) | copy-start | bytes 786436
  404.4 72.6 %copy-start.41 = (s32[128,8]{1,0:T(8,128)}, s32[128,8]{1,0:T(8,128)S(1)}, u32[]{:S(2)}) copy-start(s32[128,8]{1,0:T(8,128)S(1)} %copy.143) | copy-start | bytes 12292
  502.5 143.6 %all-to-all-start.2 = ((bf16[32,1,44,2048]{3,2,1,0:T(8,128)(2,1)}), bf16[32,1,44,2048]{3,2,1,0:T(8,128)(2,1)}, u32[]{:S(2)}, u32[]{:S(2)}) async-start(bf16[32,1,44,2048]{3,2,1,0:T(8,128)(2,1)} %bitcast.303), calls=%async_computation.3 | async-start | bytes 12582912 | tf_op jit(solution)/shard_map/all_to_all | solution.py:60
  646.0 143.7 %all-to-all-start = ((bf16[32,1,44,2048]{3,2,1,0:T(8,128)(2,1)}), bf16[32,1,44,2048]{3,2,1,0:T(8,128)(2,1)}, u32[]{:S(2)}, u32[]{:S(2)}) async-start(bf16[32,1,44,2048]{3,2,1,0:T(8,128)(2,1)} %bitcast.302), calls=%async_computation.1 | async-start | bytes 12582912 | tf_op jit(solution)/shard_map/all_to_all | solution.py:60
  798.0 12.9 copy-start.71
  817.8 143.6 %all-to-all-start.1 = ((bf16[32,1,44,2048]{3,2,1,0:T(8,128)(2,1)}), bf16[32,1,44,2048]{3,2,1,0:T(8,128)(2,1)}, u32[]{:S(2)}, u32[]{:S(2)}) async-start(bf16[32,1,44,2048]{3,2,1,0:T(8,128)(2,1)} %convert_bitcast_fusion), calls=%async_computation.2 | async-start | bytes 12582912 | tf_op jit(solution)/shard_map/all_to_all | solution.py:60
  835.8 129.3 %copy-start.54 = (s32[1024,1]{0,1:T(1,128)S(1)}, s32[1024,1]{0,1:T(1,128)}, u32[]{:S(2)}) copy-start(s32[1024,1]{0,1:T(1,128)} %compare_select_fusion) | copy-start | bytes 12292
  961.4 143.6 %all-to-all-start.3 = ((bf16[32,1,44,2048]{3,2,1,0:T(8,128)(2,1)}), bf16[32,1,44,2048]{3,2,1,0:T(8,128)(2,1)}, u32[]{:S(2)}, u32[]{:S(2)}) async-start(bf16[32,1,44,2048]{3,2,1,0:T(8,128)(2,1)} %fusion.3), calls=%async_computation.4 | async-start | bytes 12582912 | tf_op jit(solution)/shard_map/all_to_all | solution.py:60
  965.1 176.9 %all-gather.17.cloned.1.call-start = ((), (), s32[]{:S(2)}) async-start(), calls=%async_computation.13 | async-start | bytes 1572864 | tf_op jit(solution)/shard_map/all_gather | solution.py:214
  973.5 12.3 copy-start.16
  973.5 12.3 copy-start.40
  1134.2 140.5 %all-reduce.7.cloned.1.call-start = ((), (), s32[]{:S(2)}) async-start(), calls=%async_computation.16 | async-start | bytes 524288 | tf_op jit(solution)/shard_map/psum | solution.py:285
  1141.9 143.4 %reduce-scatter.6.cloned.1.call-start = ((), (), s32[]{:S(2)}) async-start(), calls=%async_computation.14 | async-start | bytes 1572864 | tf_op jit(solution)/shard_map/reduce_scatter | solution.py:260
  1181.0 655.7 %reduce-scatter.8.cloned.1.call-start = ((), (), s32[]{:S(2)}) async-start(), calls=%async_computation.15 | async-start | bytes 40108032 | tf_op jit(solution)/shard_map/reduce_scatter | solution.py:278
  1224.6 9.8 copy-start.75
  1234.3 9.8 copy-start.76
  1244.2 41.1 %copy-start.47 = (f32[2048]{0:T(1024)S(1)}, f32[2048]{0:T(1024)}, u32[]{:S(2)}) copy-start(f32[2048]{0:T(1024)} %param.16) | copy-start | bytes 24580
  1244.2 41.1 %copy-start.66 = (f32[128]{0:T(128)S(1)}, f32[128]{0:T(128)}, u32[]{:S(2)}) copy-start(f32[128]{0:T(128)} %copy-done.65) | copy-start | bytes 1540
  1244.2 42.7 %copy-start.50 = (f32[2048]{0:T(1024)S(1)}, f32[2048]{0:T(1024)}, u32[]{:S(2)}) copy-start(f32[2048]{0:T(1024)} %get-tuple-element.133) | copy-start | bytes 24580
  1244.2 87.0 %copy-start.68 = (f32[128]{0:T(128)S(1)}, f32[128]{0:T(128)}, u32[]{:S(2)}) copy-start(f32[128]{0:T(128)} %copy-done.67) | copy-start | bytes 1540
  1244.2 87.0 %copy-start.46 = (f32[2048]{0:T(1024)S(1)}, f32[2048]{0:T(1024)}, u32[]{:S(2)}) copy-start(f32[2048]{0:T(1024)} %param.23) | copy-start | bytes 24580
  1244.2 87.0 %copy-start.60 = (f32[128]{0:T(128)S(1)}, f32[128]{0:T(128)}, u32[]{:S(2)}) copy-start(f32[128]{0:T(128)} %copy-done.58) | copy-start | bytes 1540
  1331.2 512.9 %copy-start.1 = (bf16[1,2048,768]{2,1,0:T(8,128)(2,1)S(1)}, bf16[1,2048,768]{2,1,0:T(8,128)(2,1)}, u32[]{:S(2)}) copy-start(bf16[1,2048,768]{2,1,0:T(8,128)(2,1)} %param.25) | copy-start | bytes 9437188
  (60 other events, 215.5 us)
Sparse Core Ops, SparseCore 0:
  12.0 11.7 all-gather.6
  26.5 56.4 all-gather.10
  85.7 54.0 all-gather.8
  142.5 111.6 all-gather.12
  256.7 140.5 all-gather.14
  404.5 6.7 reduce-scatter.3
  1134.4 7.1 all-gather.16
  1148.6 126.0 all-reduce.6
  1277.6 7.5 reduce-scatter.5
  1291.1 545.6 reduce-scatter.7
where the time goes:
time: 1860 us; the launch traced here: 1850 us
  waiting for transfers between devices  1380 us (74%)
  matrix products  142 us (8%)
  local copies, waits for them, and re-layouts  110 us (6%)
  other arithmetic  110 us (6%)
  blocking collectives  83 us (4%)
    reduce_scatter x1, waiting for transfers between devices, local(): lax.psum_scatter(jnp.concatenate([inward, outward], axis=1), 'dp', scatte...  501 us
    all_to_all x4, waiting for transfers between devices, route_rows(): lax.all_to_all(buffer, ('dp', 'tensor'), split_axis=0, concat_axis=0, til...  490 us
    all_gather x1, waiting for transfers between devices, local(): lax.all_gather(out_weight, 'dp', axis=1, tiled=True)  122 us
    all_gather x1, waiting for transfers between devices, local(): lax.all_gather(query_weight, 'dp', axis=0, tiled=True)  112 us
    all_gather x1, waiting for transfers between devices, local(): lax.all_gather(key_weight, 'dp', axis=0, tiled=True)  59.2 us
    all_gather x1, waiting for transfers between devices, local(): lax.all_gather(value_weight, 'dp', axis=0, tiled=True)  50.4 us
    psum x1, blocking collectives, local(): lax.psum((grad_router, grad_attention_gain, grad_query_gain, grad_key_gai...  44.3 us
    all_gather x1, blocking collectives, local(): lax.all_gather(router_weight, 'dp', axis=0, tiled=True)  38.7 us
  transfers between devices with their start and end apart: 14, of which 12 were waited for; matrix products, arithmetic and copies ran while one was open for 14% of the time, Pallas kernels for 0%

commit v1 on v0

--- a/solution.py
+++ b/solution.py
@@ -1,6 +1,11 @@
+import functools
+import math
+
 import jax
 import jax.numpy as jnp
 from jax import lax
+from jax.experimental import pallas as pl
+from jax.experimental.pallas import tpu as pltpu
 from jax.sharding import PartitionSpec as P
 
 EPS = 1e-06
@@ -60,7 +65,7 @@
     return lax.all_to_all(buffer, ("dp", "tensor"), split_axis=0, concat_axis=0, tiled=True)
 
 
-def local(
+def local_any(
     inputs,
     attention_gain,
     query_weight,
@@ -308,6 +313,1094 @@
     )
 
 
+low, wide = jnp.bfloat16, jnp.float32
+Z_RING = tuple((i, (i + 4) % 16) for i in range(16))
+Z_PAIR = tuple((i, i ^ 4) for i in range(16))
+Z_FAR = tuple((i, i ^ 8) for i in range(16))
+Y_PAIR = tuple((i, i ^ 2) for i in range(16))
+X_PAIR = tuple((i, i ^ 1) for i in range(16))
+BLOCKS = tuple((k, dy, dx) for k in range(4) for dy in range(2) for dx in range(2))
+PLANE = tuple((dy, dx) for dy in range(2) for dx in range(2))
+OVER_X = (1, 2)
+ROOM = 8 * 2**20
+WHOLE = 60 * 2**20
+TILE = 256
+WIDE = 512
+HIDDEN_TILE = 768
+NT = (((1,), (1,)), ((), ()))
+TN = (((0,), (0,)), ((), ()))
+
+
+def z_next(block):
+    return lax.ppermute(block, "dp", Z_RING)
+
+
+def z_pair(block):
+    return lax.ppermute(block, "dp", Z_PAIR)
+
+
+def z_far(block):
+    return lax.ppermute(block, "dp", Z_FAR)
+
+
+def y_swap(block):
+    return lax.ppermute(block, "dp", Y_PAIR)
+
+
+def x_swap(block):
+    return lax.ppermute(block, "dp", X_PAIR)
+
+
+def core_swap(block):
+    return lax.ppermute(block, "tensor", ((0, 1), (1, 0)))
+
+
+def after(value, *earlier):
+    return lax.optimization_barrier((value, *earlier))[0]
+
+
+def plus(own, *others):
+    total = own.astype(wide)
+    for other in others:
+        total = total + other.astype(wide)
+    return total
+
+
+TOKEN_ROUNDS = (
+    (((0, 0, 0), (0, 0, 1), x_swap), ((0, 0, 0), (0, 1, 0), y_swap), ((0, 0, 0), (1, 0, 0), z_next)),
+    (((1, 0, 0), (1, 0, 1), x_swap), ((0, 0, 1), (0, 1, 1), y_swap), ((1, 0, 0), (2, 0, 0), z_next)),
+    (((2, 0, 0), (2, 0, 1), x_swap), ((1, 0, 0), (1, 1, 0), y_swap), ((2, 0, 0), (3, 0, 0), z_next)),
+    (((3, 0, 0), (3, 0, 1), x_swap), ((2, 0, 0), (2, 1, 0), y_swap), ((0, 1, 1), (1, 1, 1), z_next)),
+    (((2, 1, 0), (2, 1, 1), x_swap), ((3, 0, 1), (3, 1, 1), y_swap), ((2, 1, 0), (3, 1, 0), z_next)),
+)
+WEIGHT_ROUNDS = (
+    (
+        ((0, 0, 0), (0, 0, 1), x_swap),
+        ((0, 0, 0), (0, 1, 0), y_swap),
+        ((0, 0, 0), (2, 0, 0), z_far, True),
+    ),
+    (
+        ((1, 0, 0), (1, 0, 1), x_swap),
+        ((1, 0, 0), (1, 1, 0), y_swap),
+        ((1, 0, 0), (3, 0, 0), z_far, True),
+        ((0, 0, 1), (0, 1, 1), y_swap),
+    ),
+    (
+        ((2, 0, 0), (2, 0, 1), x_swap),
+        ((2, 0, 0), (2, 1, 0), y_swap),
+        ((1, 1, 0), (1, 1, 1), x_swap),
+    ),
+    (
+        ((3, 0, 0), (3, 1, 0), y_swap),
+        ((3, 0, 0), (3, 0, 1), x_swap),
+        ((2, 0, 1), (2, 1, 1), y_swap),
+    ),
+    (((3, 1, 0), (3, 1, 1), x_swap),),
+)
+SHORT_ROUNDS = (
+    (*WEIGHT_ROUNDS[0][:2],),
+    (((0, 0, 0), (2, 0, 0), z_far, True), *WEIGHT_ROUNDS[1][:2], WEIGHT_ROUNDS[1][3]),
+    (((1, 0, 0), (3, 0, 0), z_far), *WEIGHT_ROUNDS[2]),
+    (*WEIGHT_ROUNDS[3], ((1, 1, 1), (3, 1, 1), z_far)),
+)
+WEIGHT_RETURNS = (
+    (((3, 1, 1), (3, 1, 0), x_swap),),
+    (
+        ((3, 1, 0), (3, 0, 0), y_swap),
+        ((3, 0, 1), (3, 0, 0), x_swap),
+        ((2, 1, 1), (2, 0, 1), y_swap),
+    ),
+    (
+        ((3, 0, 0), (1, 0, 0), z_far, True),
+        ((2, 0, 1), (2, 0, 0), x_swap),
+        ((2, 1, 0), (2, 0, 0), y_swap),
+        ((1, 1, 1), (1, 1, 0), x_swap),
+    ),
+    (
+        ((2, 0, 0), (0, 0, 0), z_far, True),
+        ((1, 1, 0), (1, 0, 0), y_swap),
+        ((1, 0, 1), (1, 0, 0), x_swap),
+        ((0, 1, 1), (0, 0, 1), y_swap),
+    ),
+    (((0, 0, 1), (0, 0, 0), x_swap), ((0, 1, 0), (0, 0, 0), y_swap)),
+)
+
+
+def turned(block):
+    k, dy, dx = block
+    return (-k) % 4, dy, dx
+
+
+RETURN_ROUNDS = tuple(
+    tuple((turned(end), turned(start), over) for start, end, over in moves)
+    for moves in reversed(TOKEN_ROUNDS)
+)
+OUTPUT_ROUNDS = (
+    (((2, 1, 1), (2, 1, 0), x_swap), ((1, 1, 0), (2, 1, 0), z_next)),
+    (((1, 1, 1), (1, 0, 1), y_swap), ((2, 0, 1), (2, 0, 0), x_swap), ((3, 1, 1), (0, 1, 1), z_next)),
+    (((1, 0, 1), (1, 0, 0), x_swap), ((2, 1, 0), (2, 0, 0), y_swap)),
+    (((3, 1, 0), (3, 0, 0), y_swap), ((3, 0, 1), (3, 0, 0), x_swap), ((1, 0, 0), (2, 0, 0), z_next)),
+    (((0, 1, 1), (0, 0, 1), y_swap), ((2, 0, 0), (3, 0, 0), z_next)),
+    (((0, 0, 1), (0, 0, 0), x_swap), ((0, 1, 0), (0, 0, 0), y_swap), ((3, 0, 0), (0, 0, 0), z_next)),
+)
+
+
+class Chain:
+    def __init__(self):
+        self.earlier = []
+        self.late = []
+        self.values = []
+
+    def add(self, *values):
+        self.earlier.extend(values)
+
+    def send(self, values, ways, late=()):
+        values = lax.optimization_barrier((*values, *self.earlier))[: len(values)]
+        self.values = values
+        results = [way(value) for value, way in zip(values, ways)]
+        self.earlier = self.late + [r for i, r in enumerate(results) if i not in late]
+        self.late = [results[i] for i in late]
+        return results
+
+    def round(self, values, moves, others):
+        late = [i for i, move in enumerate(moves) if len(move) > 3]
+        values = values + [value for value, _ in others]
+        ways = [move[2] for move in moves] + [way for _, way in others]
+        results = self.send(values, ways, late)
+        return results[: len(moves)], results[len(moves) :]
+
+    def gather(self, pairs, others=()):
+        values = [held[move[0]] for held, moves in pairs for move in moves]
+        moves = [move for _, moves in pairs for move in moves]
+        results, rest = self.round(values, moves, others)
+        for (held, end), result in zip([(h, m[1]) for h, ms in pairs for m in ms], results):
+            held[end] = result
+        return rest
+
+    def scatter(self, pairs, others=()):
+        values = totals([terms[move[0]] for terms, moves in pairs for move in moves])
+        moves = [move for _, moves in pairs for move in moves]
+        results, rest = self.round(values, moves, others)
+        for (terms, end), result in zip([(t, m[1]) for t, ms in pairs for m in ms], results):
+            terms[end].append(result)
+        return rest
+
+
+def sum_kernel(counts, *refs):
+    outs = refs[sum(counts) :]
+    for count, out in zip(counts, outs):
+        terms, refs = refs[:count], refs[count:]
+        out[...] = plus(*[term[...] for term in terms]).astype(out.dtype)
+
+
+def totals(lists):
+    several = [terms for terms in lists if len(terms) > 1]
+    if not several:
+        return [terms[0] for terms in lists]
+    operands = [term for terms in several for term in terms]
+    rows = operands[0].shape[0] // 4
+    whole = [(a.shape[0] // 4, a.shape[1]) for a in operands]
+    specs = [pl.BlockSpec(block, lambda i: (i, 0)) for block in whole]
+    firsts = [terms[0] for terms in several]
+    sums = pl.pallas_call(
+        functools.partial(sum_kernel, [len(terms) for terms in several]),
+        grid=(4,),
+        out_shape=[jax.ShapeDtypeStruct(a.shape, low) for a in firsts],
+        in_specs=specs,
+        out_specs=[pl.BlockSpec((rows, a.shape[1]), lambda i: (i, 0)) for a in firsts],
+        name="sums",
+        compiler_params=pltpu.CompilerParams(vmem_limit_bytes=2 * ROOM),
+    )(*operands)
+    sums = list(sums)
+    return [sums.pop(0) if len(terms) > 1 else terms[0] for terms in lists]
+
+
+def dot(left, right, dims=None):
+    if dims is None:
+        return jnp.dot(left, right, preferred_element_type=wide)
+    return lax.dot_general(left, right, dims, preferred_element_type=wide)
+
+
+def lanes(start, size):
+    return pl.ds(pl.multiple_of(start, 128), size)
+
+
+def spot(ids, i):
+    return pl.multiple_of(ids[i] * 128, 128)
+
+
+def row_copies(ids, blocks, whole, sems):
+    return [
+        pltpu.make_async_copy(block, whole.at[pl.ds(spot(ids, i), 128), :], sems.at[i])
+        for i, block in enumerate(blocks)
+    ]
+
+
+def column_copies(ids, blocks, whole, sems):
+    return [
+        pltpu.make_async_copy(block, whole.at[:, pl.ds(spot(ids, i), 128)], sems.at[i])
+        for i, block in enumerate(blocks)
+    ]
+
+
+def stack_copies(blocks, whole, sems):
+    rows = blocks[0].shape[0]
+    return [
+        pltpu.make_async_copy(block, whole.at[pl.ds(i * rows, rows), :], sems.at[i])
+        for i, block in enumerate(blocks)
+    ]
+
+
+def start_all(copies):
+    for copy in copies:
+        copy.start()
+
+
+def wait_all(copies):
+    for copy in copies:
+        copy.wait()
+
+
+def head_forward(raw, gain, cosine, sine):
+    inverse = lax.rsqrt(jnp.mean(raw * raw, axis=-1, keepdims=True) + EPS)
+    unit = raw * inverse
+    shaped = unit * gain
+    return unit, inverse, shaped * cosine + pltpu.roll(shaped, 64, 1) * sine
+
+
+def head_backward(grad, unit, inverse, gain, cosine, sine):
+    back = grad * cosine - pltpu.roll(grad, 64, 1) * sine
+    gain_grad = jnp.sum(back * unit, axis=0, keepdims=True)
+    scaled = back * gain
+    return gain_grad, inverse * (scaled - unit * jnp.mean(scaled * unit, axis=-1, keepdims=True))
+
+
+def causal(core, length):
+    half = length // 2
+    rows = lax.broadcasted_iota(jnp.int32, (length, length), 0)
+    columns = lax.broadcasted_iota(jnp.int32, (length, length), 1)
+
+    def place(i):
+        return jnp.where(i < half, i + core * half, i - half + (1 - core) * half)
+
+    return place(columns) <= place(rows)
+
+
+def soft(query, key, allowed, scale):
+    scores = jnp.where(allowed, dot(query, key, NT) * scale, -1e30)
+    raised = jnp.exp(scores - jnp.max(scores, axis=-1, keepdims=True))
+    return raised / jnp.sum(raised, axis=-1, keepdims=True)
+
+
+def raw_kernel(ids, block_ids, *refs):
+    seq_blocks, blocks = refs[:4], refs[4:20]
+    raw, router, rest, whole, seq, sems = refs[20:]
+    copies = stack_copies(seq_blocks, seq, sems.at[pl.ds(16, 4)]) + row_copies(
+        ids, blocks, whole, sems
+    )
+    start_all(copies)
+    wait_all(copies)
+    width = raw.shape[1]
+
+    @pl.loop(0, width // TILE)
+    def _(j):
+        span = lanes(j * TILE, TILE)
+        raw[:, span] = dot(seq[...], whole[:, span])
+
+    router[...] = whole[:, width:]
+    for p in range(16):
+        rest[p * 128 : (p + 1) * 128, :] = whole[pl.ds(spot(block_ids, p), 128), width:]
+
+
+def forward_kernel(head_count, core, raw, cosine, sine, query_gain, key_gain, attended):
+    length = raw.shape[0] // 2
+    key_start = head_count * 128
+    allowed = causal(core[0], length)
+    scale = 128 ** (-0.5)
+    for s in range(2):
+        span = slice(s * length, (s + 1) * length)
+        turn = (cosine[...], sine[...])
+        key_raw = raw[span, key_start : key_start + 128]
+        key = head_forward(key_raw, key_gain[...], *turn)[2].astype(low)
+        value = raw[span, key_start + 128 : key_start + 256].astype(low)
+
+        @pl.loop(0, head_count, unroll=2)
+        def _(h):
+            columns = lanes(h * 128, 128)
+            query = head_forward(raw[span, columns], query_gain[...], *turn)[2].astype(low)
+            weights = soft(query, key, allowed, scale)
+            attended[span, columns] = dot(weights.astype(low), value).astype(low)
+
+
+def split_rows(product, span, sent, kept):
+    rows = product.shape[0] // 4
+    kept[:rows, span] = product[:rows]
+    sent[:rows, span] = product[rows : 2 * rows].astype(low)
+    kept[rows:, span] = product[2 * rows : 3 * rows]
+    sent[rows:, span] = product[3 * rows :].astype(low)
+
+
+def out_kernel(ids, attended, *refs):
+    blocks, (sent, kept, whole, sems) = refs[:16], refs[16:]
+    copies = column_copies(ids, blocks, whole, sems)
+    start_all(copies)
+    wait_all(copies)
+
+    @pl.loop(0, whole.shape[1] // WIDE)
+    def _(j):
+        span = lanes(j * WIDE, WIDE)
+        split_rows(dot(attended[...], whole[:, span]), span, sent, kept)
+
+
+def normed_grad_kernel(ids, grad_raw, gain, *refs):
+    seq_blocks, blocks = refs[:4], refs[4:20]
+    sent, kept, gain_grad, whole, seq, sems = refs[20:]
+    copies = row_copies(ids, blocks, whole, sems) + stack_copies(
+        seq_blocks, seq, sems.at[pl.ds(16, 4)]
+    )
+    start_all(copies)
+    wait_all(copies)
+    width = grad_raw.shape[1]
+
+    @pl.loop(0, whole.shape[0] // WIDE)
+    def _(j):
+        span = lanes(j * WIDE, WIDE)
+        product = dot(grad_raw[...], whole[span, :width], NT)
+        split_rows(product, span, sent, kept)
+        unit = seq[:, span].astype(wide) / gain[:, span]
+        gain_grad[:, span] = jnp.sum(product * unit, axis=0, keepdims=True)
+
+
+def attended_grad_kernel(ids, *refs):
+    grad_blocks, blocks = refs[:4], refs[4:20]
+    grad_attended, grad_branch, whole, sems = refs[20:]
+    copies = stack_copies(grad_blocks, grad_branch, sems.at[pl.ds(16, 4)]) + column_copies(
+        ids, blocks, whole, sems
+    )
+    start_all(copies)
+    wait_all(copies)
+
+    @pl.loop(0, grad_attended.shape[1] // WIDE)
+    def _(j):
+        span = lanes(j * WIDE, WIDE)
+        grad_attended[:, span] = dot(grad_branch[...], whole[span, :], NT).astype(low)
+
+
+def map_kernel(capacity, expert_count, experts, named, picks, turned_picks):
+    slot_rows = 4 * capacity
+    early = lax.broadcasted_iota(jnp.int32, (128, 128), 0)
+    late = lax.broadcasted_iota(jnp.int32, (128, 128), 1)
+    before = jnp.where(early < late, 1.0, 0.0).astype(low)
+    behind = jnp.where(late < early, 1.0, 0.0).astype(low)
+    slot_numbers = lax.broadcasted_iota(jnp.int32, (slot_rows, 128), 0)
+    slot_lanes = lax.broadcasted_iota(jnp.int32, (128, turned_picks.shape[1]), 1)
+    for b in range(16):
+        k, i = b // 4, b % 4
+        block = named[b * 128 : (b + 1) * 128, :]
+        turned_slots = []
+        for c in range(2):
+            column = experts[c] + expert_count
+            own_lane = lax.broadcasted_iota(jnp.int32, (8, 128), 1) == column
+            hit = dot(jnp.where(own_lane, 1.0, 0.0).astype(low), block, NT)
+            slot = dot(hit.astype(low), before) + float(i * capacity)
+            slot = jnp.where(hit > 0.5, slot, -1.0).astype(jnp.int32)
+            first = (2 * k + c) * slot_rows
+            picks[first : first + slot_rows, i * 128 : (i + 1) * 128] = jnp.where(
+                slot_numbers == slot[:1], 1.0, 0.0
+            ).astype(low)
+            mine = jnp.where(late == column, block.astype(wide), 0.0)
+            hit = jnp.sum(mine, axis=1, keepdims=True)
+            slot = jnp.sum(dot(behind, mine.astype(low)), axis=1, keepdims=True)
+            slot = slot + float(i * capacity + c * slot_rows)
+            turned_slots.append(jnp.where(hit > 0.5, slot, -1.0).astype(jnp.int32))
+        either = jnp.logical_or(slot_lanes == turned_slots[0], slot_lanes == turned_slots[1])
+        turned_picks[b * 128 : (b + 1) * 128, :] = jnp.where(either, 1.0, 0.0).astype(low)
+
+
+def pick_kernel(k, picks_in, named, *refs):
+    tokens, cots, (own, other, picks, rows, sems) = refs[:4], refs[4:8], refs[8:]
+    quad_rows, full = rows.shape
+    width = tokens[0].shape[1]
+    copies = (
+        stack_copies(tokens, rows.at[:, pl.ds(0, width)], sems.at[pl.ds(0, 4)])
+        + stack_copies(cots, rows.at[:, pl.ds(width + 128, width)], sems.at[pl.ds(4, 4)])
+        + [
+            pltpu.make_async_copy(
+                picks_in.at[pl.ds(k * picks.shape[0], picks.shape[0]), :], picks, sems.at[8]
+            ),
+            pltpu.make_async_copy(
+                named.at[pl.ds(k * quad_rows, quad_rows), :],
+                rows.at[:, pl.ds(width, 128)],
+                sems.at[9],
+            ),
+        ]
+    )
+    start_all(copies)
+    wait_all(copies)
+    slot_rows = own.shape[0]
+    for start in range(0, full, WIDE):
+        span = slice(start, min(start + WIDE, full))
+        made = dot(picks[...], rows[:, span]).astype(low)
+        own[:, span] = made[:slot_rows]
+        other[:, span] = made[slot_rows:]
+
+
+def expert_kernel(expert_count, k, experts, router, *refs):
+    sides, weights = refs[:2], refs[2:5]
+    refs = refs[5 + (5 if k else 0) :]
+    (all_rows, all_act, all_grads, all_gate, all_up, own_out, back_out) = refs[:7]
+    (rows, v_gate, v_up, v_down, act, grads, gate_back, up_back) = refs[7:15]
+    (gate_pre, up_pre, sig, sems) = refs[15:]
+    slot_rows = own_out.shape[0]
+    width, hidden = v_gate.shape
+    after_width = width + 128
+    spans = [slice(c * slot_rows, (c + 1) * slot_rows) for c in range(2)]
+    side_copies = stack_copies(sides, rows, sems.at[pl.ds(0, 2)])
+    weight_copies = [
+        pltpu.make_async_copy(a, b, sems.at[2 + i])
+        for i, (a, b) in enumerate(zip(weights, (v_gate, v_up, v_down)))
+    ]
+    start_all(side_copies + weight_copies)
+    kept = []
+
+    def keep(source, target, sem):
+        copy = pltpu.make_async_copy(
+            source.at[:, pl.ds(0, target.shape[1])],
+            target.at[pl.ds(k * 2 * slot_rows, 2 * slot_rows), :],
+            sems.at[sem],
+        )
+        copy.start()
+        kept.append(copy)
+
+    wait_all(side_copies)
+    keep(rows, all_rows, 5)
+    logits = dot(rows[:, :width], router[...])
+    numbers = lax.broadcasted_iota(jnp.int32, logits.shape, 1)
+    is_named = pltpu.roll(rows[:, width:after_width].astype(wide), 128 - expert_count, 1)
+    is_named = jnp.logical_and(is_named > 0.5, numbers < expert_count)
+    lifted = jnp.where(is_named, logits, -1e30)
+    lifted = jnp.where(
+        is_named, jnp.exp(lifted - jnp.max(lifted, axis=1, keepdims=True)), 0.0
+    )
+    mine = jnp.sum(jnp.where(numbers == experts[0], lifted, 0.0), axis=1, keepdims=True)
+    gates = mine / jnp.maximum(jnp.sum(lifted, axis=1, keepdims=True), 1e-30)
+    wait_all(weight_copies[:2])
+    pre = dot(rows[:, :width], v_gate[...])
+    up = dot(rows[:, :width], v_up[...])
+    s = jax.nn.sigmoid(pre)
+    gate_pre[...] = pre
+    up_pre[...] = up
+    sig[...] = s
+    act[...] = (pre * s * up).astype(low)
+    keep(act, all_act, 6)
+    wait_all(weight_copies[2:])
+    slot_grads = jnp.zeros((2 * slot_rows, 1), wide)
+    for j in range(width // WIDE):
+        span = slice(j * WIDE, (j + 1) * WIDE)
+        later = slice(after_width + j * WIDE, after_width + (j + 1) * WIDE)
+        out = dot(act[...], v_down[:, span]).astype(low).astype(wide)
+        cot = rows[:, later].astype(wide)
+        grads[:, span] = (gates * cot).astype(low)
+        scaled = (gates * out).astype(low)
+        own_out[:, later] = scaled[spans[0]]
+        back_out[:, later] = scaled[spans[1]]
+        slot_grads = slot_grads + jnp.sum(cot * out, axis=1, keepdims=True)
+    keep(grads, all_grads, 7)
+    back = dot(grads[...], v_down[...], NT)
+    pre, s = gate_pre[...], sig[...]
+    gate_back[...] = (back * up_pre[...] * s * (1.0 + pre * (1.0 - s))).astype(low)
+    up_back[...] = (back * (pre * s)).astype(low)
+    keep(gate_back, all_gate, 8)
+    keep(up_back, all_up, 9)
+    for j in range(width // WIDE):
+        span = slice(j * WIDE, (j + 1) * WIDE)
+        back = dot(gate_back[...], v_gate[span, :], NT) + dot(up_back[...], v_up[span, :], NT)
+        back = back.astype(low)
+        own_out[:, span] = back[spans[0]]
+        back_out[:, span] = back[spans[1]]
+    high = slot_grads.astype(low).astype(wide)
+    rest = jnp.where(numbers == experts[0] + expert_count, slot_grads - high, 0.0)
+    parts = jnp.where(numbers == experts[0], high, rest).astype(low)
+    own_out[:, width:after_width] = parts[spans[0]]
+    back_out[:, width:after_width] = parts[spans[1]]
+    wait_all(kept)
+
+
+def token_sum_kernel(k, turned_picks, *refs):
+    sides, blocks, outputs, (picks, rows, out_rows, sems) = refs[:2], refs[2:6], refs[6:10], refs[10:]
+    quad_rows, width = out_rows.shape
+    copies = stack_copies(sides, rows, sems.at[pl.ds(0, 2)]) + [
+        pltpu.make_async_copy(
+            turned_picks.at[pl.ds(k * quad_rows, quad_rows), :], picks, sems.at[2]
+        )
+    ]
+    start_all(copies)
+    wait_all(copies)
+    slots = rows.shape[0]
+    size, first = blocks[0].shape
+    for j in range(0, width, WIDE):
+        span = slice(j, j + WIDE)
+        out_rows[:, span] = dot(picks[:, :slots], rows[:, first + j : first + j + WIDE]).astype(low)
+    copies = [
+        pltpu.make_async_copy(out_rows.at[pl.ds(i * size, size), :], output, sems.at[3 + i])
+        for i, output in enumerate(outputs)
+    ]
+    start_all(copies)
+    for j in range(0, first, WIDE):
+        span = slice(j, min(j + WIDE, first))
+        made = dot(picks[:, :slots], rows[:, span]).astype(low)
+        for i, block in enumerate(blocks):
+            block[:, span] = made[i * size : (i + 1) * size]
+    wait_all(copies)
+
+
+def backward_kernel(head_count, core, raw, grad_attended, *refs):
+    cosine, sine, query_gain, key_gain = refs[:4]
+    grad_raw, query_gain_grad, key_gain_grad, key_sum, value_sum = refs[4:]
+    length = raw.shape[0] // 2
+    key_start = head_count * 128
+    allowed = causal(core[0], length)
+    scale = 128 ** (-0.5)
+    turn = (cosine[...], sine[...])
+    query_gain_grad[...] = jnp.zeros_like(query_gain_grad)
+    key_gain_grad[...] = jnp.zeros_like(key_gain_grad)
+    for s in range(2):
+        span = slice(s * length, (s + 1) * length)
+        key_raw = raw[span, key_start : key_start + 128]
+        key_unit, key_inverse, key = head_forward(key_raw, key_gain[...], *turn)
+        key = key.astype(low)
+        value = raw[span, key_start + 128 : key_start + 256].astype(low)
+        key_sum[...] = jnp.zeros_like(key_sum)
+        value_sum[...] = jnp.zeros_like(value_sum)
+
+        @pl.loop(0, head_count, unroll=2)
+        def _(h):
+            columns = lanes(h * 128, 128)
+            unit, inverse, query = head_forward(raw[span, columns], query_gain[...], *turn)
+            query = query.astype(low)
+            weights = soft(query, key, allowed, scale)
+            grad = grad_attended[span, columns]
+            grad_soft = dot(grad, value, NT)
+            inner = jnp.sum(weights * grad_soft, axis=-1, keepdims=True)
+            grad_scores = (weights * (grad_soft - inner)).astype(low)
+            value_sum[...] += dot(weights.astype(low), grad, TN)
+            key_sum[...] += dot(grad_scores, query, TN) * scale
+            grad_query = dot(grad_scores, key) * scale
+            gain_grad, back = head_backward(grad_query, unit, inverse, query_gain[...], *turn)
+            query_gain_grad[...] += gain_grad
+            grad_raw[span, columns] = back.astype(low)
+
+        gain_grad, back = head_backward(
+            key_sum[...], key_unit, key_inverse, key_gain[...], *turn
+        )
+        key_gain_grad[...] += gain_grad
+        grad_raw[span, key_start : key_start + 128] = back.astype(low)
+        grad_raw[span, key_start + 128 : key_start + 256] = value_sum[...].astype(low)
+
+
+def block_product_kernel(with_rest, ids, right, *refs):
+    left_blocks, refs = refs[:4], refs[4:]
+    rest, refs = (refs[0], refs[1:]) if with_rest else (None, refs)
+    outs, (left, sems) = refs[:16], refs[16:]
+    copies = stack_copies(left_blocks, left, sems)
+    start_all(copies)
+    wait_all(copies)
+    width = right.shape[1]
+    for i, out in enumerate(outs):
+        part = left[:, pl.ds(spot(ids, i), 128)]
+        out[:, :width] = dot(part, right[...], TN).astype(low)
+        if with_rest:
+            out[:, width:] = jnp.transpose(rest[:, pl.ds(spot(ids, i), 128)]).astype(low)
+
+
+SMEM = pl.BlockSpec(memory_space=pltpu.SMEM)
+VMEM = pl.BlockSpec(memory_space=pltpu.VMEM)
+FAR = pl.BlockSpec(memory_space=pl.ANY)
+HBM = pl.BlockSpec(memory_space=pltpu.HBM)
+
+
+def call(kernel, name, ins, outs, scratch, flops, specs=None, aliases=None, alone=False):
+    operands = [value for value, _ in ins]
+    moved = sum(a.size * a.dtype.itemsize for a in operands + outs)
+    placed = [value for value, spec in ins if spec is VMEM] + scratch
+    placed += [out for out, spec in zip(outs, specs or [VMEM] * len(outs)) if spec is VMEM]
+    held = sum(
+        math.prod(a.shape) * jnp.dtype(a.dtype).itemsize
+        for a in placed
+        if jnp.issubdtype(a.dtype, jnp.floating)
+    )
+    return pl.pallas_call(
+        kernel,
+        out_shape=outs,
+        in_specs=[spec for _, spec in ins],
+        out_specs=specs or [VMEM] * len(outs),
+        scratch_shapes=scratch,
+        name=name,
+        input_output_aliases=aliases or {},
+        compiler_params=pltpu.CompilerParams(vmem_limit_bytes=WHOLE if alone else ROOM + held),
+        cost_estimate=pl.CostEstimate(flops=flops, bytes_accessed=moved, transcendentals=0),
+    )(*operands)
+
+
+def shape(rows, columns, dtype):
+    return jax.ShapeDtypeStruct((rows, columns), dtype)
+
+
+def copies_sem(count):
+    return pltpu.SemaphoreType.DMA((count,))
+
+
+def local_sixteen(
+    inputs,
+    attention_gain,
+    query_weight,
+    key_weight,
+    value_weight,
+    query_gain,
+    key_gain,
+    out_weight,
+    feedforward_gain,
+    router_weight,
+    gate_weight,
+    up_weight,
+    down_weight,
+    routes,
+    cotangent,
+):
+    tok_rows, model_width = inputs.shape
+    head_width = query_gain.shape[0]
+    top_count = routes.shape[1]
+    expert_count = router_weight.shape[1]
+    hidden_width = gate_weight.shape[2]
+    capacity = tok_rows * top_count * 11 // (expert_count * 8)
+    query_cols, key_cols = query_weight.shape[1] // 2, key_weight.shape[1] // 2
+    raw_cols = query_cols + 2 * key_cols
+    head_count = query_cols // head_width
+    place = lax.axis_index("dp")
+    core = lax.axis_index("tensor")
+    z, y, x = place // 4, (place // 2) % 2, place % 2
+    even = z % 2 == 0
+    core_id = core.astype(jnp.int32)[None]
+    block_ids = jnp.stack(
+        [((z - k) % 4) * 4 + (y ^ dy) * 2 + (x ^ dx) for k, dy, dx in BLOCKS]
+    ).astype(jnp.int32)
+    weight_ids = jnp.stack(
+        [(z ^ w) * 4 + (y ^ dy) * 2 + (x ^ dx) for w, dy, dx in BLOCKS]
+    ).astype(jnp.int32)
+
+    def halves(values, axis):
+        first, second = jnp.split(values, 2, axis=axis)
+        return jnp.where(even, first, second), jnp.where(even, second, first)
+
+    def in_order(mine, theirs, axis):
+        return jnp.where(
+            even,
+            jnp.concatenate([mine, theirs], axis=axis),
+            jnp.concatenate([theirs, mine], axis=axis),
+        )
+
+    chain = Chain()
+    numbers = jnp.arange(expert_count, dtype=jnp.int32)
+    own_named = jnp.any(routes[:, :, None] == numbers, axis=1)
+    splits = [halves(w, 1) for w in (query_weight, key_weight, value_weight)]
+    rest = [
+        router_weight,
+        own_named.astype(low),
+        jnp.zeros((tok_rows, 128 - 2 * expert_count), low),
+    ]
+    mine = jnp.concatenate([s[0] for s in splits] + rest, axis=1)
+    theirs = jnp.concatenate([s[1] for s in splits] + rest, axis=1)
+    held = {(0, 0, 0): mine}
+    (held[1, 0, 0],) = chain.gather([(held, WEIGHT_ROUNDS[0])], [(theirs, z_pair)])
+    inputs_float = inputs.astype(wide)
+    normed_attention, attention_back = jax.vjp(rms_scale, inputs_float, attention_gain)
+    normed = normed_attention.astype(low)
+    chain.add(normed)
+    chain.gather([(held, WEIGHT_ROUNDS[1])])
+    chain.gather([(held, WEIGHT_ROUNDS[2])])
+    far, swapped = chain.gather(
+        [(held, WEIGHT_ROUNDS[3])], [(normed, z_pair), (normed, core_swap)]
+    )
+    out_mine, out_theirs = halves(out_weight, 0)
+    out_held = {(0, 0, 0): out_mine}
+    cot_held = {(0, 0, 0): cotangent}
+    far_swapped, out_held[1, 0, 0] = chain.gather(
+        [(held, WEIGHT_ROUNDS[4]), (out_held, SHORT_ROUNDS[0])],
+        [(far, core_swap), (out_theirs, z_pair)],
+    )
+    sequence = [normed, swapped, far, far_swapped]
+    blocks = [held[b] for b in BLOCKS]
+    chain.gather([(out_held, SHORT_ROUNDS[1])])
+    grad_output = cotangent.astype(wide)
+    length = 2 * tok_rows
+    own_places = jnp.arange(tok_rows, dtype=jnp.int32)
+    places = jnp.concatenate([own_places + core * tok_rows, own_places + (1 - core) * tok_rows])
+    halfway = head_width // 2
+    frequency = THETA ** (-(jnp.arange(halfway, dtype=wide) * 2.0 / head_width))
+    angles = places.astype(wide)[:, None] * frequency[None, :]
+    cosine, sine = jnp.cos(angles), jnp.sin(angles)
+    turns = [
+        (jnp.concatenate([cosine, cosine], axis=1), VMEM),
+        (jnp.concatenate([-sine, sine], axis=1), VMEM),
+        (query_gain[None, :], VMEM),
+        (key_gain[None, :], VMEM),
+    ]
+    both = 2 * length
+    raw, router_rows, rest_rows = call(
+        raw_kernel,
+        "attention_raw",
+        [(weight_ids, SMEM), (block_ids, SMEM)]
+        + [(b, FAR) for b in sequence]
+        + [(b, HBM) for b in blocks],
+        [
+            shape(both, raw_cols, wide),
+            shape(model_width, 128, low),
+            shape(model_width, 128, low),
+        ],
+        [
+            pltpu.VMEM((model_width, raw_cols + 128), low),
+            pltpu.VMEM((both, model_width), low),
+            copies_sem(20),
+        ],
+        2 * both * model_width * raw_cols,
+        alone=True,
+    )
+    chain.add(raw)
+    chain.gather([(out_held, SHORT_ROUNDS[2])])
+    (attended,) = call(
+        functools.partial(forward_kernel, head_count),
+        "attention_forward",
+        [(core_id, SMEM), (raw, VMEM)] + turns,
+        [shape(both, query_cols, low)],
+        [],
+        4 * both * length * query_cols,
+    )
+    chain.add(attended)
+    chain.gather([(out_held, SHORT_ROUNDS[3])])
+    out_blocks = [out_held[b] for b in BLOCKS]
+    chain.gather([(cot_held, TOKEN_ROUNDS[0])])
+    sent, kept = call(
+        out_kernel,
+        "attention_out",
+        [(weight_ids, SMEM), (attended, VMEM)] + [(b, HBM) for b in out_blocks],
+        [shape(length, model_width, low), shape(length, model_width, wide)],
+        [pltpu.VMEM((query_cols, model_width), low), copies_sem(16)],
+        2 * both * model_width * query_cols,
+    )
+
+    pair_total = kept + core_swap(sent).astype(wide)
+    leaving = pair_total[tok_rows:].astype(low)
+    from_pair = z_pair(leaving)
+    chain.add(leaving)
+    chain.gather([(cot_held, TOKEN_ROUNDS[1])])
+    chain.gather([(cot_held, TOKEN_ROUNDS[2])])
+    hidden = inputs_float + pair_total[:tok_rows] + from_pair.astype(wide)
+    normed_experts, experts_back = jax.vjp(rms_scale, hidden, feedforward_gain)
+    moe_in = normed_experts.astype(low)
+    chain.add(moe_in)
+
+    token_held = {(0, 0, 0): moe_in}
+    chain.gather([(token_held, TOKEN_ROUNDS[0])])
+    chain.gather([(token_held, TOKEN_ROUNDS[1])])
+    slot_rows = 4 * capacity
+    quad_rows = 4 * tok_rows
+    rows_of = 2 * slot_rows
+    all_slots = 4 * rows_of
+    experts = jnp.stack([place * 2 + core, place * 2 + 1 - core]).astype(jnp.int32)
+    w_gate, w_up, w_down = gate_weight[0], up_weight[0], down_weight[0]
+    turned_width = -(-rows_of // 128) * 128
+    picks, turned_picks = call(
+        functools.partial(map_kernel, capacity, expert_count),
+        "pick_maps",
+        [(experts, SMEM), (rest_rows, VMEM)],
+        [shape(all_slots, quad_rows, low), shape(model_width, turned_width, low)],
+        [],
+        2 * 128 * 128 * model_width,
+    )
+
+    logits = jnp.dot(moe_in, router_rows, preferred_element_type=wide)[:, :expert_count]
+    lifted = jnp.where(own_named, logits, -1e30)
+    lifted = jnp.where(own_named, jnp.exp(lifted - jnp.max(lifted, axis=1, keepdims=True)), 0.0)
+    gate_dense = lifted / jnp.sum(lifted, axis=1, keepdims=True)
+
+    full = 2 * model_width + 128
+
+    def pick_tokens(k, *earlier):
+        return call(
+            functools.partial(pick_kernel, k),
+            "picks",
+            [(after(picks, *earlier), FAR), (rest_rows, FAR)]
+            + [(token_held[k, dy, dx], FAR) for dy, dx in PLANE]
+            + [(cot_held[k, dy, dx], HBM) for dy, dx in PLANE],
+            [shape(slot_rows, full, low)] * 2,
+            [
+                pltpu.VMEM((rows_of, quad_rows), low),
+                pltpu.VMEM((quad_rows, full), low),
+                copies_sem(10),
+            ],
+            2 * rows_of * quad_rows * full,
+            alone=k == 0,
+        )
+
+    stores = []
+
+    def run_experts(k, own, back):
+        ins = (
+            [(experts, SMEM), (router_rows, VMEM), (own, FAR), (back, FAR)]
+            + [(w, HBM) for w in (w_gate, w_up, w_down)]
+        )
+        made = call(
+            functools.partial(expert_kernel, expert_count, k),
+            "experts",
+            ins + [(store, HBM) for store in stores],
+            [
+                shape(all_slots, model_width, low),
+                shape(all_slots, hidden_width, low),
+                shape(all_slots, model_width, low),
+                shape(all_slots, hidden_width, low),
+                shape(all_slots, hidden_width, low),
+                shape(slot_rows, full, low),
+                shape(slot_rows, full, low),
+            ],
+            [
+                pltpu.VMEM((rows_of, full), low),
+                pltpu.VMEM((model_width, hidden_width), low),
+                pltpu.VMEM((model_width, hidden_width), low),
+                pltpu.VMEM((hidden_width, model_width), low),
+                pltpu.VMEM((rows_of, hidden_width), low),
+                pltpu.VMEM((rows_of, model_width), low),
+                pltpu.VMEM((rows_of, hidden_width), low),
+                pltpu.VMEM((rows_of, hidden_width), low),
+                pltpu.VMEM((rows_of, hidden_width), wide),
+                pltpu.VMEM((rows_of, hidden_width), wide),
+                pltpu.VMEM((rows_of, hidden_width), wide),
+                copies_sem(10),
+            ],
+            12 * rows_of * model_width * hidden_width,
+            [HBM] * 5 + [VMEM] * 2,
+            {len(ins) + i: i for i in range(len(stores))},
+        )
+        stores[:] = made[:5]
+        return made[5:]
+
+    terms, y_terms = {}, {}
+
+    def sum_tokens(k, own, back):
+        made = call(
+            functools.partial(token_sum_kernel, k),
+            "token_sums",
+            [(turned_picks, FAR), (own, FAR), (back, FAR)],
+            [shape(tok_rows, model_width + 128, low)] * 4 + [shape(tok_rows, model_width, low)] * 4,
+            [
+                pltpu.VMEM((quad_rows, turned_width), low),
+                pltpu.VMEM((rows_of, full), low),
+                pltpu.VMEM((quad_rows, model_width), low),
+                copies_sem(7),
+            ],
+            2 * rows_of * quad_rows * full,
+            [VMEM] * 4 + [HBM] * 4,
+        )
+        for i, p in enumerate(PLANE):
+            terms[(k, *p)] = [made[i]]
+            y_terms[(k, *p)] = [made[4 + i]]
+        return made[0]
+
+    def row_product(left, right, *earlier):
+        return lax.dot_general(after(left, *earlier), right, TN, preferred_element_type=wide)[None]
+
+    own, other = pick_tokens(0)
+    chain.add(other)
+    (back,) = chain.gather([(token_held, TOKEN_ROUNDS[2])], [(other, core_swap)])
+    own, sent = run_experts(0, own, back)
+    chain.add(sent)
+    (back,) = chain.gather([(token_held, TOKEN_ROUNDS[3])], [(sent, core_swap)])
+    summed = sum_tokens(0, own, back)
+    chain.gather([(cot_held, TOKEN_ROUNDS[3])])
+    own, other = pick_tokens(1, summed)
+    (back,) = chain.gather([(token_held, TOKEN_ROUNDS[4])], [(other, core_swap)])
+    own, sent = run_experts(1, own, back)
+    chain.add(own)
+    chain.gather([(cot_held, TOKEN_ROUNDS[4])])
+    own_two, other_two = pick_tokens(2, sent)
+    back, back_two = chain.send([sent, other_two], [core_swap] * 2)
+    first_own, first_back = own, back
+    own, sent = run_experts(2, own_two, back_two)
+    own_three, other_three = pick_tokens(3, sent)
+    back, back_three = chain.send([sent, other_three], [core_swap] * 2)
+    sum_tokens(1, after(first_own, sent), first_back)
+    sum_tokens(2, own, back)
+    chain.scatter([(terms, RETURN_ROUNDS[0]), (y_terms, OUTPUT_ROUNDS[0])])
+    own, sent = run_experts(3, own_three, back_three)
+    all_rows, all_act, all_grads, all_gate, all_up = stores
+    (back,) = chain.send([sent], [core_swap])
+    sum_tokens(3, own, back)
+    weight_grads = []
+    for moves, pair in zip(
+        RETURN_ROUNDS[1:], ((all_act, all_grads), (all_rows, all_gate), (all_rows, all_up), None)
+    ):
+        chain.scatter([(terms, moves)])
+        if pair:
+            weight_grads.append(row_product(*pair, *chain.values))
+            chain.add(weight_grads[-1])
+    grad_down, grad_gate, grad_up = weight_grads
+
+    summed = plus(*terms[0, 0, 0])
+    gate_parts = summed[:, model_width:]
+    grad_gates = gate_parts[:, :expert_count] + gate_parts[:, expert_count : 2 * expert_count]
+    grad_logits = gate_dense * (
+        grad_gates - jnp.sum(gate_dense * grad_gates, axis=1, keepdims=True)
+    )
+    router_wide = router_rows[:, :expert_count].astype(wide)
+    grad_moe_in = summed[:, :model_width] + jnp.einsum(
+        "te,de->td", grad_logits, router_wide, precision=HIGH
+    )
+
+    grad_hidden_norm, grad_feed_gain = experts_back(grad_moe_in)
+    grad_hidden = grad_output + grad_hidden_norm
+    grad_own = grad_hidden.astype(low)
+    chain.scatter([(y_terms, OUTPUT_ROUNDS[1])])
+    chain.add(grad_own)
+    far, swapped = chain.scatter(
+        [(y_terms, OUTPUT_ROUNDS[2])], [(grad_own, z_pair), (grad_own, core_swap)]
+    )
+
+    grad_router = jnp.einsum(
+        "td,te->ed", moe_in.astype(wide), after(grad_logits, grad_own), precision=HIGH
+    )
+    (far_swapped,) = chain.scatter([(y_terms, OUTPUT_ROUNDS[3])], [(far, core_swap)])
+    grad_branch = [grad_own, swapped, far, far_swapped]
+
+    def block_products(left_blocks, right, rest, name):
+        width = right.shape[1] + (0 if rest is None else 128)
+        return call(
+            functools.partial(block_product_kernel, rest is not None),
+            name,
+            [(weight_ids, SMEM), (right, VMEM)]
+            + [(b, FAR) for b in left_blocks]
+            + ([] if rest is None else [(rest, VMEM)]),
+            [shape(tok_rows, width, low)] * 16,
+            [pltpu.VMEM((both, model_width), low), copies_sem(4)],
+            2 * both * model_width * right.shape[1],
+        )
+
+    out_products = block_products(grad_branch, attended, None, "out_weight_grad")
+    out_terms = {b: [block] for b, block in zip(BLOCKS, out_products)}
+    chain.add(out_products[0])
+    (router_part,) = chain.scatter(
+        [(y_terms, OUTPUT_ROUNDS[4]), (out_terms, WEIGHT_RETURNS[0])], [(grad_router, core_swap)]
+    )
+    grad_router = grad_router + router_part
+    (grad_attended,) = call(
+        attended_grad_kernel,
+        "attended_grad",
+        [(weight_ids, SMEM)]
+        + [(b, FAR) for b in (after(grad_branch[0], out_products[0]), *grad_branch[1:])]
+        + [(b, HBM) for b in out_blocks],
+        [shape(both, query_cols, low)],
+        [
+            pltpu.VMEM((both, model_width), low),
+            pltpu.VMEM((query_cols, model_width), low),
+            copies_sem(20),
+        ],
+        2 * both * model_width * query_cols,
+    )
+    chain.add(grad_attended)
+    (router_part,) = chain.scatter([(out_terms, WEIGHT_RETURNS[1])], [(grad_router, z_pair)])
+    grad_rest = jnp.pad(grad_router + router_part, ((0, 128 - expert_count), (0, 0)))
+    grad_raw, query_gain_grad, key_gain_grad = call(
+        functools.partial(backward_kernel, head_count),
+        "attention_backward",
+        [(core_id, SMEM), (raw, VMEM), (after(grad_attended, *chain.values), VMEM)] + turns,
+        [shape(both, raw_cols, low), shape(1, head_width, wide), shape(1, head_width, wide)],
+        [pltpu.VMEM((length, head_width), wide), pltpu.VMEM((length, head_width), wide)],
+        10 * both * length * query_cols,
+    )
+    chain.add(grad_raw)
+    chain.scatter([(out_terms, WEIGHT_RETURNS[2])])
+    raw_products = block_products(
+        sequence, after(grad_raw, *chain.values), grad_rest, "raw_weight_grad"
+    )
+    raw_terms = {b: [block] for b, block in zip(BLOCKS, raw_products)}
+    chain.add(raw_products[0])
+    chain.scatter([(raw_terms, WEIGHT_RETURNS[0]), (y_terms, OUTPUT_ROUNDS[5])])
+    sent, kept, attention_part = call(
+        normed_grad_kernel,
+        "normed_grad",
+        [
+            (weight_ids, SMEM),
+            (after(grad_raw, *chain.values), VMEM),
+            (attention_gain[None, :], VMEM),
+        ]
+        + [(b, FAR) for b in sequence]
+        + [(b, HBM) for b in blocks],
+        [
+            shape(length, model_width, low),
+            shape(length, model_width, wide),
+            shape(1, model_width, wide),
+        ],
+        [
+            pltpu.VMEM((model_width, raw_cols + 128), low),
+            pltpu.VMEM((both, model_width), low),
+            copies_sem(20),
+        ],
+        2 * both * model_width * raw_cols,
+    )
+    chain.add(kept)
+    gains = jnp.concatenate(
+        [attention_part[0], grad_feed_gain, query_gain_grad[0], key_gain_grad[0]]
+    ).reshape(-1, head_width)
+    from_core, gain_part = chain.scatter(
+        [(out_terms, WEIGHT_RETURNS[3])], [(sent, core_swap), (gains, core_swap)]
+    )
+    pair_total = kept + from_core.astype(wide)
+    gains = gains + gain_part
+    from_pair, gain_part = chain.scatter(
+        [(raw_terms, WEIGHT_RETURNS[1])],
+        [(pair_total[tok_rows:].astype(low), z_pair), (gains, x_swap)],
+    )
+    gains = gains + gain_part
+    chain.scatter([(raw_terms, WEIGHT_RETURNS[2]), (out_terms, WEIGHT_RETURNS[4])])
+    grad_normed = pair_total[:tok_rows] + from_pair.astype(wide)
+    grad_inputs_norm, _ = attention_back(grad_normed)
+    grad_inputs = grad_hidden + grad_inputs_norm
+    gains = gains + y_swap(after(gains, *chain.values))
+    chain.add(grad_inputs, gains)
+    out_theirs = plus(*out_terms[1, 0, 0]).astype(low)
+    out_theirs, gain_part = chain.scatter(
+        [(raw_terms, WEIGHT_RETURNS[3])], [(out_theirs, z_pair), (gains, z_pair)]
+    )
+    gains = gains + gain_part
+    raw_theirs = plus(*raw_terms[1, 0, 0]).astype(low)
+    raw_theirs, gain_part = chain.scatter(
+        [(raw_terms, WEIGHT_RETURNS[4])], [(raw_theirs, z_pair), (gains, z_far)]
+    )
+    gains = (gains + gain_part).reshape(-1)
+    output = (hidden + plus(*y_terms[0, 0, 0])).astype(low)
+    grad_out_weight = in_order(plus(*out_terms[0, 0, 0]), out_theirs.astype(wide), 1).T
+    mine, theirs = plus(*raw_terms[0, 0, 0]), raw_theirs.astype(wide)
+    spans = ((0, query_cols), (query_cols, query_cols + key_cols), (query_cols + key_cols, raw_cols))
+    grad_query_weight, grad_key_weight, grad_value_weight = [
+        in_order(mine[:, a:b], theirs[:, a:b], 1) for a, b in spans
+    ]
+    router_share = mine[:, raw_cols : raw_cols + expert_count]
+    return (
+        output,
+        grad_inputs,
+        gains[:model_width],
+        grad_query_weight,
+        grad_key_weight,
+        grad_value_weight,
+        gains[2 * model_width : 2 * model_width + head_width],
+        gains[2 * model_width + head_width :],
+        grad_out_weight,
+        gains[model_width : 2 * model_width],
+        router_share,
+        grad_gate,
+        grad_up,
+        grad_down,
+    )
+
+
 def solution(mesh):
     in_specs = (
         P(("dp", "tensor"), None),
@@ -342,4 +1435,6 @@
         P(("dp", "tensor"), None, None),
         P(("dp", "tensor"), None, None),
     )
+    fits = mesh.shape["dp"] == 16 and mesh.shape["tensor"] == 2
+    local = local_sixteen if fits else local_any
     return jax.shard_map(local, mesh=mesh, in_specs=in_specs, out_specs=out_specs, check_vma=False)

time: 1860 us -> 682 us (0.37)
  waiting for transfers between devices: 1380 us -> 330 us
  Pallas kernels: 0 us -> 145 us
  starting transfers between devices: 15.1 us -> 130 us
  matrix products: 142 us -> 28.5 us
  other arithmetic: 110 us -> 14 us
  local copies, waits for them, and re-layouts: 110 us -> 22.8 us
  blocking collectives: 83 us -> 0 us
    reduce_scatter x3 -> x0, waiting for transfers between devices: 511 us -> none  [the longest x1 501 us: local(): lax.psum_scatter(jnp.concatenate([inward, outward], axis=1), 'dp', scatte...]
    all_to_all x4 -> x0, waiting for transfers between devices: 490 us -> none  [route_rows(): lax.all_to_all(buffer, ('dp', 'tensor'), split_axis=0, concat_axis=0, til...]
    all_gather x6 -> x0, waiting for transfers between devices: 352 us -> none  [the longest x1 122 us: local(): lax.all_gather(out_weight, 'dp', axis=1, tiled=True)]
    ppermute x0 -> x145, waiting for transfers between devices: none -> 330 us  [the longest x20 91 us: z_next(): return lax.ppermute(block, 'dp', Z_RING)]
    pallas_call x0 -> x36, Pallas kernels: none -> 145 us  [the longest x21 141 us: call(): pl.pallas_call(kernel, out_shape=outs, in_specs=[spec for _, spec in ins]...]
    ppermute x0 -> x145, starting transfers between devices: none -> 130 us  [the longest x44 51.1 us: x_swap(): return lax.ppermute(block, 'dp', X_PAIR)]
    dot_general x30 -> x6, matrix products: 142 us -> 28.5 us  [the longest x3 26.8 us: row_product(): lax.dot_general(after(left, *earlier), right, TN, preferred_element_type=...]
    psum x1 -> x0, blocking collectives: 44.3 us -> none  [local(): lax.psum((grad_router, grad_attention_gain, grad_query_gain, grad_key_gai...]
  transfers between devices with their start and end apart: 14 -> 145, of which waited for: 12 -> 69; matrix products, arithmetic and copies ran while one was open for 14% -> 6% of each run, Pallas kernels for 0% -> 20%
where the time goes in v1:
time: 682 us; the launch traced here: 674 us
  waiting for transfers between devices  330 us (48%)
  Pallas kernels  145 us (21%)
  starting transfers between devices  130 us (19%)
  matrix products  28.5 us (4%)
  local copies, waits for them, and re-layouts  22.8 us (3%)
  other arithmetic  14 us (2%)
    pallas_call x21, Pallas kernels, call(): pl.pallas_call(kernel, out_shape=outs, in_specs=[spec for _, spec in ins]...  141 us
    ppermute x20, waiting for transfers between devices, z_next(): return lax.ppermute(block, 'dp', Z_RING)  91 us
    ppermute x44, waiting for transfers between devices, x_swap(): return lax.ppermute(block, 'dp', X_PAIR)  90 us
    ppermute x45, waiting for transfers between devices, y_swap(): return lax.ppermute(block, 'dp', Y_PAIR)  76.8 us
    ppermute x44, starting transfers between devices, x_swap(): return lax.ppermute(block, 'dp', X_PAIR)  51.1 us
    ppermute x45, starting transfers between devices, y_swap(): return lax.ppermute(block, 'dp', Y_PAIR)  48 us
    ppermute x10, waiting for transfers between devices, z_pair(): return lax.ppermute(block, 'dp', Z_PAIR)  35.2 us
    dot_general x3, matrix products, row_product(): lax.dot_general(after(left, *earlier), right, TN, preferred_element_type=...  26.8 us
  transfers between devices with their start and end apart: 145, of which 69 were waited for; matrix products, arithmetic and copies ran while one was open for 6% of the time, Pallas kernels for 20%

profile of v1, /device:TPU:0, one launch (start us, length us, event | category | flops | bytes accessed | tf_op | source)
XLA Modules:
  0.0 674.1 jit_solution(6091100641889669275)
XLA Ops:
  14.5 7.6 %collective-permute-done.refs_8_ = bf16[128,1408]{1,0:T(8,128)(2,1)S(1)} collective-permute-done((bf16[128,1408]{1,0:T(8,128)(2,1)S(1)}, bf16[128,1408]{1,0:T(8,128)(2,1)S(1)}, u32[]{:S(2)}, u32[]{:S(2)}) %collective-permute-start) | collective-permute-done | bytes 360480 | tf_op jit(solution)/shard_map/ppermute | solution.py:339
  27.9 9.5 %collective-permute-done.4.refs_12_ = bf16[128,1408]{1,0:T(8,128)(2,1)S(1)} collective-permute-done((bf16[128,1408]{1,0:T(8,128)(2,1)S(1)}, bf16[128,1408]{1,0:T(8,128)(2,1)S(1)}, u32[]{:S(2)}, u32[]{:S(2)}) %collective-permute-start.4) | collective-permute-done | bytes 360480 | tf_op jit(solution)/shard_map/ppermute | solution.py:343
  44.9 7.0 %collective-permute-done.10.refs_11_ = bf16[128,1408]{1,0:T(8,128)(2,1)S(1)} collective-permute-done((bf16[128,1408]{1,0:T(8,128)(2,1)S(1)}, bf16[128,1408]{1,0:T(8,128)(2,1)S(1)}, u32[]{:S(2)}, u32[]{:S(2)}) %collective-permute-start.10) | collective-permute-done | bytes 360480 | tf_op jit(solution)/shard_map/ppermute | solution.py:351
  62.0 6.7 %collective-permute-done.13.refs_18_ = bf16[128,1408]{1,0:T(8,128)(2,1)} collective-permute-done((bf16[128,1408]{1,0:T(8,128)(2,1)S(1)}, bf16[128,1408]{1,0:T(8,128)(2,1)}, u32[]{:S(2)}, u32[]{:S(2)}) %collective-permute-start.13) | collective-permute-done | bytes 360480 | tf_op jit(solution)/shard_map/ppermute | solution.py:347
  81.5 11.0 %collective-permute-done.18.refs_1_.refs_5_ = bf16[1024,128]{1,0:T(8,128)(2,1)S(1)} collective-permute-done((bf16[1024,128]{1,0:T(8,128)(2,1)S(1)}, bf16[1024,128]{1,0:T(8,128)(2,1)S(1)}, u32[]{:S(2)}, u32[]{:S(2)}) %collective-permute-start.18) | collective-permute-done | bytes 262176 | tf_op jit(solution)/shard_map/ppermute | solution.py:351
  101.9 9.8 %attention_raw.1 = (f32[512,1280]{1,0:T(8,128)}, bf16[2048,128]{1,0:T(8,128)(2,1)}, bf16[2048,128]{1,0:T(8,128)(2,1)}) custom-call(s32[16]{0:T(128)} %stack.127.ids, s32[16]{0:T(128)} %stack.144.block_ids, bf16[128,2048]{1,0:T(8,128)(2,1)} %copy-done.22, bf16[128,2048]{1,0:T(8,128)(2,1)} %copy-done.47, bf16[128,2048]{1,0:T(8,128)(2,1)} %copy-done.49, ...), custom_call_target="tpu_custom_call" | custom-call | flops 2684354560 | bytes 11534464 | tf_op jit(solution)/shard_map/attention_raw/pallas_call | solution.py:932
  117.5 9.4 %attention_forward.1.attended.right = bf16[512,1024]{1,0:T(8,128)(2,1)S(1)} custom-call(s32[1]{0:T(128)} %bitcast.16.core, f32[512,1280]{1,0:T(8,128)S(1)} %copy-done.8, f32[256,128]{1,0:T(8,128)S(1)} %pad_maximum_fusion.cosine.refs_0_, f32[256,128]{1,0:T(8,128)S(1)} %pad_maximum_fusion.1.sine.refs_1_, f32[1,128]{1,0:T(1,128)S(1)} %bitcast.98, ...), custom_call_target="tpu_custom_call" | custom-call | flops 536870912 | bytes 3933188 | tf_op jit(solution)/shard_map/attention_forward/pallas_call | solution.py:932
  151.0 13.0 %collective-permute-done.35.refs_4_ = bf16[128,2048]{1,0:T(8,128)(2,1)S(1)} collective-permute-done((bf16[128,2048]{1,0:T(8,128)(2,1)S(1)}, bf16[128,2048]{1,0:T(8,128)(2,1)S(1)}, u32[]{:S(2)}, u32[]{:S(2)}) %collective-permute-start.35) | collective-permute-done | bytes 524320 | tf_op jit(solution)/shard_map/ppermute | solution.py:335
  167.5 13.2 %collective-permute-done.38.refs_4_ = bf16[128,2048]{1,0:T(8,128)(2,1)S(1)} collective-permute-done((bf16[128,2048]{1,0:T(8,128)(2,1)S(1)}, bf16[128,2048]{1,0:T(8,128)(2,1)S(1)}, u32[]{:S(2)}, u32[]{:S(2)}) %collective-permute-start.38) | collective-permute-done | bytes 524320 | tf_op jit(solution)/shard_map/ppermute | solution.py:335
  183.7 8.0 %collective-permute-done.34 = bf16[128,2048]{1,0:T(8,128)(2,1)S(1)} collective-permute-done((bf16[128,2048]{1,0:T(8,128)(2,1)S(1)}, bf16[128,2048]{1,0:T(8,128)(2,1)S(1)}, u32[]{:S(2)}, u32[]{:S(2)}) %collective-permute-start.34) | collective-permute-done | bytes 524320 | tf_op jit(solution)/shard_map/ppermute | solution.py:339
  194.9 7.0 %collective-permute-done.43.refs_4_ = bf16[128,2048]{1,0:T(8,128)(2,1)} collective-permute-done((bf16[128,2048]{1,0:T(8,128)(2,1)S(1)}, bf16[128,2048]{1,0:T(8,128)(2,1)}, u32[]{:S(2)}, u32[]{:S(2)}) %collective-permute-start.43) | collective-permute-done | bytes 524320 | tf_op jit(solution)/shard_map/ppermute | solution.py:335
  204.1 10.5 %collective-permute-done.44.refs_1_ = bf16[128,2048]{1,0:T(8,128)(2,1)} collective-permute-done((bf16[128,2048]{1,0:T(8,128)(2,1)S(1)}, bf16[128,2048]{1,0:T(8,128)(2,1)}, u32[]{:S(2)}, u32[]{:S(2)}) %collective-permute-start.44) | collective-permute-done | bytes 524320 | tf_op jit(solution)/shard_map/ppermute | solution.py:351
  243.8 11.4 %experts.4 = (bf16[1408,2048]{1,0:T(8,128)(2,1)}, bf16[1408,768]{1,0:T(8,128)(2,1)S(1)}, bf16[1408,2048]{1,0:T(8,128)(2,1)}, bf16[1408,768]{1,0:T(8,128)(2,1)S(1...) custom-call(s32[2]{0:T(128)S(1)} %pad_add_fusion.experts, ...), custom_call_target="tpu_custom_call" | custom-call | flops 6643777536 | bytes 33931272 | tf_op jit(solution)/shard_map/experts/pallas_call | solution.py:932
  257.4 14.3 %collective-permute-done.55.refs_3_ = bf16[128,2048]{1,0:T(8,128)(2,1)S(1)} collective-permute-done((bf16[128,2048]{1,0:T(8,128)(2,1)}, bf16[128,2048]{1,0:T(8,128)(2,1)S(1)}, u32[]{:S(2)}, u32[]{:S(2)}) %collective-permute-start.55) | collective-permute-done | bytes 524320 | tf_op jit(solution)/shard_map/ppermute | solution.py:335
  278.0 9.5 %collective-permute-done.58.refs_7_ = bf16[128,2048]{1,0:T(8,128)(2,1)S(1)} collective-permute-done((bf16[128,2048]{1,0:T(8,128)(2,1)S(1)}, bf16[128,2048]{1,0:T(8,128)(2,1)S(1)}, u32[]{:S(2)}, u32[]{:S(2)}) %collective-permute-start.58) | collective-permute-done | bytes 524320 | tf_op jit(solution)/shard_map/ppermute | solution.py:335
  294.0 12.6 %experts.5 = (bf16[1408,2048]{1,0:T(8,128)(2,1)}, bf16[1408,768]{1,0:T(8,128)(2,1)S(1)}, bf16[1408,2048]{1,0:T(8,128)(2,1)}, bf16[1408,768]{1,0:T(8,128)(2,1)S(1...) custom-call(s32[2]{0:T(128)S(1)} %pad_add_fusion.experts, ...), custom_call_target="tpu_custom_call", output_to_operand_aliasing={{0}: (7, {}), {1}: (8, {}), {2}: (9, {}), {3}: (10, {}), {4... | custom-call | flops 6643777536 | bytes 51953672 | tf_op jit(solution)/shard_map/experts/pallas_call | solution.py:932
  310.5 10.5 %collective-permute-done.65.refs_7_ = bf16[128,2048]{1,0:T(8,128)(2,1)S(1)} collective-permute-done((bf16[128,2048]{1,0:T(8,128)(2,1)S(1)}, bf16[128,2048]{1,0:T(8,128)(2,1)S(1)}, u32[]{:S(2)}, u32[]{:S(2)}) %collective-permute-start.65) | collective-permute-done | bytes 524320 | tf_op jit(solution)/shard_map/ppermute | solution.py:351
  329.9 11.5 %experts.6 = (bf16[1408,2048]{1,0:T(8,128)(2,1)}, bf16[1408,768]{1,0:T(8,128)(2,1)S(1)}, bf16[1408,2048]{1,0:T(8,128)(2,1)}, bf16[1408,768]{1,0:T(8,128)(2,1)S(1...) custom-call(s32[2]{0:T(128)S(1)} %pad_add_fusion.experts, ...), custom_call_target="tpu_custom_call", output_to_operand_aliasing={{0}: (7, {}), {1}: (8, {}), {2}: (9, {}), {3}: (10, {}), {4... | custom-call | flops 6643777536 | bytes 51953672 | tf_op jit(solution)/shard_map/experts/pallas_call | solution.py:932
  362.7 11.9 %experts.7 = (bf16[1408,2048]{1,0:T(8,128)(2,1)}, bf16[1408,768]{1,0:T(8,128)(2,1)S(1)}, bf16[1408,2048]{1,0:T(8,128)(2,1)}, bf16[1408,768]{1,0:T(8,128)(2,1)S(1...) custom-call(s32[2]{0:T(128)S(1)} %pad_add_fusion.experts, ...), custom_call_target="tpu_custom_call", output_to_operand_aliasing={{0}: (7, {}), {1}: (8, {}), {2}: (9, {}), {3}: (10, {}), {4... | custom-call | flops 6643777536 | bytes 51953672 | tf_op jit(solution)/shard_map/experts/pallas_call | solution.py:932
  374.6 10.7 %collective-permute-done.75.refs_3_ = bf16[128,2048]{1,0:T(8,128)(2,1)S(1)} collective-permute-done((bf16[128,2048]{1,0:T(8,128)(2,1)}, bf16[128,2048]{1,0:T(8,128)(2,1)S(1)}, u32[]{:S(2)}, u32[]{:S(2)}) %collective-permute-start.75) | collective-permute-done | bytes 524320 | tf_op jit(solution)/shard_map/ppermute | solution.py:351
  397.7 9.7 %convolution_bitcast_fusion.2 = f32[1,768,2048]{2,1,0:T(8,128)} fusion(bf16[1408,768]{1,0:T(8,128)(2,1)S(1)} %get-tuple-element.444, bf16[1408,2048]{1,0:T(8,128)(2,1)} %get-tuple-element.445), kind=kOutput, calls=%fused_computation.2 | convolution fusion | flops 4429185024 | bytes 14221312 | tf_op jit(solution)/shard_map/dot_general | solution.py:1209
  414.2 9.9 %convolution_bitcast_fusion.1 = f32[1,2048,768]{2,1,0:T(8,128)} fusion(bf16[1408,2048]{1,0:T(8,128)(2,1)} %get-tuple-element.461, bf16[1408,768]{1,0:T(8,128)(2,1)S(1)} %get-tuple-element.453), kind=kOutput, calls=%fused_computation.1 | convolution fusion | flops 4429185024 | bytes 14221312 | tf_op jit(solution)/shard_map/dot_general | solution.py:1209
  431.5 7.2 %convolution_bitcast_fusion = f32[1,2048,768]{2,1,0:T(8,128)} fusion(bf16[1408,2048]{1,0:T(8,128)(2,1)S(1)} %bitcast.103, bf16[1408,768]{1,0:T(8,128)(2,1)S(1)} %get-tuple-element.462), kind=kOutput, calls=%fused_computation | convolution fusion | flops 4429185024 | bytes 14221312 | tf_op jit(solution)/shard_map/dot_general | solution.py:1209
  448.1 8.4 %collective-permute-done.87 = bf16[128,2176]{1,0:T(8,128)(2,1)S(1)} collective-permute-done((bf16[128,2176]{1,0:T(8,128)(2,1)S(1)}, bf16[128,2176]{1,0:T(8,128)(2,1)S(1)}, u32[]{:S(2)}, u32[]{:S(2)}) %collective-permute-start.87) | collective-permute-done | bytes 557088 | tf_op jit(solution)/shard_map/ppermute | solution.py:351
  476.3 7.3 %collective-permute-done.95.refs_1_ = bf16[128,2048]{1,0:T(8,128)(2,1)S(1)} collective-permute-done((bf16[128,2048]{1,0:T(8,128)(2,1)S(1)}, bf16[128,2048]{1,0:T(8,128)(2,1)S(1)}, u32[]{:S(2)}, u32[]{:S(2)}) %collective-permute-start.95) | collective-permute-done | bytes 524320 | tf_op jit(solution)/shard_map/ppermute | solution.py:351
  494.3 10.3 %collective-permute-done.98.refs_5_ = bf16[128,2048]{1,0:T(8,128)(2,1)S(1)} collective-permute-done((bf16[128,2048]{1,0:T(8,128)(2,1)S(1)}, bf16[128,2048]{1,0:T(8,128)(2,1)S(1)}, u32[]{:S(2)}, u32[]{:S(2)}) %collective-permute-start.98) | collective-permute-done | bytes 524320 | tf_op jit(solution)/shard_map/ppermute | solution.py:335
  527.6 14.5 %attention_backward.1 = (bf16[512,1280]{1,0:T(8,128)(2,1)S(1)}, f32[1,128]{1,0:T(1,128)S(1)}, f32[1,128]{1,0:T(1,128)S(1)}) custom-call(s32[1]{0:T(128)} %bitcast.16.core, f32[512,1280]{1,0:T(8,128)S(1)} %copy-done.9, bf16[512,1024]{1,0:T(8,128)(2,1)S(1)} %attended_grad.1.grad_attended, f32[256,128]{1,0:T(8,128)S(1)} %pad_maximum_fusion.cosine.refs_0_, ...), custom_call_target="tpu_custom_call" | custom-call | flops 1342177280 | bytes 5244932 | tf_op jit(solution)/shard_map/attention_backward/pallas_call | solution.py:932
  559.8 7.7 %normed_grad.1 = (bf16[256,2048]{1,0:T(8,128)(2,1)S(1)}, f32[256,2048]{1,0:T(8,128)S(1)}, f32[1,2048]{1,0:T(1,128)S(1)}) custom-call(s32[16]{0:T(128)S(1)} %copy-done.31, bf16[512,1280]{1,0:T(8,128)(2,1)S(1)} %get-tuple-element.530.right.grad_raw, f32[1,2048]{1,0:T(1,128)S(1)} %bitcast.88, bf16[128,2048]{1,0:T(8,128)(2,1)S(1)} %copy-done.23, ...), custom_call_target="tpu_custom_call" | custom-call | flops 2684354560 | bytes 12337216 | tf_op jit(solution)/shard_map/normed_grad/pallas_call | solution.py:932
  567.6 8.8 %collective-permute-done.115 = bf16[128,1024]{1,0:T(8,128)(2,1)S(1)} collective-permute-done((bf16[128,1024]{1,0:T(8,128)(2,1)S(1)}, bf16[128,1024]{1,0:T(8,128)(2,1)S(1)}, u32[]{:S(2)}, u32[]{:S(2)}) %collective-permute-start.115) | collective-permute-done | bytes 262176 | tf_op jit(solution)/shard_map/ppermute | solution.py:343
  596.8 8.6 %collective-permute-done.124.refs_1_ = bf16[128,1408]{1,0:T(8,128)(2,1)S(1)} collective-permute-done((bf16[128,1408]{1,0:T(8,128)(2,1)S(1)}, bf16[128,1408]{1,0:T(8,128)(2,1)S(1)}, u32[]{:S(2)}, u32[]{:S(2)}) %collective-permute-start.124) | collective-permute-done | bytes 360480 | tf_op jit(solution)/shard_map/ppermute | solution.py:347
  616.8 9.5 %collective-permute-done.128 = f32[34,128]{1,0:T(8,128)S(1)} collective-permute-done((f32[34,128]{1,0:T(8,128)S(1)}, f32[34,128]{1,0:T(8,128)S(1)}, u32[]{:S(2)}, u32[]{:S(2)}) %collective-permute-start.128) | collective-permute-done | bytes 17440 | tf_op jit(solution)/shard_map/ppermute | solution.py:347
  646.4 9.2 %collective-permute-done.139 = bf16[128,1024]{1,0:T(8,128)(2,1)S(1)} collective-permute-done((bf16[128,1024]{1,0:T(8,128)(2,1)S(1)}, bf16[128,1024]{1,0:T(8,128)(2,1)S(1)}, u32[]{:S(2)}, u32[]{:S(2)}) %collective-permute-start.139) | collective-permute-done | bytes 262176 | tf_op jit(solution)/shard_map/ppermute | solution.py:339
  (615 shorter events, 354.5 us)
Async XLA Ops:
  11.5 25.9 %collective-permute-start.4 = (bf16[128,1408]{1,0:T(8,128)(2,1)S(1)}, bf16[128,1408]{1,0:T(8,128)(2,1)S(1)}, u32[]{:S(2)}, u32[]{:S(2)}) collective-permute-start(bf16[128,1408]{1,0:T(8,128)(2,1)S(1)} %concatenate.46.refs_4_), channel_id=1, source_target_pairs={{0,16},{2,18},{4,20},{6,22},{8,24},{10,26},{12,28},{14,30},{16,0},... | collective-permute-start | bytes 1081352 | tf_op jit(solution)/shard_map/ppermute | solution.py:343
  27.3 17.6 %collective-permute-start.3 = (bf16[128,1408]{1,0:T(8,128)(2,1)S(1)}, bf16[128,1408]{1,0:T(8,128)(2,1)S(1)}, u32[]{:S(2)}, u32[]{:S(2)}) collective-permute-start(bf16[128,1408]{1,0:T(8,128)(2,1)S(1)} %collective-permute-done.refs_8_), channel_id=1, source_target_pairs={{0,16},{2,18},{4,20},{6,22},{8,24},{10,26},{12,28},{14,30},{16,0},... | collective-permute-start | bytes 1081352 | tf_op jit(solution)/shard_map/ppermute | solution.py:343
  57.2 18.6 %collective-permute-start.11 = (bf16[128,2048]{1,0:T(8,128)(2,1)S(1)}, bf16[128,2048]{1,0:T(8,128)(2,1)S(1)}, u32[]{:S(2)}, u32[]{:S(2)}) collective-permute-start(bf16[128,2048]{1,0:T(8,128)(2,1)S(1)} %fusion.4.refs_0_), channel_id=1, source_target_pairs={{0,1},{1,0},{2,3},{3,2},{4,5},{5,4},{6,7},{7,6},{8,9},{9,8},{10,11... | collective-permute-start | bytes 1572872 | tf_op jit(solution)/shard_map/ppermute | solution.py:355
  57.3 18.6 %collective-permute-start.12 = (bf16[128,2048]{1,0:T(8,128)(2,1)S(1)}, bf16[128,2048]{1,0:T(8,128)(2,1)S(1)}, u32[]{:S(2)}, u32[]{:S(2)}) collective-permute-start(bf16[128,2048]{1,0:T(8,128)(2,1)S(1)} %fusion.4.refs_0_), channel_id=1, source_target_pairs={{0,8},{2,10},{4,12},{6,14},{8,0},{10,2},{12,4},{14,6},{16,24},{18,... | collective-permute-start | bytes 1572872 | tf_op jit(solution)/shard_map/ppermute | solution.py:339
  92.6 19.1 %collective-permute-start.21 = (bf16[1024,128]{1,0:T(8,128)(2,1)S(1)}, bf16[1024,128]{1,0:T(8,128)(2,1)}, u32[]{:S(2)}, u32[]{:S(2)}) collective-permute-start(bf16[1024,128]{1,0:T(8,128)(2,1)S(1)} %collective-permute-done.18.refs_1_.refs_5_), channel_id=1, source_target_pairs={{0,4},{2,6},{4,0},{6,2},{8,12},{10,14},{12,8},{14,10},{16,20},{18,... | collective-permute-start | bytes 786440 | tf_op jit(solution)/shard_map/ppermute | solution.py:347
  166.3 25.4 %collective-permute-start.34 = (bf16[128,2048]{1,0:T(8,128)(2,1)S(1)}, bf16[128,2048]{1,0:T(8,128)(2,1)S(1)}, u32[]{:S(2)}, u32[]{:S(2)}) collective-permute-start(bf16[128,2048]{1,0:T(8,128)(2,1)S(1)} %slice.152), channel_id=1, source_target_pairs={{0,8},{2,10},{4,12},{6,14},{8,0},{10,2},{12,4},{14,6},{16,24},{18,... | collective-permute-start | bytes 1572872 | tf_op jit(solution)/shard_map/ppermute | solution.py:339
  183.7 18.2 %collective-permute-start.43 = (bf16[128,2048]{1,0:T(8,128)(2,1)S(1)}, bf16[128,2048]{1,0:T(8,128)(2,1)}, u32[]{:S(2)}, u32[]{:S(2)}) collective-permute-start(bf16[128,2048]{1,0:T(8,128)(2,1)S(1)} %collective-permute-done.38.refs_4_), channel_id=1, source_target_pairs={{0,8},{2,10},{4,12},{6,14},{8,16},{10,18},{12,20},{14,22},{16,24},... | collective-permute-start | bytes 1572872 | tf_op jit(solution)/shard_map/ppermute | solution.py:335
  235.2 20.1 %collective-permute-start.51 = (bf16[128,2048]{1,0:T(8,128)(2,1)}, bf16[128,2048]{1,0:T(8,128)(2,1)S(1)}, u32[]{:S(2)}, u32[]{:S(2)}) collective-permute-start(bf16[128,2048]{1,0:T(8,128)(2,1)} %collective-permute-done.48.refs_0_), channel_id=1, source_target_pairs={{0,8},{2,10},{4,12},{6,14},{8,16},{10,18},{12,20},{14,22},{16,24},... | collective-permute-start | bytes 1572872 | tf_op jit(solution)/shard_map/ppermute | solution.py:335
  235.3 20.1 %collective-permute-start.52 = (bf16[128,2048]{1,0:T(8,128)(2,1)}, bf16[128,2048]{1,0:T(8,128)(2,1)S(1)}, u32[]{:S(2)}, u32[]{:S(2)}) collective-permute-start(bf16[128,2048]{1,0:T(8,128)(2,1)} %collective-permute-done.48.refs_0_), channel_id=1, source_target_pairs={{0,2},{2,0},{4,6},{6,4},{8,10},{10,8},{12,14},{14,12},{16,18},{18,... | collective-permute-start | bytes 1572872 | tf_op jit(solution)/shard_map/ppermute | solution.py:351
  235.8 19.6 %collective-permute-start.53 = (bf16[128,2048]{1,0:T(8,128)(2,1)}, bf16[128,2048]{1,0:T(8,128)(2,1)S(1)}, u32[]{:S(2)}, u32[]{:S(2)}) collective-permute-start(bf16[128,2048]{1,0:T(8,128)(2,1)} %collective-permute-done.46.refs_0_), channel_id=1, source_target_pairs={{0,4},{2,6},{4,0},{6,2},{8,12},{10,14},{12,8},{14,10},{16,20},{18,... | collective-permute-start | bytes 1572872 | tf_op jit(solution)/shard_map/ppermute | solution.py:347
  272.3 18.3 %collective-permute-start.59 = (bf16[128,2048]{1,0:T(8,128)(2,1)}, bf16[128,2048]{1,0:T(8,128)(2,1)S(1)}, u32[]{:S(2)}, u32[]{:S(2)}) collective-permute-start(bf16[128,2048]{1,0:T(8,128)(2,1)} %collective-permute-done.43.refs_4_), channel_id=1, source_target_pairs={{0,2},{2,0},{4,6},{6,4},{8,10},{10,8},{12,14},{14,12},{16,18},{18,... | collective-permute-start | bytes 1572872 | tf_op jit(solution)/shard_map/ppermute | solution.py:351
  272.8 17.8 %collective-permute-start.60 = (bf16[128,2048]{1,0:T(8,128)(2,1)S(1)}, bf16[128,2048]{1,0:T(8,128)(2,1)S(1)}, u32[]{:S(2)}, u32[]{:S(2)}) collective-permute-start(bf16[128,2048]{1,0:T(8,128)(2,1)S(1)} %copy-done.13), channel_id=1, source_target_pairs={{0,4},{2,6},{4,0},{6,2},{8,12},{10,14},{12,8},{14,10},{16,20},{18,... | collective-permute-start | bytes 1572872 | tf_op jit(solution)/shard_map/ppermute | solution.py:347
  324.6 22.3 %collective-permute-start.69 = (bf16[176,4224]{1,0:T(8,128)(2,1)}, bf16[176,4224]{1,0:T(8,128)(2,1)}, u32[]{:S(2)}, u32[]{:S(2)}) collective-permute-start(bf16[176,4224]{1,0:T(8,128)(2,1)} %get-tuple-element.406), channel_id=1, source_target_pairs={{0,1},{1,0},{2,3},{3,2},{4,5},{5,4},{6,7},{7,6},{8,9},{9,8},{10,11... | collective-permute-start | bytes 4460552 | tf_op jit(solution)/shard_map/ppermute | solution.py:355
  359.2 29.2 %collective-permute-start.72 = (bf16[128,2176]{1,0:T(8,128)(2,1)}, bf16[128,2176]{1,0:T(8,128)(2,1)S(1)}, u32[]{:S(2)}, u32[]{:S(2)}) collective-permute-start(bf16[128,2176]{1,0:T(8,128)(2,1)} %get-tuple-element.423), channel_id=1, source_target_pairs={{0,2},{2,0},{4,6},{6,4},{8,10},{10,8},{12,14},{14,12},{16,18},{18,... | collective-permute-start | bytes 1671176 | tf_op jit(solution)/shard_map/ppermute | solution.py:351
  359.5 29.0 %collective-permute-start.73 = (bf16[128,2176]{1,0:T(8,128)(2,1)}, bf16[128,2176]{1,0:T(8,128)(2,1)S(1)}, u32[]{:S(2)}, u32[]{:S(2)}) collective-permute-start(bf16[128,2176]{1,0:T(8,128)(2,1)} %get-tuple-element.424), channel_id=1, source_target_pairs={{0,4},{2,6},{4,0},{6,2},{8,12},{10,14},{12,8},{14,10},{16,20},{18,... | collective-permute-start | bytes 1671176 | tf_op jit(solution)/shard_map/ppermute | solution.py:347
  361.1 27.4 %collective-permute-start.74 = (bf16[128,2176]{1,0:T(8,128)(2,1)}, bf16[128,2176]{1,0:T(8,128)(2,1)S(1)}, u32[]{:S(2)}, u32[]{:S(2)}) collective-permute-start(bf16[128,2176]{1,0:T(8,128)(2,1)} %get-tuple-element.425), channel_id=1, source_target_pairs={{0,8},{2,10},{4,12},{6,14},{8,16},{10,18},{12,20},{14,22},{16,24},... | collective-permute-start | bytes 1671176 | tf_op jit(solution)/shard_map/ppermute | solution.py:335
  361.1 24.2 %collective-permute-start.75 = (bf16[128,2048]{1,0:T(8,128)(2,1)}, bf16[128,2048]{1,0:T(8,128)(2,1)S(1)}, u32[]{:S(2)}, u32[]{:S(2)}) collective-permute-start(bf16[128,2048]{1,0:T(8,128)(2,1)} %get-tuple-element.426), channel_id=1, source_target_pairs={{0,2},{2,0},{4,6},{6,4},{8,10},{10,8},{12,14},{14,12},{16,18},{18,... | collective-permute-start | bytes 1572872 | tf_op jit(solution)/shard_map/ppermute | solution.py:351
  362.7 25.8 %collective-permute-start.76 = (bf16[128,2048]{1,0:T(8,128)(2,1)}, bf16[128,2048]{1,0:T(8,128)(2,1)S(1)}, u32[]{:S(2)}, u32[]{:S(2)}) collective-permute-start(bf16[128,2048]{1,0:T(8,128)(2,1)} %get-tuple-element.427), channel_id=1, source_target_pairs={{0,8},{2,10},{4,12},{6,14},{8,16},{10,18},{12,20},{14,22},{16,24},... | collective-permute-start | bytes 1572872 | tf_op jit(solution)/shard_map/ppermute | solution.py:335
  524.1 18.1 %collective-permute-start.105 = (bf16[128,1024]{1,0:T(8,128)(2,1)S(1)}, bf16[128,1024]{1,0:T(8,128)(2,1)S(1)}, u32[]{:S(2)}, u32[]{:S(2)}) collective-permute-start(bf16[128,1024]{1,0:T(8,128)(2,1)S(1)} %sums.22), channel_id=1, source_target_pairs={{0,4},{2,6},{4,0},{6,2},{8,12},{10,14},{12,8},{14,10},{16,20},{18,... | collective-permute-start | bytes 786440 | tf_op jit(solution)/shard_map/ppermute | solution.py:347
  554.6 21.8 %collective-permute-start.112 = (bf16[128,2048]{1,0:T(8,128)(2,1)S(1)}, bf16[128,2048]{1,0:T(8,128)(2,1)S(1)}, u32[]{:S(2)}, u32[]{:S(2)}) collective-permute-start(bf16[128,2048]{1,0:T(8,128)(2,1)S(1)} %get-tuple-element.526), channel_id=1, source_target_pairs={{0,2},{2,0},{4,6},{6,4},{8,10},{10,8},{12,14},{14,12},{16,18},{18,... | collective-permute-start | bytes 1572872 | tf_op jit(solution)/shard_map/ppermute | solution.py:351
  555.1 21.3 %collective-permute-start.113 = (bf16[128,2048]{1,0:T(8,128)(2,1)S(1)}, bf16[128,2048]{1,0:T(8,128)(2,1)S(1)}, u32[]{:S(2)}, u32[]{:S(2)}) collective-permute-start(bf16[128,2048]{1,0:T(8,128)(2,1)S(1)} %copy-done.54), channel_id=1, source_target_pairs={{0,4},{2,6},{4,0},{6,2},{8,12},{10,14},{12,8},{14,10},{16,20},{18,... | collective-permute-start | bytes 1572872 | tf_op jit(solution)/shard_map/ppermute | solution.py:347
  555.7 20.7 %collective-permute-start.114 = (bf16[128,2048]{1,0:T(8,128)(2,1)S(1)}, bf16[128,2048]{1,0:T(8,128)(2,1)S(1)}, u32[]{:S(2)}, u32[]{:S(2)}) collective-permute-start(bf16[128,2048]{1,0:T(8,128)(2,1)S(1)} %get-tuple-element.528), channel_id=1, source_target_pairs={{0,8},{2,10},{4,12},{6,14},{8,16},{10,18},{12,20},{14,22},{16,24},... | collective-permute-start | bytes 1572872 | tf_op jit(solution)/shard_map/ppermute | solution.py:335
  557.7 18.7 %collective-permute-start.115 = (bf16[128,1024]{1,0:T(8,128)(2,1)S(1)}, bf16[128,1024]{1,0:T(8,128)(2,1)S(1)}, u32[]{:S(2)}, u32[]{:S(2)}) collective-permute-start(bf16[128,1024]{1,0:T(8,128)(2,1)S(1)} %get-tuple-element.514), channel_id=1, source_target_pairs={{0,16},{2,18},{4,20},{6,22},{8,24},{10,26},{12,28},{14,30},{16,0},... | collective-permute-start | bytes 786440 | tf_op jit(solution)/shard_map/ppermute | solution.py:343
  557.7 18.7 %collective-permute-start.116 = (bf16[128,1408]{1,0:T(8,128)(2,1)S(1)}, bf16[128,1408]{1,0:T(8,128)(2,1)S(1)}, u32[]{:S(2)}, u32[]{:S(2)}) collective-permute-start(bf16[128,1408]{1,0:T(8,128)(2,1)S(1)} %get-tuple-element.529), channel_id=1, source_target_pairs={{0,2},{2,0},{4,6},{6,4},{8,10},{10,8},{12,14},{14,12},{16,18},{18,... | collective-permute-start | bytes 1081352 | tf_op jit(solution)/shard_map/ppermute | solution.py:351
  591.1 19.7 %collective-permute-start.122 = (bf16[128,2048]{1,0:T(8,128)(2,1)S(1)}, bf16[128,2048]{1,0:T(8,128)(2,1)S(1)}, u32[]{:S(2)}, u32[]{:S(2)}) collective-permute-start(bf16[128,2048]{1,0:T(8,128)(2,1)S(1)} %slice.151), channel_id=1, source_target_pairs={{0,8},{2,10},{4,12},{6,14},{8,0},{10,2},{12,4},{14,6},{16,24},{18,... | collective-permute-start | bytes 1572872 | tf_op jit(solution)/shard_map/ppermute | solution.py:339
  592.7 18.2 %collective-permute-start.127 = (bf16[128,1024]{1,0:T(8,128)(2,1)S(1)}, bf16[128,1024]{1,0:T(8,128)(2,1)S(1)}, u32[]{:S(2)}, u32[]{:S(2)}) collective-permute-start(bf16[128,1024]{1,0:T(8,128)(2,1)S(1)} %get-tuple-element.564), channel_id=1, source_target_pairs={{0,16},{2,18},{4,20},{6,22},{8,24},{10,26},{12,28},{14,30},{16,0},... | collective-permute-start | bytes 786440 | tf_op jit(solution)/shard_map/ppermute | solution.py:343
  610.9 23.5 %collective-permute-start.132 = (bf16[128,1024]{1,0:T(8,128)(2,1)S(1)}, bf16[128,1024]{1,0:T(8,128)(2,1)S(1)}, u32[]{:S(2)}, u32[]{:S(2)}) collective-permute-start(bf16[128,1024]{1,0:T(8,128)(2,1)S(1)} %get-tuple-element.569), channel_id=1, source_target_pairs={{0,2},{2,0},{4,6},{6,4},{8,10},{10,8},{12,14},{14,12},{16,18},{18,... | collective-permute-start | bytes 786440 | tf_op jit(solution)/shard_map/ppermute | solution.py:351
  611.5 23.0 %collective-permute-start.133 = (bf16[128,1024]{1,0:T(8,128)(2,1)S(1)}, bf16[128,1024]{1,0:T(8,128)(2,1)S(1)}, u32[]{:S(2)}, u32[]{:S(2)}) collective-permute-start(bf16[128,1024]{1,0:T(8,128)(2,1)S(1)} %get-tuple-element.570), channel_id=1, source_target_pairs={{0,4},{2,6},{4,0},{6,2},{8,12},{10,14},{12,8},{14,10},{16,20},{18,... | collective-permute-start | bytes 786440 | tf_op jit(solution)/shard_map/ppermute | solution.py:347
  634.4 21.3 %collective-permute-start.135 = (bf16[128,1408]{1,0:T(8,128)(2,1)S(1)}, bf16[128,1408]{1,0:T(8,128)(2,1)S(1)}, u32[]{:S(2)}, u32[]{:S(2)}) collective-permute-start(bf16[128,1408]{1,0:T(8,128)(2,1)S(1)} %get-tuple-element.581), channel_id=1, source_target_pairs={{0,4},{2,6},{4,0},{6,2},{8,12},{10,14},{12,8},{14,10},{16,20},{18,... | collective-permute-start | bytes 1081352 | tf_op jit(solution)/shard_map/ppermute | solution.py:347
  635.9 20.0 %collective-permute-start.136 = (bf16[128,1408]{1,0:T(8,128)(2,1)S(1)}, bf16[128,1408]{1,0:T(8,128)(2,1)S(1)}, u32[]{:S(2)}, u32[]{:S(2)}) collective-permute-start(bf16[128,1408]{1,0:T(8,128)(2,1)S(1)} %get-tuple-element.565), channel_id=1, source_target_pairs={{0,16},{2,18},{4,20},{6,22},{8,24},{10,26},{12,28},{14,30},{16,0},... | collective-permute-start | bytes 1081352 | tf_op jit(solution)/shard_map/ppermute | solution.py:343
  636.4 19.5 %collective-permute-start.137 = (bf16[128,1408]{1,0:T(8,128)(2,1)S(1)}, bf16[128,1408]{1,0:T(8,128)(2,1)S(1)}, u32[]{:S(2)}, u32[]{:S(2)}) collective-permute-start(bf16[128,1408]{1,0:T(8,128)(2,1)S(1)} %get-tuple-element.584), channel_id=1, source_target_pairs={{0,4},{2,6},{4,0},{6,2},{8,12},{10,14},{12,8},{14,10},{16,20},{18,... | collective-permute-start | bytes 1081352 | tf_op jit(solution)/shard_map/ppermute | solution.py:347
  637.0 18.9 %collective-permute-start.138 = (bf16[128,1408]{1,0:T(8,128)(2,1)S(1)}, bf16[128,1408]{1,0:T(8,128)(2,1)S(1)}, u32[]{:S(2)}, u32[]{:S(2)}) collective-permute-start(bf16[128,1408]{1,0:T(8,128)(2,1)S(1)} %get-tuple-element.585), channel_id=1, source_target_pairs={{0,2},{2,0},{4,6},{6,4},{8,10},{10,8},{12,14},{14,12},{16,18},{18,... | collective-permute-start | bytes 1081352 | tf_op jit(solution)/shard_map/ppermute | solution.py:351
  (237 other events, 3503.8 us)

commit v2 on v1

--- a/solution.py
+++ b/solution.py
@@ -411,13 +411,13 @@
         ((2, 1, 1), (2, 0, 1), y_swap),
     ),
     (
-        ((3, 0, 0), (1, 0, 0), z_far, True),
+        ((3, 0, 0), (1, 0, 0), z_far),
         ((2, 0, 1), (2, 0, 0), x_swap),
         ((2, 1, 0), (2, 0, 0), y_swap),
         ((1, 1, 1), (1, 1, 0), x_swap),
     ),
     (
-        ((2, 0, 0), (0, 0, 0), z_far, True),
+        ((2, 0, 0), (0, 0, 0), z_far),
         ((1, 1, 0), (1, 0, 0), y_swap),
         ((1, 0, 1), (1, 0, 0), x_swap),
         ((0, 1, 1), (0, 0, 1), y_swap),
@@ -426,21 +426,19 @@
 )
 
 
-def turned(block):
-    k, dy, dx = block
-    return (-k) % 4, dy, dx
-
-
-RETURN_ROUNDS = tuple(
-    tuple((turned(end), turned(start), over) for start, end, over in moves)
-    for moves in reversed(TOKEN_ROUNDS)
+RETURN_ROUNDS = (
+    (((1, 1, 1), (1, 0, 1), y_swap), ((0, 1, 1), (0, 1, 0), x_swap), ((1, 1, 0), (2, 1, 0), z_next)),
+    (((1, 0, 1), (1, 0, 0), x_swap), ((2, 1, 1), (2, 0, 1), y_swap), ((2, 1, 0), (2, 0, 0), y_swap)),
+    (((2, 0, 1), (2, 0, 0), x_swap), ((3, 1, 1), (3, 0, 1), y_swap), ((1, 0, 0), (2, 0, 0), z_next)),
+    (((3, 0, 1), (3, 0, 0), x_swap), ((3, 1, 0), (3, 0, 0), y_swap), ((2, 0, 0), (3, 0, 0), z_next)),
+    (((0, 0, 1), (0, 0, 0), x_swap), ((0, 1, 0), (0, 0, 0), y_swap), ((3, 0, 0), (0, 0, 0), z_next)),
 )
 OUTPUT_ROUNDS = (
-    (((2, 1, 1), (2, 1, 0), x_swap), ((1, 1, 0), (2, 1, 0), z_next)),
-    (((1, 1, 1), (1, 0, 1), y_swap), ((2, 0, 1), (2, 0, 0), x_swap), ((3, 1, 1), (0, 1, 1), z_next)),
-    (((1, 0, 1), (1, 0, 0), x_swap), ((2, 1, 0), (2, 0, 0), y_swap)),
-    (((3, 1, 0), (3, 0, 0), y_swap), ((3, 0, 1), (3, 0, 0), x_swap), ((1, 0, 0), (2, 0, 0), z_next)),
-    (((0, 1, 1), (0, 0, 1), y_swap), ((2, 0, 0), (3, 0, 0), z_next)),
+    (((3, 1, 1), (3, 1, 0), x_swap), ((1, 1, 1), (1, 0, 1), y_swap), ((1, 1, 0), (2, 1, 0), z_next)),
+    (((1, 0, 1), (1, 0, 0), x_swap), ((2, 1, 1), (2, 0, 1), y_swap)),
+    (((2, 0, 1), (2, 0, 0), x_swap), ((2, 1, 0), (2, 0, 0), y_swap), ((1, 0, 0), (2, 0, 0), z_next)),
+    (((3, 0, 1), (3, 0, 0), x_swap), ((3, 1, 0), (3, 0, 0), y_swap), ((2, 0, 0), (3, 0, 0), z_next)),
+    (((0, 1, 1), (0, 1, 0), x_swap),),
     (((0, 0, 1), (0, 0, 0), x_swap), ((0, 1, 0), (0, 0, 0), y_swap), ((3, 0, 0), (0, 0, 0), z_next)),
 )
 
@@ -477,7 +475,11 @@
             held[end] = result
         return rest
 
-    def scatter(self, pairs, others=()):
+    def scatter(self, pairs, others=(), later=None):
+        if later is not None:
+            for terms, moves in pairs:
+                for move in moves:
+                    terms[move[0]][-1] = after(terms[move[0]][-1], later)
         values = totals([terms[move[0]] for terms, moves in pairs for move in moves])
         moves = [move for _, moves in pairs for move in moves]
         results, rest = self.round(values, moves, others)
@@ -1183,7 +1185,7 @@
         stores[:] = made[:5]
         return made[5:]
 
-    terms, y_terms = {}, {}
+    terms, y_terms = {b: [] for b in BLOCKS}, {}
 
     def sum_tokens(k, own, back):
         made = call(
@@ -1201,7 +1203,7 @@
             [VMEM] * 4 + [HBM] * 4,
         )
         for i, p in enumerate(PLANE):
-            terms[(k, *p)] = [made[i]]
+            terms[(k, *p)].append(made[i])
             y_terms[(k, *p)] = [made[4 + i]]
         return made[0]
 
@@ -1223,25 +1225,24 @@
     chain.gather([(cot_held, TOKEN_ROUNDS[4])])
     own_two, other_two = pick_tokens(2, sent)
     back, back_two = chain.send([sent, other_two], [core_swap] * 2)
-    first_own, first_back = own, back
-    own, sent = run_experts(2, own_two, back_two)
+    sum_tokens(1, own, back)
+    chain.scatter([(terms, RETURN_ROUNDS[0])])
+    own, sent = run_experts(2, own_two, after(back_two, *chain.values))
     own_three, other_three = pick_tokens(3, sent)
     back, back_three = chain.send([sent, other_three], [core_swap] * 2)
-    sum_tokens(1, after(first_own, sent), first_back)
     sum_tokens(2, own, back)
-    chain.scatter([(terms, RETURN_ROUNDS[0]), (y_terms, OUTPUT_ROUNDS[0])])
+    chain.scatter([(terms, RETURN_ROUNDS[1])])
     own, sent = run_experts(3, own_three, back_three)
     all_rows, all_act, all_grads, all_gate, all_up = stores
     (back,) = chain.send([sent], [core_swap])
     sum_tokens(3, own, back)
     weight_grads = []
     for moves, pair in zip(
-        RETURN_ROUNDS[1:], ((all_act, all_grads), (all_rows, all_gate), (all_rows, all_up), None)
+        RETURN_ROUNDS[2:], ((all_act, all_grads), (all_rows, all_gate), (all_rows, all_up))
     ):
         chain.scatter([(terms, moves)])
-        if pair:
-            weight_grads.append(row_product(*pair, *chain.values))
-            chain.add(weight_grads[-1])
+        weight_grads.append(row_product(*pair, *chain.values))
+        chain.add(weight_grads[-1])
     grad_down, grad_gate, grad_up = weight_grads
 
     summed = plus(*terms[0, 0, 0])
@@ -1258,16 +1259,16 @@
     grad_hidden_norm, grad_feed_gain = experts_back(grad_moe_in)
     grad_hidden = grad_output + grad_hidden_norm
     grad_own = grad_hidden.astype(low)
-    chain.scatter([(y_terms, OUTPUT_ROUNDS[1])])
+    chain.scatter([(y_terms, OUTPUT_ROUNDS[0])])
     chain.add(grad_own)
     far, swapped = chain.scatter(
-        [(y_terms, OUTPUT_ROUNDS[2])], [(grad_own, z_pair), (grad_own, core_swap)]
+        [(y_terms, OUTPUT_ROUNDS[1])], [(grad_own, z_pair), (grad_own, core_swap)]
     )
 
     grad_router = jnp.einsum(
         "td,te->ed", moe_in.astype(wide), after(grad_logits, grad_own), precision=HIGH
     )
-    (far_swapped,) = chain.scatter([(y_terms, OUTPUT_ROUNDS[3])], [(far, core_swap)])
+    (far_swapped,) = chain.scatter([(y_terms, OUTPUT_ROUNDS[2])], [(far, core_swap)])
     grad_branch = [grad_own, swapped, far, far_swapped]
 
     def block_products(left_blocks, right, rest, name):
@@ -1287,7 +1288,9 @@
     out_terms = {b: [block] for b, block in zip(BLOCKS, out_products)}
     chain.add(out_products[0])
     (router_part,) = chain.scatter(
-        [(y_terms, OUTPUT_ROUNDS[4]), (out_terms, WEIGHT_RETURNS[0])], [(grad_router, core_swap)]
+        [(y_terms, OUTPUT_ROUNDS[3]), (out_terms, WEIGHT_RETURNS[0])],
+        [(grad_router, core_swap)],
+        out_products[0],
     )
     grad_router = grad_router + router_part
     (grad_attended,) = call(
@@ -1305,7 +1308,9 @@
         2 * both * model_width * query_cols,
     )
     chain.add(grad_attended)
-    (router_part,) = chain.scatter([(out_terms, WEIGHT_RETURNS[1])], [(grad_router, z_pair)])
+    (router_part,) = chain.scatter(
+        [(out_terms, WEIGHT_RETURNS[1]), (y_terms, OUTPUT_ROUNDS[4])], [(grad_router, z_pair)]
+    )
     grad_rest = jnp.pad(grad_router + router_part, ((0, 128 - expert_count), (0, 0)))
     grad_raw, query_gain_grad, key_gain_grad = call(
         functools.partial(backward_kernel, head_count),
@@ -1349,31 +1354,28 @@
     gains = jnp.concatenate(
         [attention_part[0], grad_feed_gain, query_gain_grad[0], key_gain_grad[0]]
     ).reshape(-1, head_width)
-    from_core, gain_part = chain.scatter(
-        [(out_terms, WEIGHT_RETURNS[3])], [(sent, core_swap), (gains, core_swap)]
-    )
+    gains = gains + core_swap(gains)
+    (from_core,) = chain.scatter([(out_terms, WEIGHT_RETURNS[3])], [(sent, core_swap)])
     pair_total = kept + from_core.astype(wide)
-    gains = gains + gain_part
     from_pair, gain_part = chain.scatter(
         [(raw_terms, WEIGHT_RETURNS[1])],
         [(pair_total[tok_rows:].astype(low), z_pair), (gains, x_swap)],
     )
     gains = gains + gain_part
-    chain.scatter([(raw_terms, WEIGHT_RETURNS[2]), (out_terms, WEIGHT_RETURNS[4])])
+    (gain_part,) = chain.scatter([(raw_terms, WEIGHT_RETURNS[2])], [(gains, y_swap)])
     grad_normed = pair_total[:tok_rows] + from_pair.astype(wide)
     grad_inputs_norm, _ = attention_back(grad_normed)
     grad_inputs = grad_hidden + grad_inputs_norm
-    gains = gains + y_swap(after(gains, *chain.values))
-    chain.add(grad_inputs, gains)
-    out_theirs = plus(*out_terms[1, 0, 0]).astype(low)
-    out_theirs, gain_part = chain.scatter(
-        [(raw_terms, WEIGHT_RETURNS[3])], [(out_theirs, z_pair), (gains, z_pair)]
-    )
+    chain.add(grad_inputs)
     gains = gains + gain_part
-    raw_theirs = plus(*raw_terms[1, 0, 0]).astype(low)
-    raw_theirs, gain_part = chain.scatter(
-        [(raw_terms, WEIGHT_RETURNS[4])], [(raw_theirs, z_pair), (gains, z_far)]
-    )
+    (gain_part,) = chain.scatter([(raw_terms, WEIGHT_RETURNS[3])], [(gains, z_pair)])
+    gains = gains + gain_part
+    theirs = jnp.concatenate([plus(*t[1, 0, 0]).astype(low) for t in (out_terms, raw_terms)], axis=1)
+    theirs, gain_part = chain.scatter(
+        [(raw_terms, WEIGHT_RETURNS[4]), (out_terms, WEIGHT_RETURNS[4])],
+        [(theirs, z_pair), (gains, z_far)],
+    )
+    out_theirs, raw_theirs = theirs[:, :query_cols], theirs[:, query_cols:]
     gains = (gains + gain_part).reshape(-1)
     output = (hidden + plus(*y_terms[0, 0, 0])).astype(low)
     grad_out_weight = in_order(plus(*out_terms[0, 0, 0]), out_theirs.astype(wide), 1).T

time: 682 us -> 674 us (0.988)
    ppermute x45 -> x46, waiting for transfers between devices: 76.8 us -> 94.9 us  [y_swap(): return lax.ppermute(block, 'dp', Y_PAIR)]
    ppermute x10 -> x9, waiting for transfers between devices: 35.2 us -> 21.1 us  [z_pair(): return lax.ppermute(block, 'dp', Z_PAIR)]
    ppermute x10, waiting for transfers between devices: 26.2 us -> 18.3 us  [z_far(): return lax.ppermute(block, 'dp', Z_FAR)]
    ppermute x20 -> x18, waiting for transfers between devices: 91 us -> 83.4 us  [z_next(): return lax.ppermute(block, 'dp', Z_RING)]
    ppermute x44 -> x45, waiting for transfers between devices: 90 us -> 94 us  [x_swap(): return lax.ppermute(block, 'dp', X_PAIR)]
    ppermute x45 -> x46, starting transfers between devices: 48 us -> 51.1 us  [y_swap(): return lax.ppermute(block, 'dp', Y_PAIR)]
    ppermute x44 -> x45, starting transfers between devices: 51.1 us -> 49.4 us  [x_swap(): return lax.ppermute(block, 'dp', X_PAIR)]
    unnamed x251 -> x253, local copies, waits for them, and re-layouts: 19.7 us -> 19.6 us
  transfers between devices with their start and end apart: 145 -> 144, of which waited for: 69 -> 77; matrix products, arithmetic and copies ran while one was open for 6% -> 6% of each run, Pallas kernels for 20% -> 20%
where the time goes in v2:
time: 674 us; the launch traced here: 666 us
  waiting for transfers between devices  325 us (48%)
  Pallas kernels  142 us (21%)
  starting transfers between devices  131 us (19%)
  matrix products  25.9 us (4%)
  local copies, waits for them, and re-layouts  24 us (4%)
  other arithmetic  15 us (2%)
    pallas_call x21, Pallas kernels, call(): pl.pallas_call(kernel, out_shape=outs, in_specs=[spec for _, spec in ins]...  138 us
    ppermute x46, waiting for transfers between devices, y_swap(): return lax.ppermute(block, 'dp', Y_PAIR)  94.9 us
    ppermute x45, waiting for transfers between devices, x_swap(): return lax.ppermute(block, 'dp', X_PAIR)  94 us
    ppermute x18, waiting for transfers between devices, z_next(): return lax.ppermute(block, 'dp', Z_RING)  83.4 us
    ppermute x46, starting transfers between devices, y_swap(): return lax.ppermute(block, 'dp', Y_PAIR)  51.1 us
    ppermute x45, starting transfers between devices, x_swap(): return lax.ppermute(block, 'dp', X_PAIR)  49.4 us
    dot_general x3, matrix products, row_product(): lax.dot_general(after(left, *earlier), right, TN, preferred_element_type=...  24.2 us
    ppermute x9, waiting for transfers between devices, z_pair(): return lax.ppermute(block, 'dp', Z_PAIR)  21.1 us
  transfers between devices with their start and end apart: 144, of which 77 were waited for; matrix products, arithmetic and copies ran while one was open for 6% of the time, Pallas kernels for 20%

profile of v2, /device:TPU:0, one launch (start us, length us, event | category | flops | bytes accessed | tf_op | source)
XLA Modules:
  0.0 665.8 jit_solution(11176060383310965345)
XLA Ops:
  15.1 8.0 %collective-permute-done.refs_8_ = bf16[128,1408]{1,0:T(8,128)(2,1)S(1)} collective-permute-done((bf16[128,1408]{1,0:T(8,128)(2,1)}, bf16[128,1408]{1,0:T(8,128)(2,1)S(1)}, u32[]{:S(2)}, u32[]{:S(2)}) %collective-permute-start) | collective-permute-done | bytes 360480 | tf_op jit(solution)/shard_map/ppermute | solution.py:339
  45.6 7.3 %collective-permute-done.10.refs_11_ = bf16[128,1408]{1,0:T(8,128)(2,1)S(1)} collective-permute-done((bf16[128,1408]{1,0:T(8,128)(2,1)S(1)}, bf16[128,1408]{1,0:T(8,128)(2,1)S(1)}, u32[]{:S(2)}, u32[]{:S(2)}) %collective-permute-start.10) | collective-permute-done | bytes 360480 | tf_op jit(solution)/shard_map/ppermute | solution.py:351
  70.4 6.5 collective-permute-done.15.refs_15_
  82.6 11.1 %collective-permute-done.18.refs_1_.refs_5_ = bf16[1024,128]{1,0:T(8,128)(2,1)S(1)} collective-permute-done((bf16[1024,128]{1,0:T(8,128)(2,1)S(1)}, bf16[1024,128]{1,0:T(8,128)(2,1)S(1)}, u32[]{:S(2)}, u32[]{:S(2)}) %collective-permute-start.18) | collective-permute-done | bytes 262176 | tf_op jit(solution)/shard_map/ppermute | solution.py:351
  103.0 9.8 %attention_raw.1 = (f32[512,1280]{1,0:T(8,128)}, bf16[2048,128]{1,0:T(8,128)(2,1)}, bf16[2048,128]{1,0:T(8,128)(2,1)}) custom-call(s32[16]{0:T(128)} %stack.127.ids, s32[16]{0:T(128)} %stack.144.block_ids, bf16[128,2048]{1,0:T(8,128)(2,1)} %copy-done.22, bf16[128,2048]{1,0:T(8,128)(2,1)} %copy-done.42, bf16[128,2048]{1,0:T(8,128)(2,1)} %copy-done.44, ...), custom_call_target="tpu_custom_call" | custom-call | flops 2684354560 | bytes 11534464 | tf_op jit(solution)/shard_map/attention_raw/pallas_call | solution.py:934
  118.6 9.4 %attention_forward.1.attended.right = bf16[512,1024]{1,0:T(8,128)(2,1)S(1)} custom-call(s32[1]{0:T(128)} %bitcast.16.core, f32[512,1280]{1,0:T(8,128)S(1)} %copy-done.8, f32[256,128]{1,0:T(8,128)S(1)} %pad_maximum_fusion.1.cosine.refs_0_, f32[256,128]{1,0:T(8,128)S(1)} %pad_maximum_fusion.2.sine.refs_1_, f32[1,128]{1,0:T(1,128)S(1)} %bitcast.98, ...), custom_call_target="tpu_custom_call" | custom-call | flops 536870912 | bytes 3933188 | tf_op jit(solution)/shard_map/attention_forward/pallas_call | solution.py:934
  152.1 13.0 %collective-permute-done.35.refs_4_ = bf16[128,2048]{1,0:T(8,128)(2,1)S(1)} collective-permute-done((bf16[128,2048]{1,0:T(8,128)(2,1)S(1)}, bf16[128,2048]{1,0:T(8,128)(2,1)S(1)}, u32[]{:S(2)}, u32[]{:S(2)}) %collective-permute-start.35) | collective-permute-done | bytes 524320 | tf_op jit(solution)/shard_map/ppermute | solution.py:335
  168.6 13.2 %collective-permute-done.38.refs_4_ = bf16[128,2048]{1,0:T(8,128)(2,1)S(1)} collective-permute-done((bf16[128,2048]{1,0:T(8,128)(2,1)S(1)}, bf16[128,2048]{1,0:T(8,128)(2,1)S(1)}, u32[]{:S(2)}, u32[]{:S(2)}) %collective-permute-start.38) | collective-permute-done | bytes 524320 | tf_op jit(solution)/shard_map/ppermute | solution.py:335
  185.6 7.2 %collective-permute-done.34 = bf16[128,2048]{1,0:T(8,128)(2,1)S(1)} collective-permute-done((bf16[128,2048]{1,0:T(8,128)(2,1)S(1)}, bf16[128,2048]{1,0:T(8,128)(2,1)S(1)}, u32[]{:S(2)}, u32[]{:S(2)}) %collective-permute-start.34) | collective-permute-done | bytes 524320 | tf_op jit(solution)/shard_map/ppermute | solution.py:339
  196.7 6.3 collective-permute-done.43.refs_4_
  205.2 10.5 %collective-permute-done.44.refs_1_ = bf16[128,2048]{1,0:T(8,128)(2,1)} collective-permute-done((bf16[128,2048]{1,0:T(8,128)(2,1)S(1)}, bf16[128,2048]{1,0:T(8,128)(2,1)}, u32[]{:S(2)}, u32[]{:S(2)}) %collective-permute-start.44) | collective-permute-done | bytes 524320 | tf_op jit(solution)/shard_map/ppermute | solution.py:351
  245.0 11.4 %experts.4 = (bf16[1408,2048]{1,0:T(8,128)(2,1)}, bf16[1408,768]{1,0:T(8,128)(2,1)S(1)}, bf16[1408,2048]{1,0:T(8,128)(2,1)}, bf16[1408,768]{1,0:T(8,128)(2,1)S(1...) custom-call(s32[2]{0:T(128)S(1)} %pad_add_fusion.experts, ...), custom_call_target="tpu_custom_call" | custom-call | flops 6643777536 | bytes 33931272 | tf_op jit(solution)/shard_map/experts/pallas_call | solution.py:934
  258.6 14.3 %collective-permute-done.55.refs_3_ = bf16[128,2048]{1,0:T(8,128)(2,1)S(1)} collective-permute-done((bf16[128,2048]{1,0:T(8,128)(2,1)}, bf16[128,2048]{1,0:T(8,128)(2,1)S(1)}, u32[]{:S(2)}, u32[]{:S(2)}) %collective-permute-start.55) | collective-permute-done | bytes 524320 | tf_op jit(solution)/shard_map/ppermute | solution.py:335
  279.9 8.7 %collective-permute-done.58.refs_7_ = bf16[128,2048]{1,0:T(8,128)(2,1)S(1)} collective-permute-done((bf16[128,2048]{1,0:T(8,128)(2,1)S(1)}, bf16[128,2048]{1,0:T(8,128)(2,1)S(1)}, u32[]{:S(2)}, u32[]{:S(2)}) %collective-permute-start.58) | collective-permute-done | bytes 524320 | tf_op jit(solution)/shard_map/ppermute | solution.py:335
  295.1 11.5 %experts.5 = (bf16[1408,2048]{1,0:T(8,128)(2,1)}, bf16[1408,768]{1,0:T(8,128)(2,1)S(1)}, bf16[1408,2048]{1,0:T(8,128)(2,1)}, bf16[1408,768]{1,0:T(8,128)(2,1)S(1...) custom-call(s32[2]{0:T(128)S(1)} %pad_add_fusion.experts, ...), custom_call_target="tpu_custom_call", output_to_operand_aliasing={{0}: (7, {}), {1}: (8, {}), {2}: (9, {}), {3}: (10, {}), {4... | custom-call | flops 6643777536 | bytes 51953672 | tf_op jit(solution)/shard_map/experts/pallas_call | solution.py:934
  311.6 10.5 %collective-permute-done.65.refs_7_ = bf16[128,2048]{1,0:T(8,128)(2,1)S(1)} collective-permute-done((bf16[128,2048]{1,0:T(8,128)(2,1)S(1)}, bf16[128,2048]{1,0:T(8,128)(2,1)S(1)}, u32[]{:S(2)}, u32[]{:S(2)}) %collective-permute-start.65) | collective-permute-done | bytes 524320 | tf_op jit(solution)/shard_map/ppermute | solution.py:351
  337.0 11.5 %experts.6 = (bf16[1408,2048]{1,0:T(8,128)(2,1)}, bf16[1408,768]{1,0:T(8,128)(2,1)S(1)}, bf16[1408,2048]{1,0:T(8,128)(2,1)}, bf16[1408,768]{1,0:T(8,128)(2,1)S(1...) custom-call(s32[2]{0:T(128)S(1)} %pad_add_fusion.experts, ...), custom_call_target="tpu_custom_call", output_to_operand_aliasing={{0}: (7, {}), {1}: (8, {}), {2}: (9, {}), {3}: (10, {}), {4... | custom-call | flops 6643777536 | bytes 51953672 | tf_op jit(solution)/shard_map/experts/pallas_call | solution.py:934
  364.2 11.9 %experts.7 = (bf16[1408,2048]{1,0:T(8,128)(2,1)}, bf16[1408,768]{1,0:T(8,128)(2,1)S(1)}, bf16[1408,2048]{1,0:T(8,128)(2,1)}, bf16[1408,768]{1,0:T(8,128)(2,1)S(1...) custom-call(s32[2]{0:T(128)S(1)} %pad_add_fusion.experts, ...), custom_call_target="tpu_custom_call", output_to_operand_aliasing={{0}: (7, {}), {1}: (8, {}), {2}: (9, {}), {3}: (10, {}), {4... | custom-call | flops 6643777536 | bytes 51953672 | tf_op jit(solution)/shard_map/experts/pallas_call | solution.py:934
  377.7 10.8 %collective-permute-done.77.refs_3_ = bf16[128,2176]{1,0:T(8,128)(2,1)S(1)} collective-permute-done((bf16[128,2176]{1,0:T(8,128)(2,1)S(1)}, bf16[128,2176]{1,0:T(8,128)(2,1)S(1)}, u32[]{:S(2)}, u32[]{:S(2)}) %collective-permute-start.77) | collective-permute-done | bytes 557088 | tf_op jit(solution)/shard_map/ppermute | solution.py:347
  397.2 9.8 %convolution_bitcast_fusion.2 = f32[1,768,2048]{2,1,0:T(8,128)} fusion(bf16[1408,768]{1,0:T(8,128)(2,1)S(1)} %get-tuple-element.455, bf16[1408,2048]{1,0:T(8,128)(2,1)} %get-tuple-element.456), kind=kOutput, calls=%fused_computation.2 | convolution fusion | flops 4429185024 | bytes 14221312 | tf_op jit(solution)/shard_map/dot_general | solution.py:1211
  416.3 7.2 %convolution_bitcast_fusion.1 = f32[1,2048,768]{2,1,0:T(8,128)} fusion(bf16[1408,2048]{1,0:T(8,128)(2,1)S(1)} %bitcast.103, bf16[1408,768]{1,0:T(8,128)(2,1)S(1)} %get-tuple-element.464), kind=kOutput, calls=%fused_computation.1 | convolution fusion | flops 4429185024 | bytes 14221312 | tf_op jit(solution)/shard_map/dot_general | solution.py:1211
  432.8 7.2 %convolution_bitcast_fusion = f32[1,2048,768]{2,1,0:T(8,128)} fusion(bf16[1408,2048]{1,0:T(8,128)(2,1)S(1)} %bitcast.103, bf16[1408,768]{1,0:T(8,128)(2,1)S(1)} %get-tuple-element.473), kind=kOutput, calls=%fused_computation | convolution fusion | flops 4429185024 | bytes 14221312 | tf_op jit(solution)/shard_map/dot_general | solution.py:1211
  450.3 6.7 %collective-permute-done.88.refs_1_ = bf16[128,2048]{1,0:T(8,128)(2,1)S(1)} collective-permute-done((bf16[128,2048]{1,0:T(8,128)(2,1)S(1)}, bf16[128,2048]{1,0:T(8,128)(2,1)S(1)}, u32[]{:S(2)}, u32[]{:S(2)}) %collective-permute-start.88) | collective-permute-done | bytes 524320 | tf_op jit(solution)/shard_map/ppermute | solution.py:347
  462.5 7.5 %collective-permute-done.93.refs_1_ = bf16[128,2048]{1,0:T(8,128)(2,1)S(1)} collective-permute-done((bf16[128,2048]{1,0:T(8,128)(2,1)S(1)}, bf16[128,2048]{1,0:T(8,128)(2,1)S(1)}, u32[]{:S(2)}, u32[]{:S(2)}) %collective-permute-start.93) | collective-permute-done | bytes 524320 | tf_op jit(solution)/shard_map/ppermute | solution.py:347
  483.3 9.7 %collective-permute-done.98.refs_5_ = bf16[128,2048]{1,0:T(8,128)(2,1)S(1)} collective-permute-done((bf16[128,2048]{1,0:T(8,128)(2,1)S(1)}, bf16[128,2048]{1,0:T(8,128)(2,1)S(1)}, u32[]{:S(2)}, u32[]{:S(2)}) %collective-permute-start.98) | collective-permute-done | bytes 524320 | tf_op jit(solution)/shard_map/ppermute | solution.py:335
  501.9 10.8 %collective-permute-done.99.refs_1_ = bf16[128,1024]{1,0:T(8,128)(2,1)S(1)} collective-permute-done((bf16[128,1024]{1,0:T(8,128)(2,1)S(1)}, bf16[128,1024]{1,0:T(8,128)(2,1)S(1)}, u32[]{:S(2)}, u32[]{:S(2)}) %collective-permute-start.99) | collective-permute-done | bytes 262176 | tf_op jit(solution)/shard_map/ppermute | solution.py:351
  517.0 14.5 %attention_backward.1 = (bf16[512,1280]{1,0:T(8,128)(2,1)S(1)}, f32[1,128]{1,0:T(1,128)S(1)}, f32[1,128]{1,0:T(1,128)S(1)}) custom-call(s32[1]{0:T(128)} %bitcast.16.core, f32[512,1280]{1,0:T(8,128)S(1)} %copy-done.9, bf16[512,1024]{1,0:T(8,128)(2,1)S(1)} %attended_grad.1.grad_attended, f32[256,128]{1,0:T(8,128)S(1)} %pad_maximum_fusion.1.cosine.refs_0_, ...), custom_call_target="tpu_custom_call" | custom-call | flops 1342177280 | bytes 5244932 | tf_op jit(solution)/shard_map/attention_backward/pallas_call | solution.py:934
  550.2 7.7 %normed_grad.1 = (bf16[256,2048]{1,0:T(8,128)(2,1)S(1)}, f32[256,2048]{1,0:T(8,128)S(1)}, f32[1,2048]{1,0:T(1,128)S(1)}) custom-call(s32[16]{0:T(128)S(1)} %copy-done.31, bf16[512,1280]{1,0:T(8,128)(2,1)S(1)} %get-tuple-element.543.right.grad_raw, f32[1,2048]{1,0:T(1,128)S(1)} %bitcast.88, bf16[128,2048]{1,0:T(8,128)(2,1)S(1)} %copy-done.23, ...), custom_call_target="tpu_custom_call" | custom-call | flops 2684354560 | bytes 12337216 | tf_op jit(solution)/shard_map/normed_grad/pallas_call | solution.py:934
  557.9 8.8 %collective-permute-done.116.refs_1_ = bf16[128,1408]{1,0:T(8,128)(2,1)S(1)} collective-permute-done((bf16[128,1408]{1,0:T(8,128)(2,1)S(1)}, bf16[128,1408]{1,0:T(8,128)(2,1)S(1)}, u32[]{:S(2)}, u32[]{:S(2)}) %collective-permute-start.116) | collective-permute-done | bytes 360480 | tf_op jit(solution)/shard_map/ppermute | solution.py:351
  588.8 8.1 %collective-permute-done.124 = f32[34,128]{1,0:T(8,128)S(1)} collective-permute-done((f32[34,128]{1,0:T(8,128)S(1)}, f32[34,128]{1,0:T(8,128)S(1)}, u32[]{:S(2)}, u32[]{:S(2)}) %collective-permute-start.124) | collective-permute-done | bytes 17440 | tf_op jit(solution)/shard_map/ppermute | solution.py:351
  597.0 5.9 collective-permute-done.127.refs_4_
  614.5 5.9 collective-permute-done.131.refs_4_
  (618 shorter events, 359.7 us)
Async XLA Ops:
  6.0 17.1 %collective-permute-start = (bf16[128,1408]{1,0:T(8,128)(2,1)}, bf16[128,1408]{1,0:T(8,128)(2,1)S(1)}, u32[]{:S(2)}, u32[]{:S(2)}) collective-permute-start(bf16[128,1408]{1,0:T(8,128)(2,1)} %concatenate.50), channel_id=1, source_target_pairs={{0,8},{2,10},{4,12},{6,14},{8,0},{10,2},{12,4},{14,6},{16,24},{18,... | collective-permute-start | bytes 1081352 | tf_op jit(solution)/shard_map/ppermute | solution.py:339
  12.1 18.0 %collective-permute-start.4 = (bf16[128,1408]{1,0:T(8,128)(2,1)S(1)}, bf16[128,1408]{1,0:T(8,128)(2,1)S(1)}, u32[]{:S(2)}, u32[]{:S(2)}) collective-permute-start(bf16[128,1408]{1,0:T(8,128)(2,1)S(1)} %concatenate.49.refs_4_), channel_id=1, source_target_pairs={{0,16},{2,18},{4,20},{6,22},{8,24},{10,26},{12,28},{14,30},{16,0},... | collective-permute-start | bytes 1081352 | tf_op jit(solution)/shard_map/ppermute | solution.py:343
  28.4 17.2 %collective-permute-start.3 = (bf16[128,1408]{1,0:T(8,128)(2,1)S(1)}, bf16[128,1408]{1,0:T(8,128)(2,1)S(1)}, u32[]{:S(2)}, u32[]{:S(2)}) collective-permute-start(bf16[128,1408]{1,0:T(8,128)(2,1)S(1)} %collective-permute-done.refs_8_), channel_id=1, source_target_pairs={{0,16},{2,18},{4,20},{6,22},{8,24},{10,26},{12,28},{14,30},{16,0},... | collective-permute-start | bytes 1081352 | tf_op jit(solution)/shard_map/ppermute | solution.py:343
  58.3 18.6 %collective-permute-start.11 = (bf16[128,2048]{1,0:T(8,128)(2,1)S(1)}, bf16[128,2048]{1,0:T(8,128)(2,1)S(1)}, u32[]{:S(2)}, u32[]{:S(2)}) collective-permute-start(bf16[128,2048]{1,0:T(8,128)(2,1)S(1)} %fusion.4.refs_0_), channel_id=1, source_target_pairs={{0,1},{1,0},{2,3},{3,2},{4,5},{5,4},{6,7},{7,6},{8,9},{9,8},{10,11... | collective-permute-start | bytes 1572872 | tf_op jit(solution)/shard_map/ppermute | solution.py:355
  58.4 18.6 %collective-permute-start.12 = (bf16[128,2048]{1,0:T(8,128)(2,1)S(1)}, bf16[128,2048]{1,0:T(8,128)(2,1)S(1)}, u32[]{:S(2)}, u32[]{:S(2)}) collective-permute-start(bf16[128,2048]{1,0:T(8,128)(2,1)S(1)} %fusion.4.refs_0_), channel_id=1, source_target_pairs={{0,8},{2,10},{4,12},{6,14},{8,0},{10,2},{12,4},{14,6},{16,24},{18,... | collective-permute-start | bytes 1572872 | tf_op jit(solution)/shard_map/ppermute | solution.py:339
  77.0 16.8 %collective-permute-start.16 = (bf16[128,2048]{1,0:T(8,128)(2,1)S(1)}, bf16[128,2048]{1,0:T(8,128)(2,1)S(1)}, u32[]{:S(2)}, u32[]{:S(2)}) collective-permute-start(bf16[128,2048]{1,0:T(8,128)(2,1)S(1)} %collective-permute-done.12.refs_2_), channel_id=1, source_target_pairs={{0,1},{1,0},{2,3},{3,2},{4,5},{5,4},{6,7},{7,6},{8,9},{9,8},{10,11... | collective-permute-start | bytes 1572872 | tf_op jit(solution)/shard_map/ppermute | solution.py:355
  77.0 16.7 %collective-permute-start.17 = (bf16[128,1408]{1,0:T(8,128)(2,1)}, bf16[128,1408]{1,0:T(8,128)(2,1)}, u32[]{:S(2)}, u32[]{:S(2)}) collective-permute-start(bf16[128,1408]{1,0:T(8,128)(2,1)} %collective-permute-done.13.refs_18_), channel_id=1, source_target_pairs={{0,2},{2,0},{4,6},{6,4},{8,10},{10,8},{12,14},{14,12},{16,18},{18,... | collective-permute-start | bytes 1081352 | tf_op jit(solution)/shard_map/ppermute | solution.py:351
  93.7 19.1 %collective-permute-start.21 = (bf16[1024,128]{1,0:T(8,128)(2,1)S(1)}, bf16[1024,128]{1,0:T(8,128)(2,1)}, u32[]{:S(2)}, u32[]{:S(2)}) collective-permute-start(bf16[1024,128]{1,0:T(8,128)(2,1)S(1)} %collective-permute-done.18.refs_1_.refs_5_), channel_id=1, source_target_pairs={{0,4},{2,6},{4,0},{6,2},{8,12},{10,14},{12,8},{14,10},{16,20},{18,... | collective-permute-start | bytes 786440 | tf_op jit(solution)/shard_map/ppermute | solution.py:347
  95.3 17.5 %collective-permute-start.22 = (bf16[1024,128]{1,0:T(8,128)(2,1)}, bf16[1024,128]{1,0:T(8,128)(2,1)}, u32[]{:S(2)}, u32[]{:S(2)}) collective-permute-start(bf16[1024,128]{1,0:T(8,128)(2,1)} %collective-permute-done.20.refs_4_.refs_8_), channel_id=1, source_target_pairs={{0,2},{2,0},{4,6},{6,4},{8,10},{10,8},{12,14},{14,12},{16,18},{18,... | collective-permute-start | bytes 786440 | tf_op jit(solution)/shard_map/ppermute | solution.py:351
  165.1 16.7 %collective-permute-start.38 = (bf16[128,2048]{1,0:T(8,128)(2,1)S(1)}, bf16[128,2048]{1,0:T(8,128)(2,1)S(1)}, u32[]{:S(2)}, u32[]{:S(2)}) collective-permute-start(bf16[128,2048]{1,0:T(8,128)(2,1)S(1)} %collective-permute-done.35.refs_4_), channel_id=1, source_target_pairs={{0,8},{2,10},{4,12},{6,14},{8,16},{10,18},{12,20},{14,22},{16,24},... | collective-permute-start | bytes 1572872 | tf_op jit(solution)/shard_map/ppermute | solution.py:335
  165.2 16.6 %collective-permute-start.39 = (bf16[128,2048]{1,0:T(8,128)(2,1)S(1)}, bf16[128,2048]{1,0:T(8,128)(2,1)S(1)}, u32[]{:S(2)}, u32[]{:S(2)}) collective-permute-start(bf16[128,2048]{1,0:T(8,128)(2,1)S(1)} %collective-permute-done.35.refs_4_), channel_id=1, source_target_pairs={{0,2},{2,0},{4,6},{6,4},{8,10},{10,8},{12,14},{14,12},{16,18},{18,... | collective-permute-start | bytes 1572872 | tf_op jit(solution)/shard_map/ppermute | solution.py:351
  167.4 25.4 %collective-permute-start.34 = (bf16[128,2048]{1,0:T(8,128)(2,1)S(1)}, bf16[128,2048]{1,0:T(8,128)(2,1)S(1)}, u32[]{:S(2)}, u32[]{:S(2)}) collective-permute-start(bf16[128,2048]{1,0:T(8,128)(2,1)S(1)} %slice.164), channel_id=1, source_target_pairs={{0,8},{2,10},{4,12},{6,14},{8,0},{10,2},{12,4},{14,6},{16,24},{18,... | collective-permute-start | bytes 1572872 | tf_op jit(solution)/shard_map/ppermute | solution.py:339
  185.6 17.4 %collective-permute-start.43 = (bf16[128,2048]{1,0:T(8,128)(2,1)S(1)}, bf16[128,2048]{1,0:T(8,128)(2,1)}, u32[]{:S(2)}, u32[]{:S(2)}) collective-permute-start(bf16[128,2048]{1,0:T(8,128)(2,1)S(1)} %collective-permute-done.38.refs_4_), channel_id=1, source_target_pairs={{0,8},{2,10},{4,12},{6,14},{8,16},{10,18},{12,20},{14,22},{16,24},... | collective-permute-start | bytes 1572872 | tf_op jit(solution)/shard_map/ppermute | solution.py:335
  236.3 20.1 %collective-permute-start.51 = (bf16[128,2048]{1,0:T(8,128)(2,1)}, bf16[128,2048]{1,0:T(8,128)(2,1)S(1)}, u32[]{:S(2)}, u32[]{:S(2)}) collective-permute-start(bf16[128,2048]{1,0:T(8,128)(2,1)} %collective-permute-done.48.refs_0_), channel_id=1, source_target_pairs={{0,8},{2,10},{4,12},{6,14},{8,16},{10,18},{12,20},{14,22},{16,24},... | collective-permute-start | bytes 1572872 | tf_op jit(solution)/shard_map/ppermute | solution.py:335
  236.4 20.1 %collective-permute-start.52 = (bf16[128,2048]{1,0:T(8,128)(2,1)}, bf16[128,2048]{1,0:T(8,128)(2,1)S(1)}, u32[]{:S(2)}, u32[]{:S(2)}) collective-permute-start(bf16[128,2048]{1,0:T(8,128)(2,1)} %collective-permute-done.48.refs_0_), channel_id=1, source_target_pairs={{0,2},{2,0},{4,6},{6,4},{8,10},{10,8},{12,14},{14,12},{16,18},{18,... | collective-permute-start | bytes 1572872 | tf_op jit(solution)/shard_map/ppermute | solution.py:351
  236.9 19.6 %collective-permute-start.53 = (bf16[128,2048]{1,0:T(8,128)(2,1)}, bf16[128,2048]{1,0:T(8,128)(2,1)S(1)}, u32[]{:S(2)}, u32[]{:S(2)}) collective-permute-start(bf16[128,2048]{1,0:T(8,128)(2,1)} %collective-permute-done.46.refs_0_), channel_id=1, source_target_pairs={{0,4},{2,6},{4,0},{6,2},{8,12},{10,14},{12,8},{14,10},{16,20},{18,... | collective-permute-start | bytes 1572872 | tf_op jit(solution)/shard_map/ppermute | solution.py:347
  273.4 18.3 %collective-permute-start.59 = (bf16[128,2048]{1,0:T(8,128)(2,1)}, bf16[128,2048]{1,0:T(8,128)(2,1)S(1)}, u32[]{:S(2)}, u32[]{:S(2)}) collective-permute-start(bf16[128,2048]{1,0:T(8,128)(2,1)} %collective-permute-done.43.refs_4_), channel_id=1, source_target_pairs={{0,2},{2,0},{4,6},{6,4},{8,10},{10,8},{12,14},{14,12},{16,18},{18,... | collective-permute-start | bytes 1572872 | tf_op jit(solution)/shard_map/ppermute | solution.py:351
  273.9 17.8 %collective-permute-start.60 = (bf16[128,2048]{1,0:T(8,128)(2,1)S(1)}, bf16[128,2048]{1,0:T(8,128)(2,1)S(1)}, u32[]{:S(2)}, u32[]{:S(2)}) collective-permute-start(bf16[128,2048]{1,0:T(8,128)(2,1)S(1)} %copy-done.13), channel_id=1, source_target_pairs={{0,4},{2,6},{4,0},{6,2},{8,12},{10,14},{12,8},{14,10},{16,20},{18,... | collective-permute-start | bytes 1572872 | tf_op jit(solution)/shard_map/ppermute | solution.py:347
  335.1 16.6 %collective-permute-start.70 = (bf16[128,2176]{1,0:T(8,128)(2,1)S(1)}, bf16[128,2176]{1,0:T(8,128)(2,1)S(1)}, u32[]{:S(2)}, u32[]{:S(2)}) collective-permute-start(bf16[128,2176]{1,0:T(8,128)(2,1)S(1)} %copy-done.41), channel_id=1, source_target_pairs={{0,2},{2,0},{4,6},{6,4},{8,10},{10,8},{12,14},{14,12},{16,18},{18,... | collective-permute-start | bytes 1671176 | tf_op jit(solution)/shard_map/ppermute | solution.py:351
  362.9 25.7 %collective-permute-start.77 = (bf16[128,2176]{1,0:T(8,128)(2,1)S(1)}, bf16[128,2176]{1,0:T(8,128)(2,1)S(1)}, u32[]{:S(2)}, u32[]{:S(2)}) collective-permute-start(bf16[128,2176]{1,0:T(8,128)(2,1)S(1)} %get-tuple-element.438), channel_id=1, source_target_pairs={{0,4},{2,6},{4,0},{6,2},{8,12},{10,14},{12,8},{14,10},{16,20},{18,... | collective-permute-start | bytes 1671176 | tf_op jit(solution)/shard_map/ppermute | solution.py:347
  493.5 19.4 %collective-permute-start.101 = (bf16[128,2048]{1,0:T(8,128)(2,1)S(1)}, bf16[128,2048]{1,0:T(8,128)(2,1)S(1)}, u32[]{:S(2)}, u32[]{:S(2)}) collective-permute-start(bf16[128,2048]{1,0:T(8,128)(2,1)S(1)} %get-tuple-element.511), channel_id=1, source_target_pairs={{0,2},{2,0},{4,6},{6,4},{8,10},{10,8},{12,14},{14,12},{16,18},{18,... | collective-permute-start | bytes 1572872 | tf_op jit(solution)/shard_map/ppermute | solution.py:351
  494.6 18.2 %collective-permute-start.102 = (bf16[128,2048]{1,0:T(8,128)(2,1)S(1)}, bf16[128,2048]{1,0:T(8,128)(2,1)S(1)}, u32[]{:S(2)}, u32[]{:S(2)}) collective-permute-start(bf16[128,2048]{1,0:T(8,128)(2,1)S(1)} %get-tuple-element.512), channel_id=1, source_target_pairs={{0,4},{2,6},{4,0},{6,2},{8,12},{10,14},{12,8},{14,10},{16,20},{18,... | collective-permute-start | bytes 1572872 | tf_op jit(solution)/shard_map/ppermute | solution.py:347
  495.9 16.9 %collective-permute-start.103 = (bf16[128,2048]{1,0:T(8,128)(2,1)S(1)}, bf16[128,2048]{1,0:T(8,128)(2,1)S(1)}, u32[]{:S(2)}, u32[]{:S(2)}) collective-permute-start(bf16[128,2048]{1,0:T(8,128)(2,1)S(1)} %get-tuple-element.513), channel_id=1, source_target_pairs={{0,8},{2,10},{4,12},{6,14},{8,16},{10,18},{12,20},{14,22},{16,24},... | collective-permute-start | bytes 1572872 | tf_op jit(solution)/shard_map/ppermute | solution.py:335
  512.9 19.0 %collective-permute-start.107 = (bf16[128,2048]{1,0:T(8,128)(2,1)S(1)}, bf16[128,2048]{1,0:T(8,128)(2,1)S(1)}, u32[]{:S(2)}, u32[]{:S(2)}) collective-permute-start(bf16[128,2048]{1,0:T(8,128)(2,1)S(1)} %copy-done.51), channel_id=1, source_target_pairs={{0,2},{2,0},{4,6},{6,4},{8,10},{10,8},{12,14},{14,12},{16,18},{18,... | collective-permute-start | bytes 1572872 | tf_op jit(solution)/shard_map/ppermute | solution.py:351
  514.0 17.5 %collective-permute-start.104 = (bf16[128,1024]{1,0:T(8,128)(2,1)S(1)}, bf16[128,1024]{1,0:T(8,128)(2,1)S(1)}, u32[]{:S(2)}, u32[]{:S(2)}) collective-permute-start(bf16[128,1024]{1,0:T(8,128)(2,1)S(1)} %sums.22), channel_id=1, source_target_pairs={{0,4},{2,6},{4,0},{6,2},{8,12},{10,14},{12,8},{14,10},{16,20},{18,... | collective-permute-start | bytes 786440 | tf_op jit(solution)/shard_map/ppermute | solution.py:347
  546.4 20.3 %collective-permute-start.113 = (bf16[128,2048]{1,0:T(8,128)(2,1)S(1)}, bf16[128,2048]{1,0:T(8,128)(2,1)S(1)}, u32[]{:S(2)}, u32[]{:S(2)}) collective-permute-start(bf16[128,2048]{1,0:T(8,128)(2,1)S(1)} %copy-done.49), channel_id=1, source_target_pairs={{0,2},{2,0},{4,6},{6,4},{8,10},{10,8},{12,14},{14,12},{16,18},{18,... | collective-permute-start | bytes 1572872 | tf_op jit(solution)/shard_map/ppermute | solution.py:351
  547.9 18.8 %collective-permute-start.114 = (bf16[128,2048]{1,0:T(8,128)(2,1)S(1)}, bf16[128,2048]{1,0:T(8,128)(2,1)S(1)}, u32[]{:S(2)}, u32[]{:S(2)}) collective-permute-start(bf16[128,2048]{1,0:T(8,128)(2,1)S(1)} %get-tuple-element.540), channel_id=1, source_target_pairs={{0,4},{2,6},{4,0},{6,2},{8,12},{10,14},{12,8},{14,10},{16,20},{18,... | collective-permute-start | bytes 1572872 | tf_op jit(solution)/shard_map/ppermute | solution.py:347
  548.6 18.1 %collective-permute-start.115 = (bf16[128,2048]{1,0:T(8,128)(2,1)S(1)}, bf16[128,2048]{1,0:T(8,128)(2,1)S(1)}, u32[]{:S(2)}, u32[]{:S(2)}) collective-permute-start(bf16[128,2048]{1,0:T(8,128)(2,1)S(1)} %get-tuple-element.541), channel_id=1, source_target_pairs={{0,8},{2,10},{4,12},{6,14},{8,16},{10,18},{12,20},{14,22},{16,24},... | collective-permute-start | bytes 1572872 | tf_op jit(solution)/shard_map/ppermute | solution.py:335
  548.9 17.9 %collective-permute-start.116 = (bf16[128,1408]{1,0:T(8,128)(2,1)S(1)}, bf16[128,1408]{1,0:T(8,128)(2,1)S(1)}, u32[]{:S(2)}, u32[]{:S(2)}) collective-permute-start(bf16[128,1408]{1,0:T(8,128)(2,1)S(1)} %get-tuple-element.542), channel_id=1, source_target_pairs={{0,2},{2,0},{4,6},{6,4},{8,10},{10,8},{12,14},{14,12},{16,18},{18,... | collective-permute-start | bytes 1081352 | tf_op jit(solution)/shard_map/ppermute | solution.py:351
  584.8 18.3 %collective-permute-start.123 = (bf16[128,2048]{1,0:T(8,128)(2,1)S(1)}, bf16[128,2048]{1,0:T(8,128)(2,1)S(1)}, u32[]{:S(2)}, u32[]{:S(2)}) collective-permute-start(bf16[128,2048]{1,0:T(8,128)(2,1)S(1)} %slice.163), channel_id=1, source_target_pairs={{0,8},{2,10},{4,12},{6,14},{8,0},{10,2},{12,4},{14,6},{16,24},{18,... | collective-permute-start | bytes 1572872 | tf_op jit(solution)/shard_map/ppermute | solution.py:339
  606.9 17.3 %collective-permute-start.132 = (bf16[128,1408]{1,0:T(8,128)(2,1)S(1)}, bf16[128,1408]{1,0:T(8,128)(2,1)S(1)}, u32[]{:S(2)}, u32[]{:S(2)}) collective-permute-start(bf16[128,1408]{1,0:T(8,128)(2,1)S(1)} %get-tuple-element.584), channel_id=1, source_target_pairs={{0,16},{2,18},{4,20},{6,22},{8,24},{10,26},{12,28},{14,30},{16,0},... | collective-permute-start | bytes 1081352 | tf_op jit(solution)/shard_map/ppermute | solution.py:343
  626.8 17.3 %collective-permute-start.137 = (bf16[128,1408]{1,0:T(8,128)(2,1)S(1)}, bf16[128,1408]{1,0:T(8,128)(2,1)S(1)}, u32[]{:S(2)}, u32[]{:S(2)}) collective-permute-start(bf16[128,1408]{1,0:T(8,128)(2,1)S(1)} %get-tuple-element.597), channel_id=1, source_target_pairs={{0,16},{2,18},{4,20},{6,22},{8,24},{10,26},{12,28},{14,30},{16,0},... | collective-permute-start | bytes 1081352 | tf_op jit(solution)/shard_map/ppermute | solution.py:343
  (238 other events, 3478.1 us)

commit v3 on v2

--- a/solution.py
+++ b/solution.py
@@ -428,7 +428,7 @@
 
 RETURN_ROUNDS = (
     (((1, 1, 1), (1, 0, 1), y_swap), ((0, 1, 1), (0, 1, 0), x_swap), ((1, 1, 0), (2, 1, 0), z_next)),
-    (((1, 0, 1), (1, 0, 0), x_swap), ((2, 1, 1), (2, 0, 1), y_swap), ((2, 1, 0), (2, 0, 0), y_swap)),
+    (((1, 0, 1), (1, 0, 0), x_swap), ((2, 1, 1), (2, 0, 1), y_swap), ((2, 1, 0), (3, 1, 0), z_next)),
     (((2, 0, 1), (2, 0, 0), x_swap), ((3, 1, 1), (3, 0, 1), y_swap), ((1, 0, 0), (2, 0, 0), z_next)),
     (((3, 0, 1), (3, 0, 0), x_swap), ((3, 1, 0), (3, 0, 0), y_swap), ((2, 0, 0), (3, 0, 0), z_next)),
     (((0, 0, 1), (0, 0, 0), x_swap), ((0, 1, 0), (0, 0, 0), y_swap), ((3, 0, 0), (0, 0, 0), z_next)),

time: 674 us -> 664 us (0.985)
    ppermute x46 -> x45, waiting for transfers between devices: 94.9 us -> 85.7 us  [y_swap(): return lax.ppermute(block, 'dp', Y_PAIR)]
    ppermute x46 -> x45, starting transfers between devices: 51.1 us -> 47.7 us  [y_swap(): return lax.ppermute(block, 'dp', Y_PAIR)]
    ppermute x18 -> x19, waiting for transfers between devices: 83.4 us -> 84.4 us  [z_next(): return lax.ppermute(block, 'dp', Z_RING)]
    unnamed x253 -> x247, local copies, waits for them, and re-layouts: 19.6 us -> 19.1 us
  transfers between devices with their start and end apart: 144 -> 144, of which waited for: 77 -> 80; matrix products, arithmetic and copies ran while one was open for 6% -> 6% of each run, Pallas kernels for 20% -> 20%
where the time goes in v3:
time: 664 us; the launch traced here: 656 us
  waiting for transfers between devices  319 us (48%)
  Pallas kernels  142 us (21%)
  starting transfers between devices  129 us (19%)
  matrix products  25.9 us (4%)
  local copies, waits for them, and re-layouts  22.9 us (3%)
  other arithmetic  15 us (2%)
    pallas_call x21, Pallas kernels, call(): pl.pallas_call(kernel, out_shape=outs, in_specs=[spec for _, spec in ins]...  137 us
    ppermute x45, waiting for transfers between devices, x_swap(): return lax.ppermute(block, 'dp', X_PAIR)  95.9 us
    ppermute x45, waiting for transfers between devices, y_swap(): return lax.ppermute(block, 'dp', Y_PAIR)  85.7 us
    ppermute x19, waiting for transfers between devices, z_next(): return lax.ppermute(block, 'dp', Z_RING)  84.4 us
    ppermute x45, starting transfers between devices, x_swap(): return lax.ppermute(block, 'dp', X_PAIR)  51.1 us
    ppermute x45, starting transfers between devices, y_swap(): return lax.ppermute(block, 'dp', Y_PAIR)  47.7 us
    dot_general x3, matrix products, row_product(): lax.dot_general(after(left, *earlier), right, TN, preferred_element_type=...  24.2 us
    ppermute x9, waiting for transfers between devices, z_pair(): return lax.ppermute(block, 'dp', Z_PAIR)  21.7 us
  transfers between devices with their start and end apart: 144, of which 80 were waited for; matrix products, arithmetic and copies ran while one was open for 6% of the time, Pallas kernels for 20%

profile of v3, /device:TPU:0, one launch (start us, length us, event | category | flops | bytes accessed | tf_op | source)
XLA Modules:
  0.0 656.2 jit_solution(17050593499335833464)
XLA Ops:
  15.1 8.0 %collective-permute-done.refs_8_ = bf16[128,1408]{1,0:T(8,128)(2,1)S(1)} collective-permute-done((bf16[128,1408]{1,0:T(8,128)(2,1)}, bf16[128,1408]{1,0:T(8,128)(2,1)S(1)}, u32[]{:S(2)}, u32[]{:S(2)}) %collective-permute-start) | collective-permute-done | bytes 360480 | tf_op jit(solution)/shard_map/ppermute | solution.py:339
  45.6 7.3 %collective-permute-done.10.refs_11_ = bf16[128,1408]{1,0:T(8,128)(2,1)S(1)} collective-permute-done((bf16[128,1408]{1,0:T(8,128)(2,1)S(1)}, bf16[128,1408]{1,0:T(8,128)(2,1)S(1)}, u32[]{:S(2)}, u32[]{:S(2)}) %collective-permute-start.10) | collective-permute-done | bytes 360480 | tf_op jit(solution)/shard_map/ppermute | solution.py:351
  70.4 6.5 collective-permute-done.15.refs_15_
  82.7 11.0 %collective-permute-done.18.refs_1_.refs_5_ = bf16[1024,128]{1,0:T(8,128)(2,1)S(1)} collective-permute-done((bf16[1024,128]{1,0:T(8,128)(2,1)S(1)}, bf16[1024,128]{1,0:T(8,128)(2,1)S(1)}, u32[]{:S(2)}, u32[]{:S(2)}) %collective-permute-start.18) | collective-permute-done | bytes 262176 | tf_op jit(solution)/shard_map/ppermute | solution.py:351
  102.9 9.8 %attention_raw.1 = (f32[512,1280]{1,0:T(8,128)}, bf16[2048,128]{1,0:T(8,128)(2,1)}, bf16[2048,128]{1,0:T(8,128)(2,1)}) custom-call(s32[16]{0:T(128)} %stack.127.ids, s32[16]{0:T(128)} %stack.144.block_ids, bf16[128,2048]{1,0:T(8,128)(2,1)} %copy-done.22, bf16[128,2048]{1,0:T(8,128)(2,1)} %copy-done.42, bf16[128,2048]{1,0:T(8,128)(2,1)} %copy-done.44, ...), custom_call_target="tpu_custom_call" | custom-call | flops 2684354560 | bytes 11534464 | tf_op jit(solution)/shard_map/attention_raw/pallas_call | solution.py:934
  118.5 9.4 %attention_forward.1.attended.right = bf16[512,1024]{1,0:T(8,128)(2,1)S(1)} custom-call(s32[1]{0:T(128)} %bitcast.16.core, f32[512,1280]{1,0:T(8,128)S(1)} %copy-done.8, f32[256,128]{1,0:T(8,128)S(1)} %pad_maximum_fusion.1.cosine.refs_0_, f32[256,128]{1,0:T(8,128)S(1)} %pad_maximum_fusion.2.sine.refs_1_, f32[1,128]{1,0:T(1,128)S(1)} %bitcast.98, ...), custom_call_target="tpu_custom_call" | custom-call | flops 536870912 | bytes 3933188 | tf_op jit(solution)/shard_map/attention_forward/pallas_call | solution.py:934
  152.1 13.0 %collective-permute-done.35.refs_4_ = bf16[128,2048]{1,0:T(8,128)(2,1)S(1)} collective-permute-done((bf16[128,2048]{1,0:T(8,128)(2,1)S(1)}, bf16[128,2048]{1,0:T(8,128)(2,1)S(1)}, u32[]{:S(2)}, u32[]{:S(2)}) %collective-permute-start.35) | collective-permute-done | bytes 524320 | tf_op jit(solution)/shard_map/ppermute | solution.py:335
  168.6 13.2 %collective-permute-done.38.refs_4_ = bf16[128,2048]{1,0:T(8,128)(2,1)S(1)} collective-permute-done((bf16[128,2048]{1,0:T(8,128)(2,1)S(1)}, bf16[128,2048]{1,0:T(8,128)(2,1)S(1)}, u32[]{:S(2)}, u32[]{:S(2)}) %collective-permute-start.38) | collective-permute-done | bytes 524320 | tf_op jit(solution)/shard_map/ppermute | solution.py:335
  185.6 7.2 %collective-permute-done.34 = bf16[128,2048]{1,0:T(8,128)(2,1)S(1)} collective-permute-done((bf16[128,2048]{1,0:T(8,128)(2,1)S(1)}, bf16[128,2048]{1,0:T(8,128)(2,1)S(1)}, u32[]{:S(2)}, u32[]{:S(2)}) %collective-permute-start.34) | collective-permute-done | bytes 524320 | tf_op jit(solution)/shard_map/ppermute | solution.py:339
  196.7 6.3 collective-permute-done.43.refs_4_
  205.2 10.5 %collective-permute-done.44.refs_1_ = bf16[128,2048]{1,0:T(8,128)(2,1)} collective-permute-done((bf16[128,2048]{1,0:T(8,128)(2,1)S(1)}, bf16[128,2048]{1,0:T(8,128)(2,1)}, u32[]{:S(2)}, u32[]{:S(2)}) %collective-permute-start.44) | collective-permute-done | bytes 524320 | tf_op jit(solution)/shard_map/ppermute | solution.py:351
  244.9 11.4 %experts.4 = (bf16[1408,2048]{1,0:T(8,128)(2,1)}, bf16[1408,768]{1,0:T(8,128)(2,1)S(1)}, bf16[1408,2048]{1,0:T(8,128)(2,1)}, bf16[1408,768]{1,0:T(8,128)(2,1)S(1...) custom-call(s32[2]{0:T(128)S(1)} %pad_add_fusion.experts, ...), custom_call_target="tpu_custom_call" | custom-call | flops 6643777536 | bytes 33931272 | tf_op jit(solution)/shard_map/experts/pallas_call | solution.py:934
  258.5 14.3 %collective-permute-done.55.refs_3_ = bf16[128,2048]{1,0:T(8,128)(2,1)S(1)} collective-permute-done((bf16[128,2048]{1,0:T(8,128)(2,1)}, bf16[128,2048]{1,0:T(8,128)(2,1)S(1)}, u32[]{:S(2)}, u32[]{:S(2)}) %collective-permute-start.55) | collective-permute-done | bytes 524320 | tf_op jit(solution)/shard_map/ppermute | solution.py:335
  279.8 8.7 %collective-permute-done.58.refs_7_ = bf16[128,2048]{1,0:T(8,128)(2,1)S(1)} collective-permute-done((bf16[128,2048]{1,0:T(8,128)(2,1)S(1)}, bf16[128,2048]{1,0:T(8,128)(2,1)S(1)}, u32[]{:S(2)}, u32[]{:S(2)}) %collective-permute-start.58) | collective-permute-done | bytes 524320 | tf_op jit(solution)/shard_map/ppermute | solution.py:335
  295.0 11.5 %experts.5 = (bf16[1408,2048]{1,0:T(8,128)(2,1)}, bf16[1408,768]{1,0:T(8,128)(2,1)S(1)}, bf16[1408,2048]{1,0:T(8,128)(2,1)}, bf16[1408,768]{1,0:T(8,128)(2,1)S(1...) custom-call(s32[2]{0:T(128)S(1)} %pad_add_fusion.experts, ...), custom_call_target="tpu_custom_call", output_to_operand_aliasing={{0}: (7, {}), {1}: (8, {}), {2}: (9, {}), {3}: (10, {}), {4... | custom-call | flops 6643777536 | bytes 51953672 | tf_op jit(solution)/shard_map/experts/pallas_call | solution.py:934
  311.5 10.5 %collective-permute-done.65.refs_7_ = bf16[128,2048]{1,0:T(8,128)(2,1)S(1)} collective-permute-done((bf16[128,2048]{1,0:T(8,128)(2,1)S(1)}, bf16[128,2048]{1,0:T(8,128)(2,1)S(1)}, u32[]{:S(2)}, u32[]{:S(2)}) %collective-permute-start.65) | collective-permute-done | bytes 524320 | tf_op jit(solution)/shard_map/ppermute | solution.py:351
  336.9 11.5 %experts.6 = (bf16[1408,2048]{1,0:T(8,128)(2,1)}, bf16[1408,768]{1,0:T(8,128)(2,1)S(1)}, bf16[1408,2048]{1,0:T(8,128)(2,1)}, bf16[1408,768]{1,0:T(8,128)(2,1)S(1...) custom-call(s32[2]{0:T(128)S(1)} %pad_add_fusion.experts, ...), custom_call_target="tpu_custom_call", output_to_operand_aliasing={{0}: (7, {}), {1}: (8, {}), {2}: (9, {}), {3}: (10, {}), {4... | custom-call | flops 6643777536 | bytes 51953672 | tf_op jit(solution)/shard_map/experts/pallas_call | solution.py:934
  362.6 11.5 %experts.7 = (bf16[1408,2048]{1,0:T(8,128)(2,1)}, bf16[1408,768]{1,0:T(8,128)(2,1)S(1)}, bf16[1408,2048]{1,0:T(8,128)(2,1)}, bf16[1408,768]{1,0:T(8,128)(2,1)S(1...) custom-call(s32[2]{0:T(128)S(1)} %pad_add_fusion.experts, ...), custom_call_target="tpu_custom_call", output_to_operand_aliasing={{0}: (7, {}), {1}: (8, {}), {2}: (9, {}), {3}: (10, {}), {4... | custom-call | flops 6643777536 | bytes 51953672 | tf_op jit(solution)/shard_map/experts/pallas_call | solution.py:934
  387.9 9.8 %convolution_bitcast_fusion.2 = f32[1,768,2048]{2,1,0:T(8,128)} fusion(bf16[1408,768]{1,0:T(8,128)(2,1)S(1)} %get-tuple-element.457, bf16[1408,2048]{1,0:T(8,128)(2,1)} %get-tuple-element.458), kind=kOutput, calls=%fused_computation.2 | convolution fusion | flops 4429185024 | bytes 14221312 | tf_op jit(solution)/shard_map/dot_general | solution.py:1211
  406.5 7.2 %convolution_bitcast_fusion.1 = f32[1,2048,768]{2,1,0:T(8,128)} fusion(bf16[1408,2048]{1,0:T(8,128)(2,1)S(1)} %bitcast.103, bf16[1408,768]{1,0:T(8,128)(2,1)S(1)} %get-tuple-element.466), kind=kOutput, calls=%fused_computation.1 | convolution fusion | flops 4429185024 | bytes 14221312 | tf_op jit(solution)/shard_map/dot_general | solution.py:1211
  423.4 7.2 %convolution_bitcast_fusion = f32[1,2048,768]{2,1,0:T(8,128)} fusion(bf16[1408,2048]{1,0:T(8,128)(2,1)S(1)} %bitcast.103, bf16[1408,768]{1,0:T(8,128)(2,1)S(1)} %get-tuple-element.475), kind=kOutput, calls=%fused_computation | convolution fusion | flops 4429185024 | bytes 14221312 | tf_op jit(solution)/shard_map/dot_general | solution.py:1211
  440.4 7.0 %collective-permute-done.88.refs_1_ = bf16[128,2048]{1,0:T(8,128)(2,1)S(1)} collective-permute-done((bf16[128,2048]{1,0:T(8,128)(2,1)S(1)}, bf16[128,2048]{1,0:T(8,128)(2,1)S(1)}, u32[]{:S(2)}, u32[]{:S(2)}) %collective-permute-start.88) | collective-permute-done | bytes 524320 | tf_op jit(solution)/shard_map/ppermute | solution.py:347
  453.0 7.3 %collective-permute-done.93.refs_1_ = bf16[128,2048]{1,0:T(8,128)(2,1)S(1)} collective-permute-done((bf16[128,2048]{1,0:T(8,128)(2,1)S(1)}, bf16[128,2048]{1,0:T(8,128)(2,1)S(1)}, u32[]{:S(2)}, u32[]{:S(2)}) %collective-permute-start.93) | collective-permute-done | bytes 524320 | tf_op jit(solution)/shard_map/ppermute | solution.py:347
  473.6 10.0 %collective-permute-done.98.refs_5_ = bf16[128,2048]{1,0:T(8,128)(2,1)S(1)} collective-permute-done((bf16[128,2048]{1,0:T(8,128)(2,1)S(1)}, bf16[128,2048]{1,0:T(8,128)(2,1)S(1)}, u32[]{:S(2)}, u32[]{:S(2)}) %collective-permute-start.98) | collective-permute-done | bytes 524320 | tf_op jit(solution)/shard_map/ppermute | solution.py:335
  492.4 10.9 %collective-permute-done.99.refs_1_ = bf16[128,1024]{1,0:T(8,128)(2,1)S(1)} collective-permute-done((bf16[128,1024]{1,0:T(8,128)(2,1)S(1)}, bf16[128,1024]{1,0:T(8,128)(2,1)S(1)}, u32[]{:S(2)}, u32[]{:S(2)}) %collective-permute-start.99) | collective-permute-done | bytes 262176 | tf_op jit(solution)/shard_map/ppermute | solution.py:351
  507.6 14.5 %attention_backward.1 = (bf16[512,1280]{1,0:T(8,128)(2,1)S(1)}, f32[1,128]{1,0:T(1,128)S(1)}, f32[1,128]{1,0:T(1,128)S(1)}) custom-call(s32[1]{0:T(128)} %bitcast.16.core, f32[512,1280]{1,0:T(8,128)S(1)} %copy-done.9, bf16[512,1024]{1,0:T(8,128)(2,1)S(1)} %attended_grad.1.grad_attended, f32[256,128]{1,0:T(8,128)S(1)} %pad_maximum_fusion.1.cosine.refs_0_, ...), custom_call_target="tpu_custom_call" | custom-call | flops 1342177280 | bytes 5244932 | tf_op jit(solution)/shard_map/attention_backward/pallas_call | solution.py:934
  540.8 7.7 %normed_grad.1 = (bf16[256,2048]{1,0:T(8,128)(2,1)S(1)}, f32[256,2048]{1,0:T(8,128)S(1)}, f32[1,2048]{1,0:T(1,128)S(1)}) custom-call(s32[16]{0:T(128)S(1)} %copy-done.31, bf16[512,1280]{1,0:T(8,128)(2,1)S(1)} %get-tuple-element.545.right.grad_raw, f32[1,2048]{1,0:T(1,128)S(1)} %bitcast.88, bf16[128,2048]{1,0:T(8,128)(2,1)S(1)} %copy-done.23, ...), custom_call_target="tpu_custom_call" | custom-call | flops 2684354560 | bytes 12337216 | tf_op jit(solution)/shard_map/normed_grad/pallas_call | solution.py:934
  548.5 9.0 %collective-permute-done.116.refs_1_ = bf16[128,1408]{1,0:T(8,128)(2,1)S(1)} collective-permute-done((bf16[128,1408]{1,0:T(8,128)(2,1)S(1)}, bf16[128,1408]{1,0:T(8,128)(2,1)S(1)}, u32[]{:S(2)}, u32[]{:S(2)}) %collective-permute-start.116) | collective-permute-done | bytes 360480 | tf_op jit(solution)/shard_map/ppermute | solution.py:351
  569.7 6.4 collective-permute-done.119
  580.2 6.8 %collective-permute-done.124 = f32[34,128]{1,0:T(8,128)S(1)} collective-permute-done((f32[34,128]{1,0:T(8,128)S(1)}, f32[34,128]{1,0:T(8,128)S(1)}, u32[]{:S(2)}, u32[]{:S(2)}) %collective-permute-start.124) | collective-permute-done | bytes 17440 | tf_op jit(solution)/shard_map/ppermute | solution.py:351
  587.4 6.8 %collective-permute-done.127.refs_4_ = bf16[128,1408]{1,0:T(8,128)(2,1)S(1)} collective-permute-done((bf16[128,1408]{1,0:T(8,128)(2,1)S(1)}, bf16[128,1408]{1,0:T(8,128)(2,1)S(1)}, u32[]{:S(2)}, u32[]{:S(2)}) %collective-permute-start.127) | collective-permute-done | bytes 360480 | tf_op jit(solution)/shard_map/ppermute | solution.py:347
  605.9 5.9 collective-permute-done.131.refs_4_
  (612 shorter events, 354.9 us)
Async XLA Ops:
  6.0 17.1 %collective-permute-start = (bf16[128,1408]{1,0:T(8,128)(2,1)}, bf16[128,1408]{1,0:T(8,128)(2,1)S(1)}, u32[]{:S(2)}, u32[]{:S(2)}) collective-permute-start(bf16[128,1408]{1,0:T(8,128)(2,1)} %concatenate.50), channel_id=1, source_target_pairs={{0,8},{2,10},{4,12},{6,14},{8,0},{10,2},{12,4},{14,6},{16,24},{18,... | collective-permute-start | bytes 1081352 | tf_op jit(solution)/shard_map/ppermute | solution.py:339
  12.1 18.0 %collective-permute-start.4 = (bf16[128,1408]{1,0:T(8,128)(2,1)S(1)}, bf16[128,1408]{1,0:T(8,128)(2,1)S(1)}, u32[]{:S(2)}, u32[]{:S(2)}) collective-permute-start(bf16[128,1408]{1,0:T(8,128)(2,1)S(1)} %concatenate.49.refs_4_), channel_id=1, source_target_pairs={{0,16},{2,18},{4,20},{6,22},{8,24},{10,26},{12,28},{14,30},{16,0},... | collective-permute-start | bytes 1081352 | tf_op jit(solution)/shard_map/ppermute | solution.py:343
  28.4 17.2 %collective-permute-start.3 = (bf16[128,1408]{1,0:T(8,128)(2,1)S(1)}, bf16[128,1408]{1,0:T(8,128)(2,1)S(1)}, u32[]{:S(2)}, u32[]{:S(2)}) collective-permute-start(bf16[128,1408]{1,0:T(8,128)(2,1)S(1)} %collective-permute-done.refs_8_), channel_id=1, source_target_pairs={{0,16},{2,18},{4,20},{6,22},{8,24},{10,26},{12,28},{14,30},{16,0},... | collective-permute-start | bytes 1081352 | tf_op jit(solution)/shard_map/ppermute | solution.py:343
  58.3 18.6 %collective-permute-start.11 = (bf16[128,2048]{1,0:T(8,128)(2,1)S(1)}, bf16[128,2048]{1,0:T(8,128)(2,1)S(1)}, u32[]{:S(2)}, u32[]{:S(2)}) collective-permute-start(bf16[128,2048]{1,0:T(8,128)(2,1)S(1)} %fusion.4.refs_0_), channel_id=1, source_target_pairs={{0,1},{1,0},{2,3},{3,2},{4,5},{5,4},{6,7},{7,6},{8,9},{9,8},{10,11... | collective-permute-start | bytes 1572872 | tf_op jit(solution)/shard_map/ppermute | solution.py:355
  58.4 18.6 %collective-permute-start.12 = (bf16[128,2048]{1,0:T(8,128)(2,1)S(1)}, bf16[128,2048]{1,0:T(8,128)(2,1)S(1)}, u32[]{:S(2)}, u32[]{:S(2)}) collective-permute-start(bf16[128,2048]{1,0:T(8,128)(2,1)S(1)} %fusion.4.refs_0_), channel_id=1, source_target_pairs={{0,8},{2,10},{4,12},{6,14},{8,0},{10,2},{12,4},{14,6},{16,24},{18,... | collective-permute-start | bytes 1572872 | tf_op jit(solution)/shard_map/ppermute | solution.py:339
  77.0 16.8 %collective-permute-start.16 = (bf16[128,2048]{1,0:T(8,128)(2,1)S(1)}, bf16[128,2048]{1,0:T(8,128)(2,1)S(1)}, u32[]{:S(2)}, u32[]{:S(2)}) collective-permute-start(bf16[128,2048]{1,0:T(8,128)(2,1)S(1)} %collective-permute-done.12.refs_2_), channel_id=1, source_target_pairs={{0,1},{1,0},{2,3},{3,2},{4,5},{5,4},{6,7},{7,6},{8,9},{9,8},{10,11... | collective-permute-start | bytes 1572872 | tf_op jit(solution)/shard_map/ppermute | solution.py:355
  77.0 16.7 %collective-permute-start.17 = (bf16[128,1408]{1,0:T(8,128)(2,1)}, bf16[128,1408]{1,0:T(8,128)(2,1)}, u32[]{:S(2)}, u32[]{:S(2)}) collective-permute-start(bf16[128,1408]{1,0:T(8,128)(2,1)} %collective-permute-done.13.refs_18_), channel_id=1, source_target_pairs={{0,2},{2,0},{4,6},{6,4},{8,10},{10,8},{12,14},{14,12},{16,18},{18,... | collective-permute-start | bytes 1081352 | tf_op jit(solution)/shard_map/ppermute | solution.py:351
  93.7 19.0 %collective-permute-start.21 = (bf16[1024,128]{1,0:T(8,128)(2,1)S(1)}, bf16[1024,128]{1,0:T(8,128)(2,1)}, u32[]{:S(2)}, u32[]{:S(2)}) collective-permute-start(bf16[1024,128]{1,0:T(8,128)(2,1)S(1)} %collective-permute-done.18.refs_1_.refs_5_), channel_id=1, source_target_pairs={{0,4},{2,6},{4,0},{6,2},{8,12},{10,14},{12,8},{14,10},{16,20},{18,... | collective-permute-start | bytes 786440 | tf_op jit(solution)/shard_map/ppermute | solution.py:347
  95.3 17.5 %collective-permute-start.22 = (bf16[1024,128]{1,0:T(8,128)(2,1)}, bf16[1024,128]{1,0:T(8,128)(2,1)}, u32[]{:S(2)}, u32[]{:S(2)}) collective-permute-start(bf16[1024,128]{1,0:T(8,128)(2,1)} %collective-permute-done.20.refs_4_.refs_8_), channel_id=1, source_target_pairs={{0,2},{2,0},{4,6},{6,4},{8,10},{10,8},{12,14},{14,12},{16,18},{18,... | collective-permute-start | bytes 786440 | tf_op jit(solution)/shard_map/ppermute | solution.py:351
  165.1 16.7 %collective-permute-start.38 = (bf16[128,2048]{1,0:T(8,128)(2,1)S(1)}, bf16[128,2048]{1,0:T(8,128)(2,1)S(1)}, u32[]{:S(2)}, u32[]{:S(2)}) collective-permute-start(bf16[128,2048]{1,0:T(8,128)(2,1)S(1)} %collective-permute-done.35.refs_4_), channel_id=1, source_target_pairs={{0,8},{2,10},{4,12},{6,14},{8,16},{10,18},{12,20},{14,22},{16,24},... | collective-permute-start | bytes 1572872 | tf_op jit(solution)/shard_map/ppermute | solution.py:335
  165.2 16.6 %collective-permute-start.39 = (bf16[128,2048]{1,0:T(8,128)(2,1)S(1)}, bf16[128,2048]{1,0:T(8,128)(2,1)S(1)}, u32[]{:S(2)}, u32[]{:S(2)}) collective-permute-start(bf16[128,2048]{1,0:T(8,128)(2,1)S(1)} %collective-permute-done.35.refs_4_), channel_id=1, source_target_pairs={{0,2},{2,0},{4,6},{6,4},{8,10},{10,8},{12,14},{14,12},{16,18},{18,... | collective-permute-start | bytes 1572872 | tf_op jit(solution)/shard_map/ppermute | solution.py:351
  167.4 25.4 %collective-permute-start.34 = (bf16[128,2048]{1,0:T(8,128)(2,1)S(1)}, bf16[128,2048]{1,0:T(8,128)(2,1)S(1)}, u32[]{:S(2)}, u32[]{:S(2)}) collective-permute-start(bf16[128,2048]{1,0:T(8,128)(2,1)S(1)} %slice.164), channel_id=1, source_target_pairs={{0,8},{2,10},{4,12},{6,14},{8,0},{10,2},{12,4},{14,6},{16,24},{18,... | collective-permute-start | bytes 1572872 | tf_op jit(solution)/shard_map/ppermute | solution.py:339
  185.6 17.4 %collective-permute-start.43 = (bf16[128,2048]{1,0:T(8,128)(2,1)S(1)}, bf16[128,2048]{1,0:T(8,128)(2,1)}, u32[]{:S(2)}, u32[]{:S(2)}) collective-permute-start(bf16[128,2048]{1,0:T(8,128)(2,1)S(1)} %collective-permute-done.38.refs_4_), channel_id=1, source_target_pairs={{0,8},{2,10},{4,12},{6,14},{8,16},{10,18},{12,20},{14,22},{16,24},... | collective-permute-start | bytes 1572872 | tf_op jit(solution)/shard_map/ppermute | solution.py:335
  236.3 20.1 %collective-permute-start.51 = (bf16[128,2048]{1,0:T(8,128)(2,1)}, bf16[128,2048]{1,0:T(8,128)(2,1)S(1)}, u32[]{:S(2)}, u32[]{:S(2)}) collective-permute-start(bf16[128,2048]{1,0:T(8,128)(2,1)} %collective-permute-done.48.refs_0_), channel_id=1, source_target_pairs={{0,8},{2,10},{4,12},{6,14},{8,16},{10,18},{12,20},{14,22},{16,24},... | collective-permute-start | bytes 1572872 | tf_op jit(solution)/shard_map/ppermute | solution.py:335
  236.3 20.1 %collective-permute-start.52 = (bf16[128,2048]{1,0:T(8,128)(2,1)}, bf16[128,2048]{1,0:T(8,128)(2,1)S(1)}, u32[]{:S(2)}, u32[]{:S(2)}) collective-permute-start(bf16[128,2048]{1,0:T(8,128)(2,1)} %collective-permute-done.48.refs_0_), channel_id=1, source_target_pairs={{0,2},{2,0},{4,6},{6,4},{8,10},{10,8},{12,14},{14,12},{16,18},{18,... | collective-permute-start | bytes 1572872 | tf_op jit(solution)/shard_map/ppermute | solution.py:351
  236.9 19.5 %collective-permute-start.53 = (bf16[128,2048]{1,0:T(8,128)(2,1)}, bf16[128,2048]{1,0:T(8,128)(2,1)S(1)}, u32[]{:S(2)}, u32[]{:S(2)}) collective-permute-start(bf16[128,2048]{1,0:T(8,128)(2,1)} %collective-permute-done.46.refs_0_), channel_id=1, source_target_pairs={{0,4},{2,6},{4,0},{6,2},{8,12},{10,14},{12,8},{14,10},{16,20},{18,... | collective-permute-start | bytes 1572872 | tf_op jit(solution)/shard_map/ppermute | solution.py:347
  273.3 18.3 %collective-permute-start.59 = (bf16[128,2048]{1,0:T(8,128)(2,1)}, bf16[128,2048]{1,0:T(8,128)(2,1)S(1)}, u32[]{:S(2)}, u32[]{:S(2)}) collective-permute-start(bf16[128,2048]{1,0:T(8,128)(2,1)} %collective-permute-done.43.refs_4_), channel_id=1, source_target_pairs={{0,2},{2,0},{4,6},{6,4},{8,10},{10,8},{12,14},{14,12},{16,18},{18,... | collective-permute-start | bytes 1572872 | tf_op jit(solution)/shard_map/ppermute | solution.py:351
  273.8 17.8 %collective-permute-start.60 = (bf16[128,2048]{1,0:T(8,128)(2,1)S(1)}, bf16[128,2048]{1,0:T(8,128)(2,1)S(1)}, u32[]{:S(2)}, u32[]{:S(2)}) collective-permute-start(bf16[128,2048]{1,0:T(8,128)(2,1)S(1)} %copy-done.13), channel_id=1, source_target_pairs={{0,4},{2,6},{4,0},{6,2},{8,12},{10,14},{12,8},{14,10},{16,20},{18,... | collective-permute-start | bytes 1572872 | tf_op jit(solution)/shard_map/ppermute | solution.py:347
  484.1 19.4 %collective-permute-start.101 = (bf16[128,2048]{1,0:T(8,128)(2,1)S(1)}, bf16[128,2048]{1,0:T(8,128)(2,1)S(1)}, u32[]{:S(2)}, u32[]{:S(2)}) collective-permute-start(bf16[128,2048]{1,0:T(8,128)(2,1)S(1)} %get-tuple-element.513), channel_id=1, source_target_pairs={{0,2},{2,0},{4,6},{6,4},{8,10},{10,8},{12,14},{14,12},{16,18},{18,... | collective-permute-start | bytes 1572872 | tf_op jit(solution)/shard_map/ppermute | solution.py:351
  485.6 17.8 %collective-permute-start.102 = (bf16[128,2048]{1,0:T(8,128)(2,1)S(1)}, bf16[128,2048]{1,0:T(8,128)(2,1)S(1)}, u32[]{:S(2)}, u32[]{:S(2)}) collective-permute-start(bf16[128,2048]{1,0:T(8,128)(2,1)S(1)} %get-tuple-element.514), channel_id=1, source_target_pairs={{0,4},{2,6},{4,0},{6,2},{8,12},{10,14},{12,8},{14,10},{16,20},{18,... | collective-permute-start | bytes 1572872 | tf_op jit(solution)/shard_map/ppermute | solution.py:347
  486.3 17.2 %collective-permute-start.103 = (bf16[128,2048]{1,0:T(8,128)(2,1)S(1)}, bf16[128,2048]{1,0:T(8,128)(2,1)S(1)}, u32[]{:S(2)}, u32[]{:S(2)}) collective-permute-start(bf16[128,2048]{1,0:T(8,128)(2,1)S(1)} %get-tuple-element.515), channel_id=1, source_target_pairs={{0,8},{2,10},{4,12},{6,14},{8,16},{10,18},{12,20},{14,22},{16,24},... | collective-permute-start | bytes 1572872 | tf_op jit(solution)/shard_map/ppermute | solution.py:335
  486.3 17.0 %collective-permute-start.99 = (bf16[128,1024]{1,0:T(8,128)(2,1)S(1)}, bf16[128,1024]{1,0:T(8,128)(2,1)S(1)}, u32[]{:S(2)}, u32[]{:S(2)}) collective-permute-start(bf16[128,1024]{1,0:T(8,128)(2,1)S(1)} %get-tuple-element.508), channel_id=1, source_target_pairs={{0,2},{2,0},{4,6},{6,4},{8,10},{10,8},{12,14},{14,12},{16,18},{18,... | collective-permute-start | bytes 786440 | tf_op jit(solution)/shard_map/ppermute | solution.py:351
  503.5 19.0 %collective-permute-start.107 = (bf16[128,2048]{1,0:T(8,128)(2,1)S(1)}, bf16[128,2048]{1,0:T(8,128)(2,1)S(1)}, u32[]{:S(2)}, u32[]{:S(2)}) collective-permute-start(bf16[128,2048]{1,0:T(8,128)(2,1)S(1)} %copy-done.51), channel_id=1, source_target_pairs={{0,2},{2,0},{4,6},{6,4},{8,10},{10,8},{12,14},{14,12},{16,18},{18,... | collective-permute-start | bytes 1572872 | tf_op jit(solution)/shard_map/ppermute | solution.py:351
  505.0 17.1 %collective-permute-start.104 = (bf16[128,1024]{1,0:T(8,128)(2,1)S(1)}, bf16[128,1024]{1,0:T(8,128)(2,1)S(1)}, u32[]{:S(2)}, u32[]{:S(2)}) collective-permute-start(bf16[128,1024]{1,0:T(8,128)(2,1)S(1)} %sums.22), channel_id=1, source_target_pairs={{0,4},{2,6},{4,0},{6,2},{8,12},{10,14},{12,8},{14,10},{16,20},{18,... | collective-permute-start | bytes 786440 | tf_op jit(solution)/shard_map/ppermute | solution.py:347
  537.2 20.3 %collective-permute-start.113 = (bf16[128,2048]{1,0:T(8,128)(2,1)S(1)}, bf16[128,2048]{1,0:T(8,128)(2,1)S(1)}, u32[]{:S(2)}, u32[]{:S(2)}) collective-permute-start(bf16[128,2048]{1,0:T(8,128)(2,1)S(1)} %copy-done.49), channel_id=1, source_target_pairs={{0,2},{2,0},{4,6},{6,4},{8,10},{10,8},{12,14},{14,12},{16,18},{18,... | collective-permute-start | bytes 1572872 | tf_op jit(solution)/shard_map/ppermute | solution.py:351
  538.3 19.2 %collective-permute-start.114 = (bf16[128,2048]{1,0:T(8,128)(2,1)S(1)}, bf16[128,2048]{1,0:T(8,128)(2,1)S(1)}, u32[]{:S(2)}, u32[]{:S(2)}) collective-permute-start(bf16[128,2048]{1,0:T(8,128)(2,1)S(1)} %get-tuple-element.542), channel_id=1, source_target_pairs={{0,4},{2,6},{4,0},{6,2},{8,12},{10,14},{12,8},{14,10},{16,20},{18,... | collective-permute-start | bytes 1572872 | tf_op jit(solution)/shard_map/ppermute | solution.py:347
  539.7 17.9 %collective-permute-start.115 = (bf16[128,2048]{1,0:T(8,128)(2,1)S(1)}, bf16[128,2048]{1,0:T(8,128)(2,1)S(1)}, u32[]{:S(2)}, u32[]{:S(2)}) collective-permute-start(bf16[128,2048]{1,0:T(8,128)(2,1)S(1)} %get-tuple-element.543), channel_id=1, source_target_pairs={{0,8},{2,10},{4,12},{6,14},{8,16},{10,18},{12,20},{14,22},{16,24},... | collective-permute-start | bytes 1572872 | tf_op jit(solution)/shard_map/ppermute | solution.py:335
  539.9 17.7 %collective-permute-start.116 = (bf16[128,1408]{1,0:T(8,128)(2,1)S(1)}, bf16[128,1408]{1,0:T(8,128)(2,1)S(1)}, u32[]{:S(2)}, u32[]{:S(2)}) collective-permute-start(bf16[128,1408]{1,0:T(8,128)(2,1)S(1)} %get-tuple-element.544), channel_id=1, source_target_pairs={{0,2},{2,0},{4,6},{6,4},{8,10},{10,8},{12,14},{14,12},{16,18},{18,... | collective-permute-start | bytes 1081352 | tf_op jit(solution)/shard_map/ppermute | solution.py:351
  576.1 18.3 %collective-permute-start.123 = (bf16[128,2048]{1,0:T(8,128)(2,1)S(1)}, bf16[128,2048]{1,0:T(8,128)(2,1)S(1)}, u32[]{:S(2)}, u32[]{:S(2)}) collective-permute-start(bf16[128,2048]{1,0:T(8,128)(2,1)S(1)} %slice.163), channel_id=1, source_target_pairs={{0,8},{2,10},{4,12},{6,14},{8,0},{10,2},{12,4},{14,6},{16,24},{18,... | collective-permute-start | bytes 1572872 | tf_op jit(solution)/shard_map/ppermute | solution.py:339
  577.3 16.9 %collective-permute-start.127 = (bf16[128,1408]{1,0:T(8,128)(2,1)S(1)}, bf16[128,1408]{1,0:T(8,128)(2,1)S(1)}, u32[]{:S(2)}, u32[]{:S(2)}) collective-permute-start(bf16[128,1408]{1,0:T(8,128)(2,1)S(1)} %get-tuple-element.571), channel_id=1, source_target_pairs={{0,4},{2,6},{4,0},{6,2},{8,12},{10,14},{12,8},{14,10},{16,20},{18,... | collective-permute-start | bytes 1081352 | tf_op jit(solution)/shard_map/ppermute | solution.py:347
  596.9 17.3 %collective-permute-start.132 = (bf16[128,1408]{1,0:T(8,128)(2,1)S(1)}, bf16[128,1408]{1,0:T(8,128)(2,1)S(1)}, u32[]{:S(2)}, u32[]{:S(2)}) collective-permute-start(bf16[128,1408]{1,0:T(8,128)(2,1)S(1)} %get-tuple-element.586), channel_id=1, source_target_pairs={{0,16},{2,18},{4,20},{6,22},{8,24},{10,26},{12,28},{14,30},{16,0},... | collective-permute-start | bytes 1081352 | tf_op jit(solution)/shard_map/ppermute | solution.py:343
  617.3 17.2 %collective-permute-start.137 = (bf16[128,1408]{1,0:T(8,128)(2,1)S(1)}, bf16[128,1408]{1,0:T(8,128)(2,1)S(1)}, u32[]{:S(2)}, u32[]{:S(2)}) collective-permute-start(bf16[128,1408]{1,0:T(8,128)(2,1)S(1)} %get-tuple-element.599), channel_id=1, source_target_pairs={{0,16},{2,18},{4,20},{6,22},{8,24},{10,26},{12,28},{14,30},{16,0},... | collective-permute-start | bytes 1081352 | tf_op jit(solution)/shard_map/ppermute | solution.py:343
  (235 other events, 3444.5 us)

commit v4 on v3

--- a/solution.py
+++ b/solution.py
@@ -359,10 +359,14 @@
     return lax.optimization_barrier((value, *earlier))[0]
 
 
-def plus(own, *others):
-    total = own.astype(wide)
-    for other in others:
-        total = total + other.astype(wide)
+def part(term):
+    return term[0][term[1]] if isinstance(term, tuple) else term
+
+
+def plus(*terms):
+    total = part(terms[0]).astype(wide)
+    for other in terms[1:]:
+        total = total + part(other).astype(wide)
     return total
 
 
@@ -479,42 +483,75 @@
         if later is not None:
             for terms, moves in pairs:
                 for move in moves:
-                    terms[move[0]][-1] = after(terms[move[0]][-1], later)
-        values = totals([terms[move[0]] for terms, moves in pairs for move in moves])
-        moves = [move for _, moves in pairs for move in moves]
-        results, rest = self.round(values, moves, others)
-        for (terms, end), result in zip([(t, m[1]) for t, ms in pairs for m in ms], results):
-            terms[end].append(result)
+                    last = terms[move[0]][-1]
+                    held = isinstance(last, tuple)
+                    gated = after(last[0] if held else last, later)
+                    terms[move[0]][-1] = (gated, last[1]) if held else gated
+        gathered = []
+        for terms, moves in pairs:
+            for move in moves:
+                same = [g for g in gathered if g[0] is terms and g[1] is move[2] and len(g[2]) == 1]
+                if same and terms[move[0]][0].shape[-1] < 2000:
+                    same[0][2].append(move)
+                else:
+                    gathered.append((terms, move[2], [move]))
+        groups = [[terms[move[0]] for move in moves] for terms, _, moves in gathered]
+        values = totals(groups)
+        results, rest = self.round(values, [moves[0] for _, _, moves in gathered], others)
+        for (terms, _, moves), result in zip(gathered, results):
+            for index, move in enumerate(moves):
+                terms[move[1]].append((result, index) if len(moves) == 2 else result)
         return rest
 
 
-def sum_kernel(counts, *refs):
-    outs = refs[sum(counts) :]
-    for count, out in zip(counts, outs):
-        terms, refs = refs[:count], refs[count:]
-        out[...] = plus(*[term[...] for term in terms]).astype(out.dtype)
-
-
-def totals(lists):
-    several = [terms for terms in lists if len(terms) > 1]
-    if not several:
-        return [terms[0] for terms in lists]
-    operands = [term for terms in several for term in terms]
-    rows = operands[0].shape[0] // 4
-    whole = [(a.shape[0] // 4, a.shape[1]) for a in operands]
-    specs = [pl.BlockSpec(block, lambda i: (i, 0)) for block in whole]
-    firsts = [terms[0] for terms in several]
+def sum_kernel(groups, *refs):
+    outs = refs[sum(sum(group) for group in groups) :]
+    for group, out in zip(groups, outs):
+        for index, count in enumerate(group):
+            terms, refs = refs[:count], refs[count:]
+            total = terms[0][...].astype(wide)
+            for term in terms[1:]:
+                total = total + term[...].astype(wide)
+            if len(group) == 1:
+                out[...] = total.astype(out.dtype)
+            else:
+                out[index] = total.astype(out.dtype)
+
+
+def totals(groups):
+    made = [g for g in groups if len(g) > 1 or len(g[0]) > 1 or isinstance(g[0][0], tuple)]
+    if not made:
+        return [g[0][0] for g in groups]
+    operands, in_specs, out_shape, out_specs = [], [], [], []
+    for group in made:
+        for terms in group:
+            for term in terms:
+                array, index = term if isinstance(term, tuple) else (term, None)
+                rows, columns = array.shape[-2] // 4, array.shape[-1]
+                operands.append(array)
+                if index is None:
+                    in_specs.append(pl.BlockSpec((rows, columns), lambda i: (i, 0)))
+                else:
+                    in_specs.append(
+                        pl.BlockSpec((None, rows, columns), lambda i, index=index: (index, i, 0))
+                    )
+        if len(group) == 1:
+            out_shape.append(jax.ShapeDtypeStruct((4 * rows, columns), low))
+            out_specs.append(pl.BlockSpec((rows, columns), lambda i: (i, 0)))
+        else:
+            out_shape.append(jax.ShapeDtypeStruct((2, 4 * rows, columns), low))
+            out_specs.append(pl.BlockSpec((2, rows, columns), lambda i: (0, i, 0)))
     sums = pl.pallas_call(
-        functools.partial(sum_kernel, [len(terms) for terms in several]),
+        functools.partial(sum_kernel, [[len(terms) for terms in group] for group in made]),
         grid=(4,),
-        out_shape=[jax.ShapeDtypeStruct(a.shape, low) for a in firsts],
-        in_specs=specs,
-        out_specs=[pl.BlockSpec((rows, a.shape[1]), lambda i: (i, 0)) for a in firsts],
+        out_shape=out_shape,
+        in_specs=in_specs,
+        out_specs=out_specs,
         name="sums",
         compiler_params=pltpu.CompilerParams(vmem_limit_bytes=2 * ROOM),
     )(*operands)
     sums = list(sums)
-    return [sums.pop(0) if len(terms) > 1 else terms[0] for terms in lists]
+    return [sums.pop(0) if any(g is m for m in made) else g[0][0] for g in groups]
 
 
 def dot(left, right, dims=None):

time: 664 us -> 662 us (level)
  starting transfers between devices: 129 us -> 117 us
  waiting for transfers between devices: 319 us -> 326 us
    ppermute x9, waiting for transfers between devices: 21.7 us -> 31.3 us  [z_pair(): return lax.ppermute(block, 'dp', Z_PAIR)]
    ppermute x45 -> x41, waiting for transfers between devices: 85.7 us -> 77.2 us  [y_swap(): return lax.ppermute(block, 'dp', Y_PAIR)]
    ppermute x45 -> x43, waiting for transfers between devices: 95.9 us -> 103 us  [x_swap(): return lax.ppermute(block, 'dp', X_PAIR)]
    ppermute x45 -> x41, starting transfers between devices: 47.7 us -> 43.4 us  [y_swap(): return lax.ppermute(block, 'dp', Y_PAIR)]
    ppermute x45 -> x43, starting transfers between devices: 51.1 us -> 47.8 us  [x_swap(): return lax.ppermute(block, 'dp', X_PAIR)]
    unnamed x247 -> x251, local copies, waits for them, and re-layouts: 19.1 us -> 19.1 us
  transfers between devices with their start and end apart: 144 -> 138, of which waited for: 80 -> 80; matrix products, arithmetic and copies ran while one was open for 6% -> 6% of each run, Pallas kernels for 20% -> 20%
where the time goes in v4:
time: 662 us; the launch traced here: 654 us
  waiting for transfers between devices  326 us (49%)
  Pallas kernels  142 us (21%)
  starting transfers between devices  117 us (18%)
  matrix products  25.9 us (4%)
  local copies, waits for them, and re-layouts  24.2 us (4%)
  other arithmetic  15.9 us (2%)
    pallas_call x21, Pallas kernels, call(): pl.pallas_call(kernel, out_shape=outs, in_specs=[spec for _, spec in ins]...  137 us
    ppermute x43, waiting for transfers between devices, x_swap(): return lax.ppermute(block, 'dp', X_PAIR)  103 us
    ppermute x19, waiting for transfers between devices, z_next(): return lax.ppermute(block, 'dp', Z_RING)  83.8 us
    ppermute x41, waiting for transfers between devices, y_swap(): return lax.ppermute(block, 'dp', Y_PAIR)  77.2 us
    ppermute x43, starting transfers between devices, x_swap(): return lax.ppermute(block, 'dp', X_PAIR)  47.8 us
    ppermute x41, starting transfers between devices, y_swap(): return lax.ppermute(block, 'dp', Y_PAIR)  43.4 us
    ppermute x9, waiting for transfers between devices, z_pair(): return lax.ppermute(block, 'dp', Z_PAIR)  31.3 us
    dot_general x3, matrix products, row_product(): lax.dot_general(after(left, *earlier), right, TN, preferred_element_type=...  24.2 us
  transfers between devices with their start and end apart: 138, of which 80 were waited for; matrix products, arithmetic and copies ran while one was open for 6% of the time, Pallas kernels for 20%

profile of v4, /device:TPU:0, one launch (start us, length us, event | category | flops | bytes accessed | tf_op | source)
XLA Modules:
  0.0 653.8 jit_solution(13277449941517230464)
XLA Ops:
  15.1 8.0 %collective-permute-done.refs_8_ = bf16[128,1408]{1,0:T(8,128)(2,1)S(1)} collective-permute-done((bf16[128,1408]{1,0:T(8,128)(2,1)}, bf16[128,1408]{1,0:T(8,128)(2,1)S(1)}, u32[]{:S(2)}, u32[]{:S(2)}) %collective-permute-start) | collective-permute-done | bytes 360480 | tf_op jit(solution)/shard_map/ppermute | solution.py:339
  45.6 7.3 %collective-permute-done.10.refs_11_ = bf16[128,1408]{1,0:T(8,128)(2,1)S(1)} collective-permute-done((bf16[128,1408]{1,0:T(8,128)(2,1)S(1)}, bf16[128,1408]{1,0:T(8,128)(2,1)S(1)}, u32[]{:S(2)}, u32[]{:S(2)}) %collective-permute-start.10) | collective-permute-done | bytes 360480 | tf_op jit(solution)/shard_map/ppermute | solution.py:351
  70.4 6.5 %collective-permute-done.15.refs_15_ = bf16[128,1408]{1,0:T(8,128)(2,1)S(1)} collective-permute-done((bf16[128,1408]{1,0:T(8,128)(2,1)S(1)}, bf16[128,1408]{1,0:T(8,128)(2,1)S(1)}, u32[]{:S(2)}, u32[]{:S(2)}) %collective-permute-start.15) | collective-permute-done | bytes 360480 | tf_op jit(solution)/shard_map/ppermute | solution.py:347
  82.7 11.0 %collective-permute-done.18.refs_1_.refs_5_ = bf16[1024,128]{1,0:T(8,128)(2,1)S(1)} collective-permute-done((bf16[1024,128]{1,0:T(8,128)(2,1)S(1)}, bf16[1024,128]{1,0:T(8,128)(2,1)S(1)}, u32[]{:S(2)}, u32[]{:S(2)}) %collective-permute-start.18) | collective-permute-done | bytes 262176 | tf_op jit(solution)/shard_map/ppermute | solution.py:351
  102.9 9.8 %attention_raw.1 = (f32[512,1280]{1,0:T(8,128)}, bf16[2048,128]{1,0:T(8,128)(2,1)}, bf16[2048,128]{1,0:T(8,128)(2,1)}) custom-call(s32[16]{0:T(128)} %stack.127.ids, s32[16]{0:T(128)} %stack.144.block_ids, bf16[128,2048]{1,0:T(8,128)(2,1)} %copy-done.22, bf16[128,2048]{1,0:T(8,128)(2,1)} %copy-done.42, bf16[128,2048]{1,0:T(8,128)(2,1)} %copy-done.44, ...), custom_call_target="tpu_custom_call" | custom-call | flops 2684354560 | bytes 11534464 | tf_op jit(solution)/shard_map/attention_raw/pallas_call | solution.py:971
  118.5 9.4 %attention_forward.1.attended.right = bf16[512,1024]{1,0:T(8,128)(2,1)S(1)} custom-call(s32[1]{0:T(128)} %bitcast.16.core, f32[512,1280]{1,0:T(8,128)S(1)} %copy-done.8, f32[256,128]{1,0:T(8,128)S(1)} %pad_maximum_fusion.1.cosine.refs_0_, f32[256,128]{1,0:T(8,128)S(1)} %pad_maximum_fusion.2.sine.refs_1_, f32[1,128]{1,0:T(1,128)S(1)} %bitcast.108, ...), custom_call_target="tpu_custom_call" | custom-call | flops 536870912 | bytes 3933188 | tf_op jit(solution)/shard_map/attention_forward/pallas_call | solution.py:971
  152.1 13.0 %collective-permute-done.35.refs_4_ = bf16[128,2048]{1,0:T(8,128)(2,1)S(1)} collective-permute-done((bf16[128,2048]{1,0:T(8,128)(2,1)S(1)}, bf16[128,2048]{1,0:T(8,128)(2,1)S(1)}, u32[]{:S(2)}, u32[]{:S(2)}) %collective-permute-start.35) | collective-permute-done | bytes 524320 | tf_op jit(solution)/shard_map/ppermute | solution.py:335
  168.6 13.2 %collective-permute-done.38.refs_4_ = bf16[128,2048]{1,0:T(8,128)(2,1)S(1)} collective-permute-done((bf16[128,2048]{1,0:T(8,128)(2,1)S(1)}, bf16[128,2048]{1,0:T(8,128)(2,1)S(1)}, u32[]{:S(2)}, u32[]{:S(2)}) %collective-permute-start.38) | collective-permute-done | bytes 524320 | tf_op jit(solution)/shard_map/ppermute | solution.py:335
  185.6 7.2 %collective-permute-done.34 = bf16[128,2048]{1,0:T(8,128)(2,1)S(1)} collective-permute-done((bf16[128,2048]{1,0:T(8,128)(2,1)S(1)}, bf16[128,2048]{1,0:T(8,128)(2,1)S(1)}, u32[]{:S(2)}, u32[]{:S(2)}) %collective-permute-start.34) | collective-permute-done | bytes 524320 | tf_op jit(solution)/shard_map/ppermute | solution.py:339
  196.8 6.2 collective-permute-done.43.refs_4_
  205.2 10.5 %collective-permute-done.44.refs_1_ = bf16[128,2048]{1,0:T(8,128)(2,1)} collective-permute-done((bf16[128,2048]{1,0:T(8,128)(2,1)S(1)}, bf16[128,2048]{1,0:T(8,128)(2,1)}, u32[]{:S(2)}, u32[]{:S(2)}) %collective-permute-start.44) | collective-permute-done | bytes 524320 | tf_op jit(solution)/shard_map/ppermute | solution.py:351
  244.9 11.4 %experts.4 = (bf16[1408,2048]{1,0:T(8,128)(2,1)}, bf16[1408,768]{1,0:T(8,128)(2,1)S(1)}, bf16[1408,2048]{1,0:T(8,128)(2,1)}, bf16[1408,768]{1,0:T(8,128)(2,1)S(1...) custom-call(s32[2]{0:T(128)S(1)} %pad_add_fusion.experts, ...), custom_call_target="tpu_custom_call" | custom-call | flops 6643777536 | bytes 33931272 | tf_op jit(solution)/shard_map/experts/pallas_call | solution.py:971
  258.5 14.3 %collective-permute-done.55.refs_3_ = bf16[128,2048]{1,0:T(8,128)(2,1)S(1)} collective-permute-done((bf16[128,2048]{1,0:T(8,128)(2,1)}, bf16[128,2048]{1,0:T(8,128)(2,1)S(1)}, u32[]{:S(2)}, u32[]{:S(2)}) %collective-permute-start.55) | collective-permute-done | bytes 524320 | tf_op jit(solution)/shard_map/ppermute | solution.py:335
  279.8 8.7 %collective-permute-done.58.refs_7_ = bf16[128,2048]{1,0:T(8,128)(2,1)S(1)} collective-permute-done((bf16[128,2048]{1,0:T(8,128)(2,1)S(1)}, bf16[128,2048]{1,0:T(8,128)(2,1)S(1)}, u32[]{:S(2)}, u32[]{:S(2)}) %collective-permute-start.58) | collective-permute-done | bytes 524320 | tf_op jit(solution)/shard_map/ppermute | solution.py:335
  295.0 11.5 %experts.5 = (bf16[1408,2048]{1,0:T(8,128)(2,1)}, bf16[1408,768]{1,0:T(8,128)(2,1)S(1)}, bf16[1408,2048]{1,0:T(8,128)(2,1)}, bf16[1408,768]{1,0:T(8,128)(2,1)S(1...) custom-call(s32[2]{0:T(128)S(1)} %pad_add_fusion.experts, ...), custom_call_target="tpu_custom_call", output_to_operand_aliasing={{0}: (7, {}), {1}: (8, {}), {2}: (9, {}), {3}: (10, {}), {4... | custom-call | flops 6643777536 | bytes 51953672 | tf_op jit(solution)/shard_map/experts/pallas_call | solution.py:971
  311.5 10.5 %collective-permute-done.65.refs_7_ = bf16[128,2048]{1,0:T(8,128)(2,1)S(1)} collective-permute-done((bf16[128,2048]{1,0:T(8,128)(2,1)S(1)}, bf16[128,2048]{1,0:T(8,128)(2,1)S(1)}, u32[]{:S(2)}, u32[]{:S(2)}) %collective-permute-start.65) | collective-permute-done | bytes 524320 | tf_op jit(solution)/shard_map/ppermute | solution.py:351
  336.9 11.5 %experts.6 = (bf16[1408,2048]{1,0:T(8,128)(2,1)}, bf16[1408,768]{1,0:T(8,128)(2,1)S(1)}, bf16[1408,2048]{1,0:T(8,128)(2,1)}, bf16[1408,768]{1,0:T(8,128)(2,1)S(1...) custom-call(s32[2]{0:T(128)S(1)} %pad_add_fusion.experts, ...), custom_call_target="tpu_custom_call", output_to_operand_aliasing={{0}: (7, {}), {1}: (8, {}), {2}: (9, {}), {3}: (10, {}), {4... | custom-call | flops 6643777536 | bytes 51953672 | tf_op jit(solution)/shard_map/experts/pallas_call | solution.py:971
  362.6 11.5 %experts.7 = (bf16[1408,2048]{1,0:T(8,128)(2,1)}, bf16[1408,768]{1,0:T(8,128)(2,1)S(1)}, bf16[1408,2048]{1,0:T(8,128)(2,1)}, bf16[1408,768]{1,0:T(8,128)(2,1)S(1...) custom-call(s32[2]{0:T(128)S(1)} %pad_add_fusion.experts, ...), custom_call_target="tpu_custom_call", output_to_operand_aliasing={{0}: (7, {}), {1}: (8, {}), {2}: (9, {}), {3}: (10, {}), {4... | custom-call | flops 6643777536 | bytes 51953672 | tf_op jit(solution)/shard_map/experts/pallas_call | solution.py:971
  387.9 9.8 %convolution_bitcast_fusion.2 = f32[1,768,2048]{2,1,0:T(8,128)} fusion(bf16[1408,768]{1,0:T(8,128)(2,1)S(1)} %get-tuple-element.451, bf16[1408,2048]{1,0:T(8,128)(2,1)} %get-tuple-element.452), kind=kOutput, calls=%fused_computation.2 | convolution fusion | flops 4429185024 | bytes 14221312 | tf_op jit(solution)/shard_map/dot_general | solution.py:1248
  406.5 7.2 %convolution_bitcast_fusion.1 = f32[1,2048,768]{2,1,0:T(8,128)} fusion(bf16[1408,2048]{1,0:T(8,128)(2,1)S(1)} %bitcast.113, bf16[1408,768]{1,0:T(8,128)(2,1)S(1)} %get-tuple-element.460), kind=kOutput, calls=%fused_computation.1 | convolution fusion | flops 4429185024 | bytes 14221312 | tf_op jit(solution)/shard_map/dot_general | solution.py:1248
  423.3 7.2 %convolution_bitcast_fusion = f32[1,2048,768]{2,1,0:T(8,128)} fusion(bf16[1408,2048]{1,0:T(8,128)(2,1)S(1)} %bitcast.113, bf16[1408,768]{1,0:T(8,128)(2,1)S(1)} %get-tuple-element.469), kind=kOutput, calls=%fused_computation | convolution fusion | flops 4429185024 | bytes 14221312 | tf_op jit(solution)/shard_map/dot_general | solution.py:1248
  440.5 7.0 %collective-permute-done.88.refs_1_ = bf16[128,2048]{1,0:T(8,128)(2,1)S(1)} collective-permute-done((bf16[128,2048]{1,0:T(8,128)(2,1)S(1)}, bf16[128,2048]{1,0:T(8,128)(2,1)S(1)}, u32[]{:S(2)}, u32[]{:S(2)}) %collective-permute-start.88) | collective-permute-done | bytes 524320 | tf_op jit(solution)/shard_map/ppermute | solution.py:347
  453.0 7.3 %collective-permute-done.93.refs_1_ = bf16[128,2048]{1,0:T(8,128)(2,1)S(1)} collective-permute-done((bf16[128,2048]{1,0:T(8,128)(2,1)S(1)}, bf16[128,2048]{1,0:T(8,128)(2,1)S(1)}, u32[]{:S(2)}, u32[]{:S(2)}) %collective-permute-start.93) | collective-permute-done | bytes 524320 | tf_op jit(solution)/shard_map/ppermute | solution.py:347
  473.7 9.9 %collective-permute-done.98.refs_5_ = bf16[128,2048]{1,0:T(8,128)(2,1)S(1)} collective-permute-done((bf16[128,2048]{1,0:T(8,128)(2,1)S(1)}, bf16[128,2048]{1,0:T(8,128)(2,1)S(1)}, u32[]{:S(2)}, u32[]{:S(2)}) %collective-permute-start.98) | collective-permute-done | bytes 524320 | tf_op jit(solution)/shard_map/ppermute | solution.py:335
  492.5 10.8 %collective-permute-done.99.refs_1_ = bf16[128,1024]{1,0:T(8,128)(2,1)S(1)} collective-permute-done((bf16[128,1024]{1,0:T(8,128)(2,1)S(1)}, bf16[128,1024]{1,0:T(8,128)(2,1)S(1)}, u32[]{:S(2)}, u32[]{:S(2)}) %collective-permute-start.99) | collective-permute-done | bytes 262176 | tf_op jit(solution)/shard_map/ppermute | solution.py:351
  506.8 14.5 %attention_backward.1 = (bf16[512,1280]{1,0:T(8,128)(2,1)S(1)}, f32[1,128]{1,0:T(1,128)S(1)}, f32[1,128]{1,0:T(1,128)S(1)}) custom-call(s32[1]{0:T(128)} %bitcast.16.core, f32[512,1280]{1,0:T(8,128)S(1)} %copy-done.9, bf16[512,1024]{1,0:T(8,128)(2,1)S(1)} %attended_grad.1.grad_attended, f32[256,128]{1,0:T(8,128)S(1)} %pad_maximum_fusion.1.cosine.refs_0_, ...), custom_call_target="tpu_custom_call" | custom-call | flops 1342177280 | bytes 5244932 | tf_op jit(solution)/shard_map/attention_backward/pallas_call | solution.py:971
  540.6 7.7 %normed_grad.1 = (bf16[256,2048]{1,0:T(8,128)(2,1)S(1)}, f32[256,2048]{1,0:T(8,128)S(1)}, f32[1,2048]{1,0:T(1,128)S(1)}) custom-call(s32[16]{0:T(128)S(1)} %copy-done.31, bf16[512,1280]{1,0:T(8,128)(2,1)S(1)} %get-tuple-element.537.right.grad_raw, f32[1,2048]{1,0:T(1,128)S(1)} %bitcast.98, bf16[128,2048]{1,0:T(8,128)(2,1)S(1)} %copy-done.23, ...), custom_call_target="tpu_custom_call" | custom-call | flops 2684354560 | bytes 12337216 | tf_op jit(solution)/shard_map/normed_grad/pallas_call | solution.py:971
  548.3 9.6 %collective-permute-done.114.refs_1_ = bf16[128,1408]{1,0:T(8,128)(2,1)S(1)} collective-permute-done((bf16[128,1408]{1,0:T(8,128)(2,1)S(1)}, bf16[128,1408]{1,0:T(8,128)(2,1)S(1)}, u32[]{:S(2)}, u32[]{:S(2)}) %collective-permute-start.114) | collective-permute-done | bytes 360480 | tf_op jit(solution)/shard_map/ppermute | solution.py:351
  562.9 6.6 %collective-permute-done.119 = bf16[128,1024]{1,0:T(8,128)(2,1)S(1)} collective-permute-done((bf16[128,1024]{1,0:T(8,128)(2,1)S(1)}, bf16[128,1024]{1,0:T(8,128)(2,1)S(1)}, u32[]{:S(2)}, u32[]{:S(2)}) %collective-permute-start.119) | collective-permute-done | bytes 262176 | tf_op jit(solution)/shard_map/ppermute | solution.py:351
  579.4 8.6 %collective-permute-done.120 = bf16[128,2048]{1,0:T(8,128)(2,1)S(1)} collective-permute-done((bf16[128,2048]{1,0:T(8,128)(2,1)S(1)}, bf16[128,2048]{1,0:T(8,128)(2,1)S(1)}, u32[]{:S(2)}, u32[]{:S(2)}) %collective-permute-start.120) | collective-permute-done | bytes 524320 | tf_op jit(solution)/shard_map/ppermute | solution.py:339
  603.0 6.0 collective-permute-done.125.refs_1_.refs_4_
  622.1 7.7 %collective-permute-done.129.refs_1_ = bf16[2,128,1408]{2,1,0:T(8,128)(2,1)S(1)} collective-permute-done((bf16[2,128,1408]{2,1,0:T(8,128)(2,1)S(1)}, bf16[2,128,1408]{2,1,0:T(8,128)(2,1)S(1)}, u32[]{:S(2)}, u32[]{:S(2)}) %collective-permute-start.129) | collective-permute-done | bytes 720928 | tf_op jit(solution)/shard_map/ppermute | solution.py:347
  (604 shorter events, 349.2 us)
Async XLA Ops:
  6.0 17.1 %collective-permute-start = (bf16[128,1408]{1,0:T(8,128)(2,1)}, bf16[128,1408]{1,0:T(8,128)(2,1)S(1)}, u32[]{:S(2)}, u32[]{:S(2)}) collective-permute-start(bf16[128,1408]{1,0:T(8,128)(2,1)} %concatenate.50), channel_id=1, source_target_pairs={{0,8},{2,10},{4,12},{6,14},{8,0},{10,2},{12,4},{14,6},{16,24},{18,... | collective-permute-start | bytes 1081352 | tf_op jit(solution)/shard_map/ppermute | solution.py:339
  12.1 18.0 %collective-permute-start.4 = (bf16[128,1408]{1,0:T(8,128)(2,1)S(1)}, bf16[128,1408]{1,0:T(8,128)(2,1)S(1)}, u32[]{:S(2)}, u32[]{:S(2)}) collective-permute-start(bf16[128,1408]{1,0:T(8,128)(2,1)S(1)} %concatenate.49.refs_4_), channel_id=1, source_target_pairs={{0,16},{2,18},{4,20},{6,22},{8,24},{10,26},{12,28},{14,30},{16,0},... | collective-permute-start | bytes 1081352 | tf_op jit(solution)/shard_map/ppermute | solution.py:343
  28.4 17.2 %collective-permute-start.3 = (bf16[128,1408]{1,0:T(8,128)(2,1)S(1)}, bf16[128,1408]{1,0:T(8,128)(2,1)S(1)}, u32[]{:S(2)}, u32[]{:S(2)}) collective-permute-start(bf16[128,1408]{1,0:T(8,128)(2,1)S(1)} %collective-permute-done.refs_8_), channel_id=1, source_target_pairs={{0,16},{2,18},{4,20},{6,22},{8,24},{10,26},{12,28},{14,30},{16,0},... | collective-permute-start | bytes 1081352 | tf_op jit(solution)/shard_map/ppermute | solution.py:343
  58.3 18.6 %collective-permute-start.11 = (bf16[128,2048]{1,0:T(8,128)(2,1)S(1)}, bf16[128,2048]{1,0:T(8,128)(2,1)S(1)}, u32[]{:S(2)}, u32[]{:S(2)}) collective-permute-start(bf16[128,2048]{1,0:T(8,128)(2,1)S(1)} %fusion.4.refs_0_), channel_id=1, source_target_pairs={{0,1},{1,0},{2,3},{3,2},{4,5},{5,4},{6,7},{7,6},{8,9},{9,8},{10,11... | collective-permute-start | bytes 1572872 | tf_op jit(solution)/shard_map/ppermute | solution.py:355
  58.4 18.6 %collective-permute-start.12 = (bf16[128,2048]{1,0:T(8,128)(2,1)S(1)}, bf16[128,2048]{1,0:T(8,128)(2,1)S(1)}, u32[]{:S(2)}, u32[]{:S(2)}) collective-permute-start(bf16[128,2048]{1,0:T(8,128)(2,1)S(1)} %fusion.4.refs_0_), channel_id=1, source_target_pairs={{0,8},{2,10},{4,12},{6,14},{8,0},{10,2},{12,4},{14,6},{16,24},{18,... | collective-permute-start | bytes 1572872 | tf_op jit(solution)/shard_map/ppermute | solution.py:339
  77.0 16.8 %collective-permute-start.16 = (bf16[128,2048]{1,0:T(8,128)(2,1)S(1)}, bf16[128,2048]{1,0:T(8,128)(2,1)S(1)}, u32[]{:S(2)}, u32[]{:S(2)}) collective-permute-start(bf16[128,2048]{1,0:T(8,128)(2,1)S(1)} %collective-permute-done.12.refs_2_), channel_id=1, source_target_pairs={{0,1},{1,0},{2,3},{3,2},{4,5},{5,4},{6,7},{7,6},{8,9},{9,8},{10,11... | collective-permute-start | bytes 1572872 | tf_op jit(solution)/shard_map/ppermute | solution.py:355
  77.0 16.7 %collective-permute-start.17 = (bf16[128,1408]{1,0:T(8,128)(2,1)}, bf16[128,1408]{1,0:T(8,128)(2,1)}, u32[]{:S(2)}, u32[]{:S(2)}) collective-permute-start(bf16[128,1408]{1,0:T(8,128)(2,1)} %collective-permute-done.13.refs_18_), channel_id=1, source_target_pairs={{0,2},{2,0},{4,6},{6,4},{8,10},{10,8},{12,14},{14,12},{16,18},{18,... | collective-permute-start | bytes 1081352 | tf_op jit(solution)/shard_map/ppermute | solution.py:351
  93.7 19.0 %collective-permute-start.21 = (bf16[1024,128]{1,0:T(8,128)(2,1)S(1)}, bf16[1024,128]{1,0:T(8,128)(2,1)}, u32[]{:S(2)}, u32[]{:S(2)}) collective-permute-start(bf16[1024,128]{1,0:T(8,128)(2,1)S(1)} %collective-permute-done.18.refs_1_.refs_5_), channel_id=1, source_target_pairs={{0,4},{2,6},{4,0},{6,2},{8,12},{10,14},{12,8},{14,10},{16,20},{18,... | collective-permute-start | bytes 786440 | tf_op jit(solution)/shard_map/ppermute | solution.py:347
  95.3 17.5 %collective-permute-start.22 = (bf16[1024,128]{1,0:T(8,128)(2,1)}, bf16[1024,128]{1,0:T(8,128)(2,1)}, u32[]{:S(2)}, u32[]{:S(2)}) collective-permute-start(bf16[1024,128]{1,0:T(8,128)(2,1)} %collective-permute-done.20.refs_4_.refs_8_), channel_id=1, source_target_pairs={{0,2},{2,0},{4,6},{6,4},{8,10},{10,8},{12,14},{14,12},{16,18},{18,... | collective-permute-start | bytes 786440 | tf_op jit(solution)/shard_map/ppermute | solution.py:351
  165.1 16.7 %collective-permute-start.38 = (bf16[128,2048]{1,0:T(8,128)(2,1)S(1)}, bf16[128,2048]{1,0:T(8,128)(2,1)S(1)}, u32[]{:S(2)}, u32[]{:S(2)}) collective-permute-start(bf16[128,2048]{1,0:T(8,128)(2,1)S(1)} %collective-permute-done.35.refs_4_), channel_id=1, source_target_pairs={{0,8},{2,10},{4,12},{6,14},{8,16},{10,18},{12,20},{14,22},{16,24},... | collective-permute-start | bytes 1572872 | tf_op jit(solution)/shard_map/ppermute | solution.py:335
  167.4 25.4 %collective-permute-start.34 = (bf16[128,2048]{1,0:T(8,128)(2,1)S(1)}, bf16[128,2048]{1,0:T(8,128)(2,1)S(1)}, u32[]{:S(2)}, u32[]{:S(2)}) collective-permute-start(bf16[128,2048]{1,0:T(8,128)(2,1)S(1)} %slice.180), channel_id=1, source_target_pairs={{0,8},{2,10},{4,12},{6,14},{8,0},{10,2},{12,4},{14,6},{16,24},{18,... | collective-permute-start | bytes 1572872 | tf_op jit(solution)/shard_map/ppermute | solution.py:339
  185.6 17.4 %collective-permute-start.43 = (bf16[128,2048]{1,0:T(8,128)(2,1)S(1)}, bf16[128,2048]{1,0:T(8,128)(2,1)}, u32[]{:S(2)}, u32[]{:S(2)}) collective-permute-start(bf16[128,2048]{1,0:T(8,128)(2,1)S(1)} %collective-permute-done.38.refs_4_), channel_id=1, source_target_pairs={{0,8},{2,10},{4,12},{6,14},{8,16},{10,18},{12,20},{14,22},{16,24},... | collective-permute-start | bytes 1572872 | tf_op jit(solution)/shard_map/ppermute | solution.py:335
  236.3 20.1 %collective-permute-start.51 = (bf16[128,2048]{1,0:T(8,128)(2,1)}, bf16[128,2048]{1,0:T(8,128)(2,1)S(1)}, u32[]{:S(2)}, u32[]{:S(2)}) collective-permute-start(bf16[128,2048]{1,0:T(8,128)(2,1)} %collective-permute-done.48.refs_0_), channel_id=1, source_target_pairs={{0,8},{2,10},{4,12},{6,14},{8,16},{10,18},{12,20},{14,22},{16,24},... | collective-permute-start | bytes 1572872 | tf_op jit(solution)/shard_map/ppermute | solution.py:335
  236.4 20.1 %collective-permute-start.52 = (bf16[128,2048]{1,0:T(8,128)(2,1)}, bf16[128,2048]{1,0:T(8,128)(2,1)S(1)}, u32[]{:S(2)}, u32[]{:S(2)}) collective-permute-start(bf16[128,2048]{1,0:T(8,128)(2,1)} %collective-permute-done.48.refs_0_), channel_id=1, source_target_pairs={{0,2},{2,0},{4,6},{6,4},{8,10},{10,8},{12,14},{14,12},{16,18},{18,... | collective-permute-start | bytes 1572872 | tf_op jit(solution)/shard_map/ppermute | solution.py:351
  236.9 19.5 %collective-permute-start.53 = (bf16[128,2048]{1,0:T(8,128)(2,1)}, bf16[128,2048]{1,0:T(8,128)(2,1)S(1)}, u32[]{:S(2)}, u32[]{:S(2)}) collective-permute-start(bf16[128,2048]{1,0:T(8,128)(2,1)} %collective-permute-done.46.refs_0_), channel_id=1, source_target_pairs={{0,4},{2,6},{4,0},{6,2},{8,12},{10,14},{12,8},{14,10},{16,20},{18,... | collective-permute-start | bytes 1572872 | tf_op jit(solution)/shard_map/ppermute | solution.py:347
  273.3 18.3 %collective-permute-start.59 = (bf16[128,2048]{1,0:T(8,128)(2,1)}, bf16[128,2048]{1,0:T(8,128)(2,1)S(1)}, u32[]{:S(2)}, u32[]{:S(2)}) collective-permute-start(bf16[128,2048]{1,0:T(8,128)(2,1)} %collective-permute-done.43.refs_4_), channel_id=1, source_target_pairs={{0,2},{2,0},{4,6},{6,4},{8,10},{10,8},{12,14},{14,12},{16,18},{18,... | collective-permute-start | bytes 1572872 | tf_op jit(solution)/shard_map/ppermute | solution.py:351
  273.8 17.8 %collective-permute-start.60 = (bf16[128,2048]{1,0:T(8,128)(2,1)S(1)}, bf16[128,2048]{1,0:T(8,128)(2,1)S(1)}, u32[]{:S(2)}, u32[]{:S(2)}) collective-permute-start(bf16[128,2048]{1,0:T(8,128)(2,1)S(1)} %copy-done.13), channel_id=1, source_target_pairs={{0,4},{2,6},{4,0},{6,2},{8,12},{10,14},{12,8},{14,10},{16,20},{18,... | collective-permute-start | bytes 1572872 | tf_op jit(solution)/shard_map/ppermute | solution.py:347
  484.1 19.4 %collective-permute-start.101 = (bf16[128,2048]{1,0:T(8,128)(2,1)S(1)}, bf16[128,2048]{1,0:T(8,128)(2,1)S(1)}, u32[]{:S(2)}, u32[]{:S(2)}) collective-permute-start(bf16[128,2048]{1,0:T(8,128)(2,1)S(1)} %get-tuple-element.507), channel_id=1, source_target_pairs={{0,2},{2,0},{4,6},{6,4},{8,10},{10,8},{12,14},{14,12},{16,18},{18,... | collective-permute-start | bytes 1572872 | tf_op jit(solution)/shard_map/ppermute | solution.py:351
  485.7 17.7 %collective-permute-start.102 = (bf16[128,2048]{1,0:T(8,128)(2,1)S(1)}, bf16[128,2048]{1,0:T(8,128)(2,1)S(1)}, u32[]{:S(2)}, u32[]{:S(2)}) collective-permute-start(bf16[128,2048]{1,0:T(8,128)(2,1)S(1)} %get-tuple-element.508), channel_id=1, source_target_pairs={{0,4},{2,6},{4,0},{6,2},{8,12},{10,14},{12,8},{14,10},{16,20},{18,... | collective-permute-start | bytes 1572872 | tf_op jit(solution)/shard_map/ppermute | solution.py:347
  486.3 17.2 %collective-permute-start.103 = (bf16[128,2048]{1,0:T(8,128)(2,1)S(1)}, bf16[128,2048]{1,0:T(8,128)(2,1)S(1)}, u32[]{:S(2)}, u32[]{:S(2)}) collective-permute-start(bf16[128,2048]{1,0:T(8,128)(2,1)S(1)} %get-tuple-element.509), channel_id=1, source_target_pairs={{0,8},{2,10},{4,12},{6,14},{8,16},{10,18},{12,20},{14,22},{16,24},... | collective-permute-start | bytes 1572872 | tf_op jit(solution)/shard_map/ppermute | solution.py:335
  486.3 17.0 %collective-permute-start.99 = (bf16[128,1024]{1,0:T(8,128)(2,1)S(1)}, bf16[128,1024]{1,0:T(8,128)(2,1)S(1)}, u32[]{:S(2)}, u32[]{:S(2)}) collective-permute-start(bf16[128,1024]{1,0:T(8,128)(2,1)S(1)} %get-tuple-element.502), channel_id=1, source_target_pairs={{0,2},{2,0},{4,6},{6,4},{8,10},{10,8},{12,14},{14,12},{16,18},{18,... | collective-permute-start | bytes 786440 | tf_op jit(solution)/shard_map/ppermute | solution.py:351
  503.5 19.3 %collective-permute-start.104 = (bf16[2,128,1024]{2,1,0:T(8,128)(2,1)S(1)}, bf16[2,128,1024]{2,1,0:T(8,128)(2,1)S(1)}, u32[]{:S(2)}, u32[]{:S(2)}) collective-permute-start(bf16[2,128,1024]{2,1,0:T(8,128)(2,1)S(1)} %sums.22), channel_id=1, source_target_pairs={{0,4},{2,6},{4,0},{6,2},{8,12},{10,14},{12,8},{14,10},{16,20},{18,... | collective-permute-start | bytes 1572872 | tf_op jit(solution)/shard_map/ppermute | solution.py:347
  504.7 18.3 %collective-permute-start.106 = (bf16[128,2048]{1,0:T(8,128)(2,1)S(1)}, bf16[128,2048]{1,0:T(8,128)(2,1)S(1)}, u32[]{:S(2)}, u32[]{:S(2)}) collective-permute-start(bf16[128,2048]{1,0:T(8,128)(2,1)S(1)} %copy-done.51), channel_id=1, source_target_pairs={{0,2},{2,0},{4,6},{6,4},{8,10},{10,8},{12,14},{14,12},{16,18},{18,... | collective-permute-start | bytes 1572872 | tf_op jit(solution)/shard_map/ppermute | solution.py:351
  505.7 17.0 %collective-permute-start.105 = (bf16[128,1024]{1,0:T(8,128)(2,1)S(1)}, bf16[128,1024]{1,0:T(8,128)(2,1)S(1)}, u32[]{:S(2)}, u32[]{:S(2)}) collective-permute-start(bf16[128,1024]{1,0:T(8,128)(2,1)S(1)} %get-tuple-element.511), channel_id=1, source_target_pairs={{0,2},{2,0},{4,6},{6,4},{8,10},{10,8},{12,14},{14,12},{16,18},{18,... | collective-permute-start | bytes 786440 | tf_op jit(solution)/shard_map/ppermute | solution.py:351
  537.3 20.5 %collective-permute-start.111 = (bf16[128,2048]{1,0:T(8,128)(2,1)S(1)}, bf16[128,2048]{1,0:T(8,128)(2,1)S(1)}, u32[]{:S(2)}, u32[]{:S(2)}) collective-permute-start(bf16[128,2048]{1,0:T(8,128)(2,1)S(1)} %copy-done.49), channel_id=1, source_target_pairs={{0,2},{2,0},{4,6},{6,4},{8,10},{10,8},{12,14},{14,12},{16,18},{18,... | collective-permute-start | bytes 1572872 | tf_op jit(solution)/shard_map/ppermute | solution.py:351
  537.8 20.1 %collective-permute-start.112 = (bf16[128,2048]{1,0:T(8,128)(2,1)S(1)}, bf16[128,2048]{1,0:T(8,128)(2,1)S(1)}, u32[]{:S(2)}, u32[]{:S(2)}) collective-permute-start(bf16[128,2048]{1,0:T(8,128)(2,1)S(1)} %get-tuple-element.534), channel_id=1, source_target_pairs={{0,4},{2,6},{4,0},{6,2},{8,12},{10,14},{12,8},{14,10},{16,20},{18,... | collective-permute-start | bytes 1572872 | tf_op jit(solution)/shard_map/ppermute | solution.py:347
  539.0 18.9 %collective-permute-start.113 = (bf16[128,2048]{1,0:T(8,128)(2,1)S(1)}, bf16[128,2048]{1,0:T(8,128)(2,1)S(1)}, u32[]{:S(2)}, u32[]{:S(2)}) collective-permute-start(bf16[128,2048]{1,0:T(8,128)(2,1)S(1)} %get-tuple-element.535), channel_id=1, source_target_pairs={{0,8},{2,10},{4,12},{6,14},{8,16},{10,18},{12,20},{14,22},{16,24},... | collective-permute-start | bytes 1572872 | tf_op jit(solution)/shard_map/ppermute | solution.py:335
  539.2 18.7 %collective-permute-start.114 = (bf16[128,1408]{1,0:T(8,128)(2,1)S(1)}, bf16[128,1408]{1,0:T(8,128)(2,1)S(1)}, u32[]{:S(2)}, u32[]{:S(2)}) collective-permute-start(bf16[128,1408]{1,0:T(8,128)(2,1)S(1)} %get-tuple-element.536), channel_id=1, source_target_pairs={{0,2},{2,0},{4,6},{6,4},{8,10},{10,8},{12,14},{14,12},{16,18},{18,... | collective-permute-start | bytes 1081352 | tf_op jit(solution)/shard_map/ppermute | solution.py:351
  574.9 17.3 %collective-permute-start.122 = (bf16[2,128,1408]{2,1,0:T(8,128)(2,1)S(1)}, bf16[2,128,1408]{2,1,0:T(8,128)(2,1)S(1)}, u32[]{:S(2)}, u32[]{:S(2)}) collective-permute-start(bf16[2,128,1408]{2,1,0:T(8,128)(2,1)S(1)} %sums.26), channel_id=1, source_target_pairs={{0,4},{2,6},{4,0},{6,2},{8,12},{10,14},{12,8},{14,10},{16,20},{18,... | collective-permute-start | bytes 2162696 | tf_op jit(solution)/shard_map/ppermute | solution.py:347
  595.1 17.6 %collective-permute-start.127 = (bf16[128,1408]{1,0:T(8,128)(2,1)S(1)}, bf16[128,1408]{1,0:T(8,128)(2,1)S(1)}, u32[]{:S(2)}, u32[]{:S(2)}) collective-permute-start(bf16[128,1408]{1,0:T(8,128)(2,1)S(1)} %get-tuple-element.575), channel_id=1, source_target_pairs={{0,16},{2,18},{4,20},{6,22},{8,24},{10,26},{12,28},{14,30},{16,0},... | collective-permute-start | bytes 1081352 | tf_op jit(solution)/shard_map/ppermute | solution.py:343
  612.6 17.1 %collective-permute-start.129 = (bf16[2,128,1408]{2,1,0:T(8,128)(2,1)S(1)}, bf16[2,128,1408]{2,1,0:T(8,128)(2,1)S(1)}, u32[]{:S(2)}, u32[]{:S(2)}) collective-permute-start(bf16[2,128,1408]{2,1,0:T(8,128)(2,1)S(1)} %get-tuple-element.578), channel_id=1, source_target_pairs={{0,4},{2,6},{4,0},{6,2},{8,12},{10,14},{12,8},{14,10},{16,20},{18,... | collective-permute-start | bytes 2162696 | tf_op jit(solution)/shard_map/ppermute | solution.py:347
  614.3 17.2 %collective-permute-start.131 = (bf16[128,1408]{1,0:T(8,128)(2,1)S(1)}, bf16[128,1408]{1,0:T(8,128)(2,1)S(1)}, u32[]{:S(2)}, u32[]{:S(2)}) collective-permute-start(bf16[128,1408]{1,0:T(8,128)(2,1)S(1)} %get-tuple-element.587), channel_id=1, source_target_pairs={{0,16},{2,18},{4,20},{6,22},{8,24},{10,26},{12,28},{14,30},{16,0},... | collective-permute-start | bytes 1081352 | tf_op jit(solution)/shard_map/ppermute | solution.py:343
  (231 other events, 3343.4 us)

commit v5 on v4

--- a/solution.py
+++ b/solution.py
@@ -631,6 +631,23 @@
     return raised / jnp.sum(raised, axis=-1, keepdims=True)
 
 
+def first_blocks_kernel(odd, routes, query, key, value, router, mine, theirs, rest):
+    count = router.shape[1]
+    columns = lax.broadcasted_iota(jnp.int32, rest.shape, 1)
+    named = columns == routes[:, :1] + count
+    for j in range(1, routes.shape[1]):
+        named = jnp.logical_or(named, columns == routes[:, j : j + 1] + count)
+    rest[...] = jnp.where(named, 1.0, 0.0)
+    rest[:, :count] = router[...].astype(wide)
+    for out, side in ((mine, odd[0]), (theirs, 1 - odd[0])):
+        first = 0
+        for weight in (query, key, value):
+            size = weight.shape[1] // 2
+            out[:, first : first + size] = weight[:, lanes(side * size, size)]
+            first += size
+        out[:, first:] = rest[...].astype(low)
+
+
 def raw_kernel(ids, block_ids, *refs):
     seq_blocks, blocks = refs[:4], refs[4:20]
     raw, router, rest, whole, seq, sems = refs[20:]
@@ -1041,14 +1058,15 @@
     chain = Chain()
     numbers = jnp.arange(expert_count, dtype=jnp.int32)
     own_named = jnp.any(routes[:, :, None] == numbers, axis=1)
-    splits = [halves(w, 1) for w in (query_weight, key_weight, value_weight)]
-    rest = [
-        router_weight,
-        own_named.astype(low),
-        jnp.zeros((tok_rows, 128 - 2 * expert_count), low),
-    ]
-    mine = jnp.concatenate([s[0] for s in splits] + rest, axis=1)
-    theirs = jnp.concatenate([s[1] for s in splits] + rest, axis=1)
+    mine, theirs = call(
+        first_blocks_kernel,
+        "first_blocks",
+        [((z % 2).astype(jnp.int32)[None], SMEM)]
+        + [(a, VMEM) for a in (routes, query_weight, key_weight, value_weight, router_weight)],
+        [shape(tok_rows, raw_cols + 128, low)] * 2,
+        [pltpu.VMEM((tok_rows, 128), wide)],
+        0,
+    )
     held = {(0, 0, 0): mine}
     (held[1, 0, 0],) = chain.gather([(held, WEIGHT_ROUNDS[0])], [(theirs, z_pair)])
     inputs_float = inputs.astype(wide)

time: 662 us -> 661 us (level)
    ppermute x10, waiting for transfers between devices: 17.3 us -> 26 us  [z_far(): return lax.ppermute(block, 'dp', Z_FAR)]
    ppermute x41, waiting for transfers between devices: 77.2 us -> 69.2 us  [y_swap(): return lax.ppermute(block, 'dp', Y_PAIR)]
    unnamed x251 -> x242, local copies, waits for them, and re-layouts: 19.1 us -> 22.6 us
    pallas_call x21 -> x22, Pallas kernels: 137 us -> 137 us  [call(): pl.pallas_call(kernel, out_shape=outs, in_specs=[spec for _, spec in ins]...]
  transfers between devices with their start and end apart: 138 -> 138, of which waited for: 80 -> 78; matrix products, arithmetic and copies ran while one was open for 6% -> 6% of each run, Pallas kernels for 20% -> 20%
where the time goes in v5:
time: 661 us; the launch traced here: 653 us
  waiting for transfers between devices  325 us (49%)
  Pallas kernels  142 us (21%)
  starting transfers between devices  116 us (18%)
  local copies, waits for them, and re-layouts  26.6 us (4%)
  matrix products  25.9 us (4%)
  other arithmetic  14.6 us (2%)
    pallas_call x22, Pallas kernels, call(): pl.pallas_call(kernel, out_shape=outs, in_specs=[spec for _, spec in ins]...  137 us
    ppermute x43, waiting for transfers between devices, x_swap(): return lax.ppermute(block, 'dp', X_PAIR)  104 us
    ppermute x19, waiting for transfers between devices, z_next(): return lax.ppermute(block, 'dp', Z_RING)  83.8 us
    ppermute x41, waiting for transfers between devices, y_swap(): return lax.ppermute(block, 'dp', Y_PAIR)  69.2 us
    ppermute x43, starting transfers between devices, x_swap(): return lax.ppermute(block, 'dp', X_PAIR)  47.5 us
    ppermute x41, starting transfers between devices, y_swap(): return lax.ppermute(block, 'dp', Y_PAIR)  43.2 us
    ppermute x9, waiting for transfers between devices, z_pair(): return lax.ppermute(block, 'dp', Z_PAIR)  28.8 us
    ppermute x10, waiting for transfers between devices, z_far(): return lax.ppermute(block, 'dp', Z_FAR)  26 us
  transfers between devices with their start and end apart: 138, of which 78 were waited for; matrix products, arithmetic and copies ran while one was open for 6% of the time, Pallas kernels for 20%

profile of v5, /device:TPU:0, one launch (start us, length us, event | category | flops | bytes accessed | tf_op | source)
XLA Modules:
  0.0 652.8 jit_solution(15224903143883641537)
XLA Ops:
  27.8 9.5 %collective-permute-done.4.refs_12_ = bf16[128,1408]{1,0:T(8,128)(2,1)S(1)} collective-permute-done((bf16[128,1408]{1,0:T(8,128)(2,1)S(1)}, bf16[128,1408]{1,0:T(8,128)(2,1)S(1)}, u32[]{:S(2)}, u32[]{:S(2)}) %collective-permute-start.4) | collective-permute-done | bytes 360480 | tf_op jit(solution)/shard_map/ppermute | solution.py:343
  44.8 7.0 %collective-permute-done.10.refs_11_ = bf16[128,1408]{1,0:T(8,128)(2,1)S(1)} collective-permute-done((bf16[128,1408]{1,0:T(8,128)(2,1)S(1)}, bf16[128,1408]{1,0:T(8,128)(2,1)S(1)}, u32[]{:S(2)}, u32[]{:S(2)}) %collective-permute-start.10) | collective-permute-done | bytes 360480 | tf_op jit(solution)/shard_map/ppermute | solution.py:351
  69.5 6.5 %collective-permute-done.15.refs_15_ = bf16[128,1408]{1,0:T(8,128)(2,1)} collective-permute-done((bf16[128,1408]{1,0:T(8,128)(2,1)}, bf16[128,1408]{1,0:T(8,128)(2,1)}, u32[]{:S(2)}, u32[]{:S(2)}) %collective-permute-start.15) | collective-permute-done | bytes 360480 | tf_op jit(solution)/shard_map/ppermute | solution.py:347
  81.4 11.5 %collective-permute-done.18.refs_1_.refs_5_ = bf16[1024,128]{1,0:T(8,128)(2,1)} collective-permute-done((bf16[1024,128]{1,0:T(8,128)(2,1)S(1)}, bf16[1024,128]{1,0:T(8,128)(2,1)}, u32[]{:S(2)}, u32[]{:S(2)}) %collective-permute-start.18) | collective-permute-done | bytes 262176 | tf_op jit(solution)/shard_map/ppermute | solution.py:351
  102.1 9.8 %attention_raw.1 = (f32[512,1280]{1,0:T(8,128)}, bf16[2048,128]{1,0:T(8,128)(2,1)}, bf16[2048,128]{1,0:T(8,128)(2,1)}) custom-call(s32[16]{0:T(128)} %stack.127.ids, s32[16]{0:T(128)} %stack.144.block_ids, bf16[128,2048]{1,0:T(8,128)(2,1)} %copy-done.23, bf16[128,2048]{1,0:T(8,128)(2,1)} %copy-done.43, bf16[128,2048]{1,0:T(8,128)(2,1)} %copy-done.45, ...), custom_call_target="tpu_custom_call" | custom-call | flops 2684354560 | bytes 11534464 | tf_op jit(solution)/shard_map/attention_raw/pallas_call | solution.py:988
  117.7 9.4 %attention_forward.1.attended.right = bf16[512,1024]{1,0:T(8,128)(2,1)S(1)} custom-call(s32[1]{0:T(128)} %bitcast.16.core, f32[512,1280]{1,0:T(8,128)S(1)} %copy-done.8, f32[256,128]{1,0:T(8,128)S(1)} %pad_maximum_fusion.1.cosine.refs_0_, f32[256,128]{1,0:T(8,128)S(1)} %pad_maximum_fusion.2.sine.refs_1_, f32[1,128]{1,0:T(1,128)S(1)} %bitcast.109, ...), custom_call_target="tpu_custom_call" | custom-call | flops 536870912 | bytes 3933188 | tf_op jit(solution)/shard_map/attention_forward/pallas_call | solution.py:988
  151.1 13.0 %collective-permute-done.35.refs_4_ = bf16[128,2048]{1,0:T(8,128)(2,1)S(1)} collective-permute-done((bf16[128,2048]{1,0:T(8,128)(2,1)S(1)}, bf16[128,2048]{1,0:T(8,128)(2,1)S(1)}, u32[]{:S(2)}, u32[]{:S(2)}) %collective-permute-start.35) | collective-permute-done | bytes 524320 | tf_op jit(solution)/shard_map/ppermute | solution.py:335
  167.8 13.0 %collective-permute-done.38.refs_4_ = bf16[128,2048]{1,0:T(8,128)(2,1)S(1)} collective-permute-done((bf16[128,2048]{1,0:T(8,128)(2,1)S(1)}, bf16[128,2048]{1,0:T(8,128)(2,1)S(1)}, u32[]{:S(2)}, u32[]{:S(2)}) %collective-permute-start.38) | collective-permute-done | bytes 524320 | tf_op jit(solution)/shard_map/ppermute | solution.py:335
  184.6 7.1 %collective-permute-done.34 = bf16[128,2048]{1,0:T(8,128)(2,1)S(1)} collective-permute-done((bf16[128,2048]{1,0:T(8,128)(2,1)S(1)}, bf16[128,2048]{1,0:T(8,128)(2,1)S(1)}, u32[]{:S(2)}, u32[]{:S(2)}) %collective-permute-start.34) | collective-permute-done | bytes 524320 | tf_op jit(solution)/shard_map/ppermute | solution.py:339
  195.7 6.3 collective-permute-done.43.refs_4_
  204.1 10.6 %collective-permute-done.44.refs_1_ = bf16[128,2048]{1,0:T(8,128)(2,1)} collective-permute-done((bf16[128,2048]{1,0:T(8,128)(2,1)S(1)}, bf16[128,2048]{1,0:T(8,128)(2,1)}, u32[]{:S(2)}, u32[]{:S(2)}) %collective-permute-start.44) | collective-permute-done | bytes 524320 | tf_op jit(solution)/shard_map/ppermute | solution.py:351
  243.9 11.4 %experts.4 = (bf16[1408,2048]{1,0:T(8,128)(2,1)}, bf16[1408,768]{1,0:T(8,128)(2,1)S(1)}, bf16[1408,2048]{1,0:T(8,128)(2,1)}, bf16[1408,768]{1,0:T(8,128)(2,1)S(1...) custom-call(s32[2]{0:T(128)S(1)} %pad_add_fusion.experts, ...), custom_call_target="tpu_custom_call" | custom-call | flops 6643777536 | bytes 33931272 | tf_op jit(solution)/shard_map/experts/pallas_call | solution.py:988
  257.6 14.2 %collective-permute-done.55.refs_3_ = bf16[128,2048]{1,0:T(8,128)(2,1)S(1)} collective-permute-done((bf16[128,2048]{1,0:T(8,128)(2,1)}, bf16[128,2048]{1,0:T(8,128)(2,1)S(1)}, u32[]{:S(2)}, u32[]{:S(2)}) %collective-permute-start.55) | collective-permute-done | bytes 524320 | tf_op jit(solution)/shard_map/ppermute | solution.py:335
  278.9 8.6 %collective-permute-done.58.refs_7_ = bf16[128,2048]{1,0:T(8,128)(2,1)S(1)} collective-permute-done((bf16[128,2048]{1,0:T(8,128)(2,1)S(1)}, bf16[128,2048]{1,0:T(8,128)(2,1)S(1)}, u32[]{:S(2)}, u32[]{:S(2)}) %collective-permute-start.58) | collective-permute-done | bytes 524320 | tf_op jit(solution)/shard_map/ppermute | solution.py:335
  294.0 11.5 %experts.5 = (bf16[1408,2048]{1,0:T(8,128)(2,1)}, bf16[1408,768]{1,0:T(8,128)(2,1)S(1)}, bf16[1408,2048]{1,0:T(8,128)(2,1)}, bf16[1408,768]{1,0:T(8,128)(2,1)S(1...) custom-call(s32[2]{0:T(128)S(1)} %pad_add_fusion.experts, ...), custom_call_target="tpu_custom_call", output_to_operand_aliasing={{0}: (7, {}), {1}: (8, {}), {2}: (9, {}), {3}: (10, {}), {4... | custom-call | flops 6643777536 | bytes 51953672 | tf_op jit(solution)/shard_map/experts/pallas_call | solution.py:988
  310.5 10.6 %collective-permute-done.65.refs_7_ = bf16[128,2048]{1,0:T(8,128)(2,1)S(1)} collective-permute-done((bf16[128,2048]{1,0:T(8,128)(2,1)S(1)}, bf16[128,2048]{1,0:T(8,128)(2,1)S(1)}, u32[]{:S(2)}, u32[]{:S(2)}) %collective-permute-start.65) | collective-permute-done | bytes 524320 | tf_op jit(solution)/shard_map/ppermute | solution.py:351
  336.0 11.5 %experts.6 = (bf16[1408,2048]{1,0:T(8,128)(2,1)}, bf16[1408,768]{1,0:T(8,128)(2,1)S(1)}, bf16[1408,2048]{1,0:T(8,128)(2,1)}, bf16[1408,768]{1,0:T(8,128)(2,1)S(1...) custom-call(s32[2]{0:T(128)S(1)} %pad_add_fusion.experts, ...), custom_call_target="tpu_custom_call", output_to_operand_aliasing={{0}: (7, {}), {1}: (8, {}), {2}: (9, {}), {3}: (10, {}), {4... | custom-call | flops 6643777536 | bytes 51953672 | tf_op jit(solution)/shard_map/experts/pallas_call | solution.py:988
  361.6 11.5 %experts.7 = (bf16[1408,2048]{1,0:T(8,128)(2,1)}, bf16[1408,768]{1,0:T(8,128)(2,1)S(1)}, bf16[1408,2048]{1,0:T(8,128)(2,1)}, bf16[1408,768]{1,0:T(8,128)(2,1)S(1...) custom-call(s32[2]{0:T(128)S(1)} %pad_add_fusion.experts, ...), custom_call_target="tpu_custom_call", output_to_operand_aliasing={{0}: (7, {}), {1}: (8, {}), {2}: (9, {}), {3}: (10, {}), {4... | custom-call | flops 6643777536 | bytes 51953672 | tf_op jit(solution)/shard_map/experts/pallas_call | solution.py:988
  386.9 9.8 %convolution_bitcast_fusion.2 = f32[1,768,2048]{2,1,0:T(8,128)} fusion(bf16[1408,768]{1,0:T(8,128)(2,1)S(1)} %get-tuple-element.455, bf16[1408,2048]{1,0:T(8,128)(2,1)} %get-tuple-element.456), kind=kOutput, calls=%fused_computation.2 | convolution fusion | flops 4429185024 | bytes 14221312 | tf_op jit(solution)/shard_map/dot_general | solution.py:1266
  405.4 7.2 %convolution_bitcast_fusion.1 = f32[1,2048,768]{2,1,0:T(8,128)} fusion(bf16[1408,2048]{1,0:T(8,128)(2,1)S(1)} %bitcast.114, bf16[1408,768]{1,0:T(8,128)(2,1)S(1)} %get-tuple-element.464), kind=kOutput, calls=%fused_computation.1 | convolution fusion | flops 4429185024 | bytes 14221312 | tf_op jit(solution)/shard_map/dot_general | solution.py:1266
  422.4 7.2 %convolution_bitcast_fusion = f32[1,2048,768]{2,1,0:T(8,128)} fusion(bf16[1408,2048]{1,0:T(8,128)(2,1)S(1)} %bitcast.114, bf16[1408,768]{1,0:T(8,128)(2,1)S(1)} %get-tuple-element.473), kind=kOutput, calls=%fused_computation | convolution fusion | flops 4429185024 | bytes 14221312 | tf_op jit(solution)/shard_map/dot_general | solution.py:1266
  439.5 7.0 %collective-permute-done.88.refs_1_ = bf16[128,2048]{1,0:T(8,128)(2,1)S(1)} collective-permute-done((bf16[128,2048]{1,0:T(8,128)(2,1)S(1)}, bf16[128,2048]{1,0:T(8,128)(2,1)S(1)}, u32[]{:S(2)}, u32[]{:S(2)}) %collective-permute-start.88) | collective-permute-done | bytes 524320 | tf_op jit(solution)/shard_map/ppermute | solution.py:347
  452.0 7.2 %collective-permute-done.93.refs_1_ = bf16[128,2048]{1,0:T(8,128)(2,1)S(1)} collective-permute-done((bf16[128,2048]{1,0:T(8,128)(2,1)S(1)}, bf16[128,2048]{1,0:T(8,128)(2,1)S(1)}, u32[]{:S(2)}, u32[]{:S(2)}) %collective-permute-start.93) | collective-permute-done | bytes 524320 | tf_op jit(solution)/shard_map/ppermute | solution.py:347
  472.6 10.0 %collective-permute-done.98.refs_5_ = bf16[128,2048]{1,0:T(8,128)(2,1)S(1)} collective-permute-done((bf16[128,2048]{1,0:T(8,128)(2,1)S(1)}, bf16[128,2048]{1,0:T(8,128)(2,1)S(1)}, u32[]{:S(2)}, u32[]{:S(2)}) %collective-permute-start.98) | collective-permute-done | bytes 524320 | tf_op jit(solution)/shard_map/ppermute | solution.py:335
  491.5 10.9 %collective-permute-done.99.refs_1_ = bf16[128,1024]{1,0:T(8,128)(2,1)S(1)} collective-permute-done((bf16[128,1024]{1,0:T(8,128)(2,1)S(1)}, bf16[128,1024]{1,0:T(8,128)(2,1)S(1)}, u32[]{:S(2)}, u32[]{:S(2)}) %collective-permute-start.99) | collective-permute-done | bytes 262176 | tf_op jit(solution)/shard_map/ppermute | solution.py:351
  505.7 14.5 %attention_backward.1 = (bf16[512,1280]{1,0:T(8,128)(2,1)S(1)}, f32[1,128]{1,0:T(1,128)S(1)}, f32[1,128]{1,0:T(1,128)S(1)}) custom-call(s32[1]{0:T(128)} %bitcast.16.core, f32[512,1280]{1,0:T(8,128)S(1)} %copy-done.9, bf16[512,1024]{1,0:T(8,128)(2,1)S(1)} %attended_grad.1.grad_attended, f32[256,128]{1,0:T(8,128)S(1)} %pad_maximum_fusion.1.cosine.refs_0_, ...), custom_call_target="tpu_custom_call" | custom-call | flops 1342177280 | bytes 5244932 | tf_op jit(solution)/shard_map/attention_backward/pallas_call | solution.py:988
  539.5 7.3 %normed_grad.1 = (bf16[256,2048]{1,0:T(8,128)(2,1)S(1)}, f32[256,2048]{1,0:T(8,128)S(1)}, f32[1,2048]{1,0:T(1,128)S(1)}) custom-call(s32[16]{0:T(128)S(1)} %copy-done.32, bf16[512,1280]{1,0:T(8,128)(2,1)S(1)} %get-tuple-element.541.right.grad_raw, f32[1,2048]{1,0:T(1,128)S(1)} %bitcast.99, bf16[128,2048]{1,0:T(8,128)(2,1)S(1)} %copy-done.24, ...), custom_call_target="tpu_custom_call" | custom-call | flops 2684354560 | bytes 12337216 | tf_op jit(solution)/shard_map/normed_grad/pallas_call | solution.py:988
  546.9 9.9 %collective-permute-done.114.refs_1_ = bf16[128,1408]{1,0:T(8,128)(2,1)S(1)} collective-permute-done((bf16[128,1408]{1,0:T(8,128)(2,1)S(1)}, bf16[128,1408]{1,0:T(8,128)(2,1)S(1)}, u32[]{:S(2)}, u32[]{:S(2)}) %collective-permute-start.114) | collective-permute-done | bytes 360480 | tf_op jit(solution)/shard_map/ppermute | solution.py:351
  561.9 6.6 %collective-permute-done.119 = bf16[128,1024]{1,0:T(8,128)(2,1)S(1)} collective-permute-done((bf16[128,1024]{1,0:T(8,128)(2,1)S(1)}, bf16[128,1024]{1,0:T(8,128)(2,1)S(1)}, u32[]{:S(2)}, u32[]{:S(2)}) %collective-permute-start.119) | collective-permute-done | bytes 262176 | tf_op jit(solution)/shard_map/ppermute | solution.py:351
  578.4 8.5 %collective-permute-done.120 = bf16[128,2048]{1,0:T(8,128)(2,1)S(1)} collective-permute-done((bf16[128,2048]{1,0:T(8,128)(2,1)S(1)}, bf16[128,2048]{1,0:T(8,128)(2,1)S(1)}, u32[]{:S(2)}, u32[]{:S(2)}) %collective-permute-start.120) | collective-permute-done | bytes 524320 | tf_op jit(solution)/shard_map/ppermute | solution.py:339
  602.0 6.0 collective-permute-done.125.refs_1_.refs_4_
  621.1 7.7 %collective-permute-done.129.refs_1_ = bf16[2,128,1408]{2,1,0:T(8,128)(2,1)S(1)} collective-permute-done((bf16[2,128,1408]{2,1,0:T(8,128)(2,1)S(1)}, bf16[2,128,1408]{2,1,0:T(8,128)(2,1)S(1)}, u32[]{:S(2)}, u32[]{:S(2)}) %collective-permute-start.129) | collective-permute-done | bytes 720928 | tf_op jit(solution)/shard_map/ppermute | solution.py:347
  (589 shorter events, 346.9 us)
Async XLA Ops:
  5.3 16.7 %collective-permute-start = (bf16[128,1408]{1,0:T(8,128)(2,1)S(1)}, bf16[128,1408]{1,0:T(8,128)(2,1)S(1)}, u32[]{:S(2)}, u32[]{:S(2)}) collective-permute-start(bf16[128,1408]{1,0:T(8,128)(2,1)S(1)} %get-tuple-element.308), channel_id=1, source_target_pairs={{0,8},{2,10},{4,12},{6,14},{8,0},{10,2},{12,4},{14,6},{16,24},{18,... | collective-permute-start | bytes 1081352 | tf_op jit(solution)/shard_map/ppermute | solution.py:339
  11.4 25.9 %collective-permute-start.4 = (bf16[128,1408]{1,0:T(8,128)(2,1)S(1)}, bf16[128,1408]{1,0:T(8,128)(2,1)S(1)}, u32[]{:S(2)}, u32[]{:S(2)}) collective-permute-start(bf16[128,1408]{1,0:T(8,128)(2,1)S(1)} %get-tuple-element.312.refs_4_), channel_id=1, source_target_pairs={{0,16},{2,18},{4,20},{6,22},{8,24},{10,26},{12,28},{14,30},{16,0},... | collective-permute-start | bytes 1081352 | tf_op jit(solution)/shard_map/ppermute | solution.py:343
  27.2 17.6 %collective-permute-start.3 = (bf16[128,1408]{1,0:T(8,128)(2,1)S(1)}, bf16[128,1408]{1,0:T(8,128)(2,1)S(1)}, u32[]{:S(2)}, u32[]{:S(2)}) collective-permute-start(bf16[128,1408]{1,0:T(8,128)(2,1)S(1)} %collective-permute-done.refs_8_), channel_id=1, source_target_pairs={{0,16},{2,18},{4,20},{6,22},{8,24},{10,26},{12,28},{14,30},{16,0},... | collective-permute-start | bytes 1081352 | tf_op jit(solution)/shard_map/ppermute | solution.py:343
  57.2 18.8 %collective-permute-start.11 = (bf16[128,2048]{1,0:T(8,128)(2,1)S(1)}, bf16[128,2048]{1,0:T(8,128)(2,1)S(1)}, u32[]{:S(2)}, u32[]{:S(2)}) collective-permute-start(bf16[128,2048]{1,0:T(8,128)(2,1)S(1)} %fusion.4.refs_0_), channel_id=1, source_target_pairs={{0,1},{1,0},{2,3},{3,2},{4,5},{5,4},{6,7},{7,6},{8,9},{9,8},{10,11... | collective-permute-start | bytes 1572872 | tf_op jit(solution)/shard_map/ppermute | solution.py:355
  57.3 18.7 %collective-permute-start.12 = (bf16[128,2048]{1,0:T(8,128)(2,1)S(1)}, bf16[128,2048]{1,0:T(8,128)(2,1)S(1)}, u32[]{:S(2)}, u32[]{:S(2)}) collective-permute-start(bf16[128,2048]{1,0:T(8,128)(2,1)S(1)} %fusion.4.refs_0_), channel_id=1, source_target_pairs={{0,8},{2,10},{4,12},{6,14},{8,0},{10,2},{12,4},{14,6},{16,24},{18,... | collective-permute-start | bytes 1572872 | tf_op jit(solution)/shard_map/ppermute | solution.py:339
  76.0 16.9 %collective-permute-start.16 = (bf16[128,2048]{1,0:T(8,128)(2,1)S(1)}, bf16[128,2048]{1,0:T(8,128)(2,1)S(1)}, u32[]{:S(2)}, u32[]{:S(2)}) collective-permute-start(bf16[128,2048]{1,0:T(8,128)(2,1)S(1)} %collective-permute-done.12.refs_2_), channel_id=1, source_target_pairs={{0,1},{1,0},{2,3},{3,2},{4,5},{5,4},{6,7},{7,6},{8,9},{9,8},{10,11... | collective-permute-start | bytes 1572872 | tf_op jit(solution)/shard_map/ppermute | solution.py:355
  76.1 16.8 %collective-permute-start.17 = (bf16[128,1408]{1,0:T(8,128)(2,1)}, bf16[128,1408]{1,0:T(8,128)(2,1)}, u32[]{:S(2)}, u32[]{:S(2)}) collective-permute-start(bf16[128,1408]{1,0:T(8,128)(2,1)} %collective-permute-done.13.refs_18_), channel_id=1, source_target_pairs={{0,2},{2,0},{4,6},{6,4},{8,10},{10,8},{12,14},{14,12},{16,18},{18,... | collective-permute-start | bytes 1081352 | tf_op jit(solution)/shard_map/ppermute | solution.py:351
  92.9 19.0 %collective-permute-start.21 = (bf16[1024,128]{1,0:T(8,128)(2,1)}, bf16[1024,128]{1,0:T(8,128)(2,1)}, u32[]{:S(2)}, u32[]{:S(2)}) collective-permute-start(bf16[1024,128]{1,0:T(8,128)(2,1)} %collective-permute-done.18.refs_1_.refs_5_), channel_id=1, source_target_pairs={{0,4},{2,6},{4,0},{6,2},{8,12},{10,14},{12,8},{14,10},{16,20},{18,... | collective-permute-start | bytes 786440 | tf_op jit(solution)/shard_map/ppermute | solution.py:347
  94.4 17.5 %collective-permute-start.22 = (bf16[1024,128]{1,0:T(8,128)(2,1)}, bf16[1024,128]{1,0:T(8,128)(2,1)}, u32[]{:S(2)}, u32[]{:S(2)}) collective-permute-start(bf16[1024,128]{1,0:T(8,128)(2,1)} %collective-permute-done.20.refs_4_.refs_8_), channel_id=1, source_target_pairs={{0,2},{2,0},{4,6},{6,4},{8,10},{10,8},{12,14},{14,12},{16,18},{18,... | collective-permute-start | bytes 786440 | tf_op jit(solution)/shard_map/ppermute | solution.py:351
  164.1 16.7 %collective-permute-start.38 = (bf16[128,2048]{1,0:T(8,128)(2,1)S(1)}, bf16[128,2048]{1,0:T(8,128)(2,1)S(1)}, u32[]{:S(2)}, u32[]{:S(2)}) collective-permute-start(bf16[128,2048]{1,0:T(8,128)(2,1)S(1)} %collective-permute-done.35.refs_4_), channel_id=1, source_target_pairs={{0,8},{2,10},{4,12},{6,14},{8,16},{10,18},{12,20},{14,22},{16,24},... | collective-permute-start | bytes 1572872 | tf_op jit(solution)/shard_map/ppermute | solution.py:335
  166.4 25.3 %collective-permute-start.34 = (bf16[128,2048]{1,0:T(8,128)(2,1)S(1)}, bf16[128,2048]{1,0:T(8,128)(2,1)S(1)}, u32[]{:S(2)}, u32[]{:S(2)}) collective-permute-start(bf16[128,2048]{1,0:T(8,128)(2,1)S(1)} %slice.180), channel_id=1, source_target_pairs={{0,8},{2,10},{4,12},{6,14},{8,0},{10,2},{12,4},{14,6},{16,24},{18,... | collective-permute-start | bytes 1572872 | tf_op jit(solution)/shard_map/ppermute | solution.py:339
  184.6 17.5 %collective-permute-start.43 = (bf16[128,2048]{1,0:T(8,128)(2,1)S(1)}, bf16[128,2048]{1,0:T(8,128)(2,1)}, u32[]{:S(2)}, u32[]{:S(2)}) collective-permute-start(bf16[128,2048]{1,0:T(8,128)(2,1)S(1)} %collective-permute-done.38.refs_4_), channel_id=1, source_target_pairs={{0,8},{2,10},{4,12},{6,14},{8,16},{10,18},{12,20},{14,22},{16,24},... | collective-permute-start | bytes 1572872 | tf_op jit(solution)/shard_map/ppermute | solution.py:335
  235.3 20.1 %collective-permute-start.51 = (bf16[128,2048]{1,0:T(8,128)(2,1)}, bf16[128,2048]{1,0:T(8,128)(2,1)S(1)}, u32[]{:S(2)}, u32[]{:S(2)}) collective-permute-start(bf16[128,2048]{1,0:T(8,128)(2,1)} %collective-permute-done.48.refs_0_), channel_id=1, source_target_pairs={{0,8},{2,10},{4,12},{6,14},{8,16},{10,18},{12,20},{14,22},{16,24},... | collective-permute-start | bytes 1572872 | tf_op jit(solution)/shard_map/ppermute | solution.py:335
  235.3 20.1 %collective-permute-start.52 = (bf16[128,2048]{1,0:T(8,128)(2,1)}, bf16[128,2048]{1,0:T(8,128)(2,1)S(1)}, u32[]{:S(2)}, u32[]{:S(2)}) collective-permute-start(bf16[128,2048]{1,0:T(8,128)(2,1)} %collective-permute-done.48.refs_0_), channel_id=1, source_target_pairs={{0,2},{2,0},{4,6},{6,4},{8,10},{10,8},{12,14},{14,12},{16,18},{18,... | collective-permute-start | bytes 1572872 | tf_op jit(solution)/shard_map/ppermute | solution.py:351
  235.9 19.5 %collective-permute-start.53 = (bf16[128,2048]{1,0:T(8,128)(2,1)}, bf16[128,2048]{1,0:T(8,128)(2,1)S(1)}, u32[]{:S(2)}, u32[]{:S(2)}) collective-permute-start(bf16[128,2048]{1,0:T(8,128)(2,1)} %collective-permute-done.46.refs_0_), channel_id=1, source_target_pairs={{0,4},{2,6},{4,0},{6,2},{8,12},{10,14},{12,8},{14,10},{16,20},{18,... | collective-permute-start | bytes 1572872 | tf_op jit(solution)/shard_map/ppermute | solution.py:347
  272.3 18.3 %collective-permute-start.59 = (bf16[128,2048]{1,0:T(8,128)(2,1)}, bf16[128,2048]{1,0:T(8,128)(2,1)S(1)}, u32[]{:S(2)}, u32[]{:S(2)}) collective-permute-start(bf16[128,2048]{1,0:T(8,128)(2,1)} %collective-permute-done.43.refs_4_), channel_id=1, source_target_pairs={{0,2},{2,0},{4,6},{6,4},{8,10},{10,8},{12,14},{14,12},{16,18},{18,... | collective-permute-start | bytes 1572872 | tf_op jit(solution)/shard_map/ppermute | solution.py:351
  272.9 17.8 %collective-permute-start.60 = (bf16[128,2048]{1,0:T(8,128)(2,1)S(1)}, bf16[128,2048]{1,0:T(8,128)(2,1)S(1)}, u32[]{:S(2)}, u32[]{:S(2)}) collective-permute-start(bf16[128,2048]{1,0:T(8,128)(2,1)S(1)} %copy-done.13), channel_id=1, source_target_pairs={{0,4},{2,6},{4,0},{6,2},{8,12},{10,14},{12,8},{14,10},{16,20},{18,... | collective-permute-start | bytes 1572872 | tf_op jit(solution)/shard_map/ppermute | solution.py:347
  483.1 19.4 %collective-permute-start.101 = (bf16[128,2048]{1,0:T(8,128)(2,1)S(1)}, bf16[128,2048]{1,0:T(8,128)(2,1)S(1)}, u32[]{:S(2)}, u32[]{:S(2)}) collective-permute-start(bf16[128,2048]{1,0:T(8,128)(2,1)S(1)} %get-tuple-element.511), channel_id=1, source_target_pairs={{0,2},{2,0},{4,6},{6,4},{8,10},{10,8},{12,14},{14,12},{16,18},{18,... | collective-permute-start | bytes 1572872 | tf_op jit(solution)/shard_map/ppermute | solution.py:351
  484.7 17.8 %collective-permute-start.102 = (bf16[128,2048]{1,0:T(8,128)(2,1)S(1)}, bf16[128,2048]{1,0:T(8,128)(2,1)S(1)}, u32[]{:S(2)}, u32[]{:S(2)}) collective-permute-start(bf16[128,2048]{1,0:T(8,128)(2,1)S(1)} %get-tuple-element.512), channel_id=1, source_target_pairs={{0,4},{2,6},{4,0},{6,2},{8,12},{10,14},{12,8},{14,10},{16,20},{18,... | collective-permute-start | bytes 1572872 | tf_op jit(solution)/shard_map/ppermute | solution.py:347
  485.3 17.2 %collective-permute-start.103 = (bf16[128,2048]{1,0:T(8,128)(2,1)S(1)}, bf16[128,2048]{1,0:T(8,128)(2,1)S(1)}, u32[]{:S(2)}, u32[]{:S(2)}) collective-permute-start(bf16[128,2048]{1,0:T(8,128)(2,1)S(1)} %get-tuple-element.513), channel_id=1, source_target_pairs={{0,8},{2,10},{4,12},{6,14},{8,16},{10,18},{12,20},{14,22},{16,24},... | collective-permute-start | bytes 1572872 | tf_op jit(solution)/shard_map/ppermute | solution.py:335
  485.3 17.0 %collective-permute-start.99 = (bf16[128,1024]{1,0:T(8,128)(2,1)S(1)}, bf16[128,1024]{1,0:T(8,128)(2,1)S(1)}, u32[]{:S(2)}, u32[]{:S(2)}) collective-permute-start(bf16[128,1024]{1,0:T(8,128)(2,1)S(1)} %get-tuple-element.506), channel_id=1, source_target_pairs={{0,2},{2,0},{4,6},{6,4},{8,10},{10,8},{12,14},{14,12},{16,18},{18,... | collective-permute-start | bytes 786440 | tf_op jit(solution)/shard_map/ppermute | solution.py:351
  502.5 19.2 %collective-permute-start.104 = (bf16[2,128,1024]{2,1,0:T(8,128)(2,1)S(1)}, bf16[2,128,1024]{2,1,0:T(8,128)(2,1)S(1)}, u32[]{:S(2)}, u32[]{:S(2)}) collective-permute-start(bf16[2,128,1024]{2,1,0:T(8,128)(2,1)S(1)} %sums.22), channel_id=1, source_target_pairs={{0,4},{2,6},{4,0},{6,2},{8,12},{10,14},{12,8},{14,10},{16,20},{18,... | collective-permute-start | bytes 1572872 | tf_op jit(solution)/shard_map/ppermute | solution.py:347
  503.7 18.3 %collective-permute-start.106 = (bf16[128,2048]{1,0:T(8,128)(2,1)S(1)}, bf16[128,2048]{1,0:T(8,128)(2,1)S(1)}, u32[]{:S(2)}, u32[]{:S(2)}) collective-permute-start(bf16[128,2048]{1,0:T(8,128)(2,1)S(1)} %copy-done.52), channel_id=1, source_target_pairs={{0,2},{2,0},{4,6},{6,4},{8,10},{10,8},{12,14},{14,12},{16,18},{18,... | collective-permute-start | bytes 1572872 | tf_op jit(solution)/shard_map/ppermute | solution.py:351
  504.7 17.0 %collective-permute-start.105 = (bf16[128,1024]{1,0:T(8,128)(2,1)S(1)}, bf16[128,1024]{1,0:T(8,128)(2,1)S(1)}, u32[]{:S(2)}, u32[]{:S(2)}) collective-permute-start(bf16[128,1024]{1,0:T(8,128)(2,1)S(1)} %get-tuple-element.515), channel_id=1, source_target_pairs={{0,2},{2,0},{4,6},{6,4},{8,10},{10,8},{12,14},{14,12},{16,18},{18,... | collective-permute-start | bytes 786440 | tf_op jit(solution)/shard_map/ppermute | solution.py:351
  536.3 20.5 %collective-permute-start.111 = (bf16[128,2048]{1,0:T(8,128)(2,1)S(1)}, bf16[128,2048]{1,0:T(8,128)(2,1)S(1)}, u32[]{:S(2)}, u32[]{:S(2)}) collective-permute-start(bf16[128,2048]{1,0:T(8,128)(2,1)S(1)} %copy-done.50), channel_id=1, source_target_pairs={{0,2},{2,0},{4,6},{6,4},{8,10},{10,8},{12,14},{14,12},{16,18},{18,... | collective-permute-start | bytes 1572872 | tf_op jit(solution)/shard_map/ppermute | solution.py:351
  536.8 20.0 %collective-permute-start.112 = (bf16[128,2048]{1,0:T(8,128)(2,1)S(1)}, bf16[128,2048]{1,0:T(8,128)(2,1)S(1)}, u32[]{:S(2)}, u32[]{:S(2)}) collective-permute-start(bf16[128,2048]{1,0:T(8,128)(2,1)S(1)} %get-tuple-element.538), channel_id=1, source_target_pairs={{0,4},{2,6},{4,0},{6,2},{8,12},{10,14},{12,8},{14,10},{16,20},{18,... | collective-permute-start | bytes 1572872 | tf_op jit(solution)/shard_map/ppermute | solution.py:347
  537.9 18.9 %collective-permute-start.113 = (bf16[128,2048]{1,0:T(8,128)(2,1)S(1)}, bf16[128,2048]{1,0:T(8,128)(2,1)S(1)}, u32[]{:S(2)}, u32[]{:S(2)}) collective-permute-start(bf16[128,2048]{1,0:T(8,128)(2,1)S(1)} %get-tuple-element.539), channel_id=1, source_target_pairs={{0,8},{2,10},{4,12},{6,14},{8,16},{10,18},{12,20},{14,22},{16,24},... | collective-permute-start | bytes 1572872 | tf_op jit(solution)/shard_map/ppermute | solution.py:335
  538.1 18.7 %collective-permute-start.114 = (bf16[128,1408]{1,0:T(8,128)(2,1)S(1)}, bf16[128,1408]{1,0:T(8,128)(2,1)S(1)}, u32[]{:S(2)}, u32[]{:S(2)}) collective-permute-start(bf16[128,1408]{1,0:T(8,128)(2,1)S(1)} %get-tuple-element.540), channel_id=1, source_target_pairs={{0,2},{2,0},{4,6},{6,4},{8,10},{10,8},{12,14},{14,12},{16,18},{18,... | collective-permute-start | bytes 1081352 | tf_op jit(solution)/shard_map/ppermute | solution.py:351
  573.8 17.3 %collective-permute-start.122 = (bf16[2,128,1408]{2,1,0:T(8,128)(2,1)S(1)}, bf16[2,128,1408]{2,1,0:T(8,128)(2,1)S(1)}, u32[]{:S(2)}, u32[]{:S(2)}) collective-permute-start(bf16[2,128,1408]{2,1,0:T(8,128)(2,1)S(1)} %sums.26), channel_id=1, source_target_pairs={{0,4},{2,6},{4,0},{6,2},{8,12},{10,14},{12,8},{14,10},{16,20},{18,... | collective-permute-start | bytes 2162696 | tf_op jit(solution)/shard_map/ppermute | solution.py:347
  594.1 17.6 %collective-permute-start.127 = (bf16[128,1408]{1,0:T(8,128)(2,1)S(1)}, bf16[128,1408]{1,0:T(8,128)(2,1)S(1)}, u32[]{:S(2)}, u32[]{:S(2)}) collective-permute-start(bf16[128,1408]{1,0:T(8,128)(2,1)S(1)} %get-tuple-element.579), channel_id=1, source_target_pairs={{0,16},{2,18},{4,20},{6,22},{8,24},{10,26},{12,28},{14,30},{16,0},... | collective-permute-start | bytes 1081352 | tf_op jit(solution)/shard_map/ppermute | solution.py:343
  611.6 17.1 %collective-permute-start.129 = (bf16[2,128,1408]{2,1,0:T(8,128)(2,1)S(1)}, bf16[2,128,1408]{2,1,0:T(8,128)(2,1)S(1)}, u32[]{:S(2)}, u32[]{:S(2)}) collective-permute-start(bf16[2,128,1408]{2,1,0:T(8,128)(2,1)S(1)} %get-tuple-element.582), channel_id=1, source_target_pairs={{0,4},{2,6},{4,0},{6,2},{8,12},{10,14},{12,8},{14,10},{16,20},{18,... | collective-permute-start | bytes 2162696 | tf_op jit(solution)/shard_map/ppermute | solution.py:347
  613.3 17.2 %collective-permute-start.131 = (bf16[128,1408]{1,0:T(8,128)(2,1)S(1)}, bf16[128,1408]{1,0:T(8,128)(2,1)S(1)}, u32[]{:S(2)}, u32[]{:S(2)}) collective-permute-start(bf16[128,1408]{1,0:T(8,128)(2,1)S(1)} %get-tuple-element.591), channel_id=1, source_target_pairs={{0,16},{2,18},{4,20},{6,22},{8,24},{10,26},{12,28},{14,30},{16,0},... | collective-permute-start | bytes 1081352 | tf_op jit(solution)/shard_map/ppermute | solution.py:343
  (226 other events, 3235.0 us)
